TPU v7x, 128 devices: a whole 4x4x4 slice. The times are simulated.
128 devices in a mesh: gx: 8 (over x, y_hi), gy: 16 (over z, y_lo, core).
Axes of the slice: x: 4, y: 4 (y_hi: 2, y_lo: 2; y = y_hi * 2 + y_lo), z: 4, core: 2. Of those that a mesh axis runs over, the one named last changes fastest.
Arguments:
- child_state: float32 [4, 8, 2048, 2048], P(None, None, 'gx', 'gy'), may hold values from -6 to 6
- parent_slab: float32 [4, 8, 2048, 128], P(None, None, ('gx', 'gy')), may hold values from -6 to 6
- parent_above: float32 [4, 2048, 128], P(None, ('gx', 'gy')), may hold values from -6 to 6
- radiative_mean_kelvin: float32 [2048, 2048], P('gx', 'gy'), may hold values from -6 to 6
- courant_x: float32 [8], replicated, may hold values from -0.8 to 0.8
- courant_y: float32 [8], replicated, may hold values from -0.8 to 0.8
- diffusion: float32 [4], replicated, may hold values from 0.05 to 0.15
- building: int32 [8, 2048, 2048], P(None, 'gx', 'gy'), may hold values 0 or 1
- fine_tile: int32 [2048, 16], P(('gx', 'gy')), may hold values from 0 to 3
- fine_row: int32 [2048, 16], P(('gx', 'gy')), may hold values from 0 to 255
- fine_op: int32 [2048, 16], P(('gx', 'gy')), may hold values from 0 to 7
- fine_bank: float32 [8, 128, 128], replicated, may hold values from -0.125 to 0.125
- coarse_tile: int32 [2048, 16, 4], P('gx', 'gy'), may hold values from 0 to 3
- coarse_row: int32 [2048, 16, 4], P('gx', 'gy'), may hold values from 0 to 15
- coarse_op: int32 [2048, 16, 4], P('gx', 'gy'), may hold values from 0 to 7
- coarse_bank: float32 [8, 128, 128], replicated, may hold values from -0.25 to 0.25
Outputs:
- nested_domain_states: float32 [4, 8, 2048, 2048], P(None, None, 'gx', 'gy')
- parent_new: float32 [4, 8, 2048, 128], P(None, None, ('gx', 'gy'))
- comfort: float32 [2048, 2048], P('gx', 'gy')
All inputs are finite; a program needn't handle non-finite values. No bound on the sum of `building` on one device may be relied on, other than what follows from the above.
Results may differ from a plain program's by a relative error of at most 0.0003.
Values sent between devices are 32-bit elements; how exact they have to be, the bound alone decides.
No kernel may reach another device: no remote copies, remote signals or barrier semaphores. Data moves between devices by JAX's collectives and lax.ppermute only.
A program may use at most 128 MiB of HBM per device.

v0:
```python
import jax
import jax.numpy as jnp
from jax import lax
from jax.sharding import PartitionSpec as P

precise_setting = lax.Precision.HIGHEST
relaxation = 0.5


def from_behind(value, axis, by):
    devices = lax.axis_size(axis)
    pairs = [(i, i + by) for i in range(devices) if 0 <= i + by < devices]
    return lax.ppermute(value, axis, pairs)


def extended(value, sides, width):
    for axis, dim in sides:
        devices, length = (lax.axis_size(axis), value.shape[dim])
        up = [(i, (i + 1) % devices) for i in range(devices - 1)]
        down = [(j, i) for i, j in up]
        last = lax.slice_in_dim(value, length - width, length, axis=dim)
        initial = lax.slice_in_dim(value, 0, width, axis=dim)
        before = lax.ppermute(last, axis, up)
        after = lax.ppermute(initial, axis, down)
        value = jnp.concatenate([before, value, after], axis=dim)
    return value


def beam_warming(centre, near_low, far_low, near_high, distant_upper, courant):
    magnitude = jnp.abs(courant)
    from_low = -0.5 * magnitude * (
        3.0 * centre - 4.0 * near_low + far_low
    ) + 0.5 * magnitude * magnitude * (centre - 2.0 * near_low + far_low)
    from_high = -0.5 * magnitude * (
        3.0 * centre - 4.0 * near_high + distant_upper
    ) + 0.5 * magnitude * magnitude * (centre - 2.0 * near_high + distant_upper)
    return jnp.where(courant >= 0.0, from_low, from_high)


def advance(padded, top_ghost, courant_x, courant_y, diffusion, building):
    centre = padded[:, :, 2:-2, 2:-2]
    west_near = padded[:, :, 1:-3, 2:-2]
    west_far = padded[:, :, :-4, 2:-2]
    east_near = padded[:, :, 3:-1, 2:-2]
    east_far = padded[:, :, 4:, 2:-2]
    south_near = padded[:, :, 2:-2, 1:-3]
    south_far = padded[:, :, 2:-2, :-4]
    north_near = padded[:, :, 2:-2, 3:-1]
    north_far = padded[:, :, 2:-2, 4:]
    along_x = beam_warming(
        centre, west_near, west_far, east_near, east_far, courant_x[None, :, None, None]
    )
    along_y = beam_warming(
        centre, south_near, south_far, north_near, north_far, courant_y[None, :, None, None]
    )
    beneath = jnp.concatenate([jnp.zeros_like(centre[:, :1]), centre[:, :-1]], axis=1)
    overhead = jnp.concatenate([centre[:, 1:], top_ghost[:, None]], axis=1)
    laplace = west_near + east_near + south_near + north_near + beneath + overhead - 6.0 * centre
    stepped = centre + along_x + along_y + diffusion[:, None, None, None] * laplace
    return jnp.where(building[None] == 1, 0.0, stepped)


def comfort_index(nested_domain_states, radiative_mean_kelvin):
    wind_u = nested_domain_states[0, 0]
    wind_v = nested_domain_states[1, 0]
    ambient_kelvin = nested_domain_states[2, 0]
    moisture_ratio = nested_domain_states[3, 0]
    flow_speed_norm = jnp.sqrt(wind_u * wind_u + wind_v * wind_v + 0.25)
    excess_quantity = radiative_mean_kelvin - ambient_kelvin
    return (
        ambient_kelvin
        + 0.3 * excess_quantity
        - 0.6 * (flow_speed_norm - 1.0)
        + 0.4 * moisture_ratio
        + 0.1 * ambient_kelvin * excess_quantity
        - 0.15 * flow_speed_norm * excess_quantity
    )


def interpolate(sources, tile_ids, row_ids, op_ids, operator_library):
    picked = sources[tile_ids, :, row_ids, :]
    accumulated_total = jnp.zeros((picked.shape[2], picked.shape[0], picked.shape[3]), jnp.float32)
    for operator_position in range(operator_library.shape[0]):
        chosen = (op_ids == operator_position).astype(jnp.float32)
        combined_fields = jnp.einsum("xk,xkvb->vxb", chosen, picked, precision=precise_setting)
        accumulated_total = accumulated_total + jnp.einsum(
            "nt,pyt->pyn",
            operator_library[operator_position],
            combined_fields,
            precision=precise_setting,
        )
    return accumulated_total


def anterpolate(sources, tile_ids, row_ids, op_ids, operator_library):
    picked = sources[tile_ids, :, :, row_ids, :]
    accumulated_total = jnp.zeros(
        (picked.shape[2], picked.shape[3], picked.shape[0], picked.shape[4]), jnp.float32
    )
    for operator_position in range(operator_library.shape[0]):
        chosen = (op_ids == operator_position).astype(jnp.float32)
        combined_fields = jnp.einsum("pk,pkvzb->vzpb", chosen, picked, precision=precise_setting)
        accumulated_total = accumulated_total + jnp.einsum(
            "cb,vzpb->vzpc",
            operator_library[operator_position],
            combined_fields,
            precision=precise_setting,
        )
    return accumulated_total


def local(
    child_state,
    parent_slab,
    parent_above,
    radiative_mean_kelvin,
    courant_x,
    courant_y,
    diffusion,
    building,
    fine_tile,
    fine_row,
    fine_op,
    fine_bank,
    coarse_tile,
    coarse_row,
    coarse_op,
    coarse_bank,
):
    parent_west = from_behind(parent_above, "gx", 1)
    parent_pair = from_behind(jnp.stack([parent_above, parent_west]), "gy", 1)
    parent_sources = jnp.stack([parent_above, parent_west, parent_pair[0], parent_pair[1]])
    top_ghost = interpolate(
        parent_sources, coarse_tile[:, 0, :], coarse_row[:, 0, :], coarse_op[:, 0, :], coarse_bank
    )
    padded = extended(child_state, (("gx", 2), ("gy", 3)), 2)
    nested_domain_states = advance(padded, top_ghost, courant_x, courant_y, diffusion, building)
    child_east = from_behind(nested_domain_states, "gx", -1)
    child_pair = from_behind(jnp.stack([nested_domain_states, child_east]), "gy", -1)
    child_sources = jnp.stack([nested_domain_states, child_east, child_pair[0], child_pair[1]])
    anterp = anterpolate(child_sources, fine_tile, fine_row, fine_op, fine_bank)
    parent_new = (1.0 - relaxation) * parent_slab + relaxation * anterp
    return (
        nested_domain_states,
        parent_new,
        comfort_index(nested_domain_states, radiative_mean_kelvin),
    )


def solution(mesh):
    placed = (
        P(None, None, "gx", "gy"),
        P(None, None, ("gx", "gy"), None),
        P(None, ("gx", "gy"), None),
        P("gx", "gy"),
        P(),
        P(),
        P(),
        P(None, "gx", "gy"),
        P(("gx", "gy"), None),
        P(("gx", "gy"), None),
        P(("gx", "gy"), None),
        P(),
        P("gx", "gy", None),
        P("gx", "gy", None),
        P("gx", "gy", None),
        P(),
    )
    return jax.shard_map(
        local,
        mesh=mesh,
        in_specs=placed,
        out_specs=(P(None, None, "gx", "gy"), P(None, None, ("gx", "gy"), None), P("gx", "gy")),
        check_vma=False,
    )
```

profile of v0, /device:TPU:45, one launch (start us, length us, event | category | flops | bytes accessed | tf_op | source)
XLA Modules:
  0.0 380.3 jit_solution(5751412381375823663)
XLA Ops:
  0.6 0.8 copy.234
  1.4 3.9 %collective-permute-start.4 = (f32[4,16,128]{2,0,1:T(4,128)S(1)}, f32[4,16,128]{2,0,1:T(4,128)S(1)}, u32[]{:S(2)}, u32[]{:S(2)}) collective-permute-start(f32[4,16,128]{2,0,1:T(4,128)S(1)} %copy.234), channel_id=1, source_target_pairs={{0,16},{16,32},{32,48},{48,64},{64,80},{80,96},{96,112},{1,17},{17... | collective-permute-start | bytes 98312 | tf_op jit(solution)/shard_map/ppermute | solution.py:13
  5.3 1.0 fusion.137
  6.3 3.5 collective-permute-start
  9.9 4.3 %collective-permute-start.1 = (f32[4,8,2,128]{3,1,2,0:T(8,128)S(1)}, f32[4,8,2,128]{3,1,2,0:T(8,128)S(1)}, u32[]{:S(2)}, u32[]{:S(2)}) collective-permute-start(f32[4,8,2,128]{3,1,2,0:T(8,128)S(1)} %copy.232), channel_id=1, source_target_pairs={{16,0},{32,16},{48,32},{64,48},{80,64},{96,80},{112,96},{17,1},{33... | collective-permute-start | bytes 98312 | tf_op jit(solution)/shard_map/ppermute | solution.py:24
  14.3 6.9 %fusion.138 = (f32[4,7,256,128]{3,2,1,0:T(8,128)}, f32[4,7,256,128]{3,2,1,0:T(8,128)}) fusion(f32[4,8,256,128]{3,2,1,0:T(8,128)} %param.16), kind=kLoop, calls=%fused_computation.206 | loop fusion | bytes 14680064 | tf_op jit(solution)/shard_map/slice | solution.py:56
  21.4 0.5 abs_multiply_fusion
  21.9 0.6 broadcast_compare_fusion.1
  25.1 6.3 %copy.229 = f32[4,7,256,128]{3,1,2,0:T(8,128)} copy(f32[4,7,256,128]{3,2,1,0:T(8,128)} %get-tuple-element.17) | data formatting | bytes 7340032
  31.4 4.2 %copy.230 = f32[4,7,256,128]{3,1,2,0:T(8,128)} copy(f32[4,7,256,128]{3,2,1,0:T(8,128)S(1)} %copy-done.9) | data formatting | bytes 7340032
  35.8 5.9 %collective-permute-start.5 = (f32[2,4,16,128]{3,1,2,0:T(4,128)S(1)}, f32[2,4,16,128]{3,1,2,0:T(4,128)S(1)}, u32[]{:S(2)}, u32[]{:S(2)}) collective-permute-start(f32[2,4,16,128]{3,1,2,0:T(4,128)S(1)} %pad_maximum_fusion.7), channel_id=1, source_target_pairs={{0,1},{1,2},{2,3},{3,4},{4,5},{5,6},{6,7},{7,8},{8,9},{9,10},{10,1... | collective-permute-start | bytes 196616 | tf_op jit(solution)/shard_map/ppermute | solution.py:13
  41.7 2.6 constant_dynamic-update-slice_fusion
  44.4 5.1 %fusion.136 = (f32[4,8,260,2]{3,1,2,0:T(8,128)}, f32[4,8,260,2]{3,1,2,0:T(8,128)}) fusion(f32[4,8,260,128]{3,1,2,0:T(8,128)S(1)} %get-tuple-element.21), kind=kLoop, calls=%fused_computation.204 | loop fusion | bytes 266240 | tf_op jit(solution)/shard_map/slice | solution.py:21
  49.6 0.6 copy-done.4
  50.2 1.2 copy-done.5
  51.4 4.1 %copy.56 = f32[4,8,260,2]{2,1,3,0:T(8,128)} copy(f32[4,8,260,2]{3,1,2,0:T(8,128)} %get-tuple-element.10) | data formatting | bytes 133120 | tf_op jit(solution)/shard_map/slice | solution.py:22
  55.5 1.9 collective-permute-start.3
  57.4 4.1 %copy.53 = f32[4,8,260,2]{2,1,3,0:T(8,128)} copy(f32[4,8,260,2]{3,1,2,0:T(8,128)} %get-tuple-element.9) | data formatting | bytes 133120 | tf_op jit(solution)/shard_map/slice | solution.py:21
  61.5 4.5 %collective-permute-start.2 = (f32[4,8,260,2]{2,1,3,0:T(8,128)}, f32[4,8,260,2]{2,1,3,0:T(8,128)}, u32[]{:S(2)}, u32[]{:S(2)}) collective-permute-start(f32[4,8,260,2]{2,1,3,0:T(8,128)} %copy.53), channel_id=1, source_target_pairs={{0,1},{1,2},{2,3},{3,4},{4,5},{5,6},{6,7},{7,8},{8,9},{9,10},{10,1... | collective-permute-start | bytes 199688 | tf_op jit(solution)/shard_map/ppermute | solution.py:23
  66.1 4.7 %gather_fusion = f32[1024,4,128]{2,1,0:T(4,128)S(1)} fusion(f32[4,4,16,128]{3,1,2,0:T(4,128)S(1)} %pad_maximum_fusion.6, s32[1024]{0:T(1024)S(1)} %reshape.111), kind=kCustom, calls=%fused_computation | custom fusion | bytes 4202496 | tf_op jit(solution)/shard_map/gather | solution.py:81
  70.8 2.5 fusion.61
  73.2 2.5 fusion.59
  75.7 2.5 fusion.57
  78.2 2.5 fusion.55
  80.6 2.9 fusion.53
  83.5 2.5 fusion.51
  86.0 2.5 fusion.49
  88.5 2.5 fusion.47
  90.9 0.6 fusion.37
  91.5 0.6 convolution_add_fusion.6
  92.1 0.6 convolution_add_fusion.5
  92.7 0.6 convolution_add_fusion.4
  93.3 0.6 convolution_add_fusion.3
  93.9 0.8 convolution_add_fusion.2
  94.7 0.6 convolution_add_fusion.1
  95.2 0.6 convolution_add_fusion
  95.9 4.1 %copy.57 = f32[4,8,260,2]{3,1,2,0:T(8,128)} copy(f32[4,8,260,2]{2,1,3,0:T(8,128)} %collective-permute-done.3) | data formatting | bytes 133120 | tf_op jit(solution)/shard_map/ppermute | solution.py:24
  100.0 4.1 %copy.54 = f32[4,8,260,2]{3,1,2,0:T(8,128)} copy(f32[4,8,260,2]{2,1,3,0:T(8,128)} %collective-permute-done.2) | data formatting | bytes 133120 | tf_op jit(solution)/shard_map/ppermute | solution.py:23
  104.1 23.7 %fusion.3 = f32[4,8,256,128]{3,1,2,0:T(8,128)S(1)} fusion(f32[4,1,256,128]{3,1,2,0:T(1,128)S(1)} %bitcast.278, f32[4,7,256,128]{3,1,2,0:T(8,128)} %copy.229, f32[4,7,256,128]{3,1,2,0:T(8,128)} %copy.230, f32[4,8,260,2]{3,1,2,0:T(8,128)} %copy.57, f32[4,8,260,128]{3,1,2,0:T(8,128)} %copy-done.4, f32[4,8,260,2]{3,1,2,0:T(8,128)} %copy.54, ...), kind=kLoop, calls=%fused_computation.12 | loop fusion | flops 58720256 | bytes 37685408 | tf_op jit(solution)/shard_map/jit(_where)/select_n | solution.py:60
  127.9 1.9 collective-permute-start.6
  129.8 92.1 %collective-permute-done.6 = f32[4,8,256,128]{3,1,2,0:T(8,128)S(1)} collective-permute-done((f32[4,8,256,128]{3,1,2,0:T(8,128)S(1)}, f32[4,8,256,128]{3,1,2,0:T(8,128)S(1)}, u32[]{:S(2)}, u32[]{:S(2)}) %collective-permute-start.6) | collective-permute-done | bytes 4194336 | tf_op jit(solution)/shard_map/ppermute | solution.py:13
  221.9 4.1 %pad_maximum_fusion.1 = f32[2,4,8,256,128]{4,2,3,1,0:T(8,128)} fusion(f32[1,4,8,256,128]{4,2,3,1,0:T(8,128)S(1)} %bitcast.276, f32[1,4,8,256,128]{4,2,3,1,0:T(8,128)S(1)} %bitcast.274), kind=kLoop, calls=%fused_computation.3 | loop fusion | flops 2097152 | bytes 16777216 | tf_op jit(solution)/shard_map/stack | solution.py:139
  226.4 1.9 collective-permute-start.7
  228.5 3.1 copy.69
  232.0 1.9 copy-done.10
  233.9 0.8 fusion.83
  234.7 87.7 %collective-permute-done.7 = f32[2,4,8,256,128]{4,2,3,1,0:T(8,128)} collective-permute-done((f32[2,4,8,256,128]{4,2,3,1,0:T(8,128)}, f32[2,4,8,256,128]{4,2,3,1,0:T(8,128)}, u32[]{:S(2)}, u32[]{:S(2)}) %collective-permute-start.7) | collective-permute-done | bytes 8388640 | tf_op jit(solution)/shard_map/ppermute | solution.py:13
  322.4 10.0 %pad_maximum_fusion = f32[4,4,8,256,128]{4,2,3,1,0:T(8,128)} fusion(f32[2,4,8,256,128]{4,2,3,1,0:T(8,128)} %collective-permute-done.7, f32[1,4,8,256,128]{4,2,3,1,0:T(8,128)S(1)} %bitcast.277, f32[1,4,8,256,128]{4,2,3,1,0:T(8,128)S(1)} %bitcast.275), kind=kLoop, calls=%fused_computation.2 | loop fusion | flops 8388608 | bytes 33554432 | tf_op jit(solution)/shard_map/stack | solution.py:140
  332.4 8.8 %gather_fusion.1 = f32[256,4,8,128]{3,2,1,0:T(8,128)} fusion(f32[4,4,8,256,128]{4,2,3,1,0:T(8,128)} %pad_maximum_fusion, s32[256]{0:T(256)S(1)} %reshape.117), kind=kCustom, calls=%fused_computation.1 | custom fusion | bytes 8390656 | tf_op jit(solution)/shard_map/gather | solution.py:96
  341.2 6.0 %fusion.26 = f32[16,1,4,8,128]{4,1,3,2,0:T(1,128)S(1)} fusion(f32[16,16,4,8,128]{4,3,2,1,0:T(8,128)} %bitcast.258, pred[16,16,1,1,1]{1,0,2,3,4:T(8,128)(4,1)S(1)} %get-tuple-element.30), kind=kOutput, calls=%fused_computation.37 | convolution fusion | flops 12582912 | bytes 4456704 | tf_op jit(solution)/shard_map/pk,pkvzb->vzpb/dot_general | solution.py:102
  347.3 3.9 %fusion.24 = f32[16,1,4,8,128]{4,1,3,2,0:T(1,128)S(1)} fusion(f32[16,16,4,8,128]{4,3,2,1,0:T(8,128)S(1)} %bitcast.259, pred[16,16,1,1,1]{1,0,2,3,4:T(8,128)(4,1)S(1)} %get-tuple-element.29), kind=kOutput, calls=%fused_computation.35 | convolution fusion | flops 12582912 | bytes 4456704 | tf_op jit(solution)/shard_map/pk,pkvzb->vzpb/dot_general | solution.py:102
  351.2 4.4 %fusion.22 = f32[16,1,4,8,128]{4,1,3,2,0:T(1,128)S(1)} fusion(f32[16,16,4,8,128]{4,3,2,1,0:T(8,128)S(1)} %bitcast.260, pred[16,16,1,1,1]{1,0,2,3,4:T(8,128)(4,1)S(1)} %get-tuple-element.28), kind=kOutput, calls=%fused_computation.33 | convolution fusion | flops 12582912 | bytes 4456704 | tf_op jit(solution)/shard_map/pk,pkvzb->vzpb/dot_general | solution.py:102
  355.6 3.9 %fusion.20 = f32[16,1,4,8,128]{4,1,3,2,0:T(1,128)S(1)} fusion(f32[16,16,4,8,128]{4,3,2,1,0:T(8,128)S(1)} %bitcast.261, pred[16,16,1,1,1]{1,0,2,3,4:T(8,128)(4,1)S(1)} %get-tuple-element.27), kind=kOutput, calls=%fused_computation.31 | convolution fusion | flops 12582912 | bytes 4456704 | tf_op jit(solution)/shard_map/pk,pkvzb->vzpb/dot_general | solution.py:102
  359.5 3.9 %fusion.18 = f32[16,1,4,8,128]{4,1,3,2,0:T(1,128)S(1)} fusion(f32[16,16,4,8,128]{4,3,2,1,0:T(8,128)S(1)} %bitcast.262, pred[16,16,1,1,1]{1,0,2,3,4:T(8,128)(4,1)S(1)} %get-tuple-element.26), kind=kOutput, calls=%fused_computation.29 | convolution fusion | flops 12582912 | bytes 4456704 | tf_op jit(solution)/shard_map/pk,pkvzb->vzpb/dot_general | solution.py:102
  363.5 4.1 %fusion.16 = f32[16,1,4,8,128]{4,1,3,2,0:T(1,128)S(1)} fusion(f32[16,16,4,8,128]{4,3,2,1,0:T(8,128)S(1)} %bitcast.263, pred[16,16,1,1,1]{1,0,2,3,4:T(8,128)(4,1)S(1)} %get-tuple-element.25), kind=kOutput, calls=%fused_computation.27 | convolution fusion | flops 12582912 | bytes 4456704 | tf_op jit(solution)/shard_map/pk,pkvzb->vzpb/dot_general | solution.py:102
  367.6 3.9 %fusion.14 = f32[16,1,4,8,128]{4,1,3,2,0:T(1,128)S(1)} fusion(f32[16,16,4,8,128]{4,3,2,1,0:T(8,128)S(1)} %bitcast.264, pred[16,16,1,1,1]{1,0,2,3,4:T(8,128)(4,1)S(1)} %get-tuple-element.31), kind=kOutput, calls=%fused_computation.25 | convolution fusion | flops 12582912 | bytes 4456704 | tf_op jit(solution)/shard_map/pk,pkvzb->vzpb/dot_general | solution.py:102
  371.5 3.9 %fusion.12 = f32[16,1,4,8,128]{4,1,3,2,0:T(1,128)S(1)} fusion(f32[16,16,4,8,128]{4,3,2,1,0:T(8,128)S(1)} %bitcast.265, pred[16,16,1,1,1]{1,0,2,3,4:T(8,128)(4,1)S(1)} %get-tuple-element.24), kind=kOutput, calls=%fused_computation.23 | convolution fusion | flops 12582912 | bytes 4456704 | tf_op jit(solution)/shard_map/pk,pkvzb->vzpb/dot_general | solution.py:102
  375.5 0.5 fusion.70
  376.0 0.5 convolution_add_fusion.13
  376.4 0.5 convolution_add_fusion.12
  376.9 0.5 convolution_add_fusion.11
  377.4 0.5 convolution_add_fusion.10
  377.9 0.5 convolution_add_fusion.9
  378.9 1.2 fusion.29
  (84 shorter events, 4.4 us)
Async XLA Ops:
  1.4 34.4 %collective-permute-start.4 = (f32[4,16,128]{2,0,1:T(4,128)S(1)}, f32[4,16,128]{2,0,1:T(4,128)S(1)}, u32[]{:S(2)}, u32[]{:S(2)}) collective-permute-start(f32[4,16,128]{2,0,1:T(4,128)S(1)} %copy.234), channel_id=1, source_target_pairs={{0,16},{16,32},{32,48},{48,64},{64,80},{80,96},{96,112},{1,17},{17... | collective-permute-start | bytes 98312 | tf_op jit(solution)/shard_map/ppermute | solution.py:13
  6.3 35.4 %collective-permute-start = (f32[4,8,2,128]{3,1,2,0:T(8,128)S(1)}, f32[4,8,2,128]{3,1,2,0:T(8,128)S(1)}, u32[]{:S(2)}, u32[]{:S(2)}) collective-permute-start(f32[4,8,2,128]{3,1,2,0:T(8,128)S(1)} %copy.231), channel_id=1, source_target_pairs={{0,16},{16,32},{32,48},{48,64},{64,80},{80,96},{96,112},{1,17},{17... | collective-permute-start | bytes 98312 | tf_op jit(solution)/shard_map/ppermute | solution.py:23
  9.9 11.3 %copy-start.19 = (s32[256,1,4]{0,2,1:T(4,128)S(1)}, s32[256,1,4]{0,2,1:T(4,128)}, u32[]{:S(2)}) copy-start(s32[256,1,4]{0,2,1:T(4,128)} %param.30) | copy-start | bytes 12292
  9.9 11.3 %copy-start.11 = (s32[8,256,128]{2,1,0:T(8,128)S(1)}, s32[8,256,128]{2,1,0:T(8,128)}, u32[]{:S(2)}) copy-start(s32[8,256,128]{2,1,0:T(8,128)} %param.23) | copy-start | bytes 3145732
  9.9 11.5 %copy-start.20 = (s32[256,1,4]{0,2,1:T(4,128)S(1)}, s32[256,1,4]{0,2,1:T(4,128)}, u32[]{:S(2)}) copy-start(s32[256,1,4]{0,2,1:T(4,128)} %param.29) | copy-start | bytes 12292
  9.9 11.5 %copy-start.21 = (s32[256,1,4]{0,2,1:T(4,128)S(1)}, s32[256,1,4]{0,2,1:T(4,128)}, u32[]{:S(2)}) copy-start(s32[256,1,4]{0,2,1:T(4,128)} %param.28) | copy-start | bytes 12292
  9.9 11.5 %copy-start.25 = (f32[8]{0:T(128)S(1)}, f32[8]{0:T(128)}, u32[]{:S(2)}) copy-start(f32[8]{0:T(128)} %param.21) | copy-start | bytes 100
  9.9 11.5 %copy-start.26 = (f32[8]{0:T(128)S(1)}, f32[8]{0:T(128)}, u32[]{:S(2)}) copy-start(f32[8]{0:T(128)} %param.20) | copy-start | bytes 100
  9.9 34.5 %collective-permute-start.1 = (f32[4,8,2,128]{3,1,2,0:T(8,128)S(1)}, f32[4,8,2,128]{3,1,2,0:T(8,128)S(1)}, u32[]{:S(2)}, u32[]{:S(2)}) collective-permute-start(f32[4,8,2,128]{3,1,2,0:T(8,128)S(1)} %copy.232), channel_id=1, source_target_pairs={{16,0},{32,16},{48,32},{64,48},{80,64},{96,80},{112,96},{17,1},{33... | collective-permute-start | bytes 98312 | tf_op jit(solution)/shard_map/ppermute | solution.py:24
  25.0 6.3 %copy-start.9 = (f32[4,7,256,128]{3,2,1,0:T(8,128)S(1)}, f32[4,7,256,128]{3,2,1,0:T(8,128)}, u32[]{:S(2)}) copy-start(f32[4,7,256,128]{3,2,1,0:T(8,128)} %get-tuple-element.16) | copy-start | bytes 11010052
  31.4 10.4 %copy-start.3 = (f32[4,8,256,128]{3,2,1,0:T(8,128)S(1)}, f32[4,8,256,128]{3,2,1,0:T(8,128)}, u32[]{:S(2)}) copy-start(f32[4,8,256,128]{3,2,1,0:T(8,128)} %param.16) | copy-start | bytes 12582916
  35.8 30.2 %collective-permute-start.5 = (f32[2,4,16,128]{3,1,2,0:T(4,128)S(1)}, f32[2,4,16,128]{3,1,2,0:T(4,128)S(1)}, u32[]{:S(2)}, u32[]{:S(2)}) collective-permute-start(f32[2,4,16,128]{3,1,2,0:T(4,128)S(1)} %pad_maximum_fusion.7), channel_id=1, source_target_pairs={{0,1},{1,2},{2,3},{3,4},{4,5},{5,6},{6,7},{7,8},{8,9},{9,10},{10,1... | collective-permute-start | bytes 196616 | tf_op jit(solution)/shard_map/ppermute | solution.py:13
  44.4 5.2 %copy-start.6 = (f32[4,8,258,128]{3,1,2,0:T(8,128)}, f32[4,8,258,128]{3,1,2,0:T(8,128)S(1)}, u32[]{:S(2)}) copy-start(f32[4,8,258,128]{3,1,2,0:T(8,128)S(1)} %get-tuple-element.11) | copy-start | bytes 12681220
  44.4 5.7 %copy-start.4 = (f32[4,8,260,128]{3,1,2,0:T(8,128)}, f32[4,8,260,128]{3,1,2,0:T(8,128)S(1)}, u32[]{:S(2)}) copy-start(f32[4,8,260,128]{3,1,2,0:T(8,128)S(1)} %get-tuple-element.21) | copy-start | bytes 12779524
  44.4 7.0 %copy-start.5 = (f32[4,8,258,128]{3,1,2,0:T(8,128)}, f32[4,8,258,128]{3,1,2,0:T(8,128)S(1)}, u32[]{:S(2)}) copy-start(f32[4,8,258,128]{3,1,2,0:T(8,128)S(1)} %get-tuple-element.20) | copy-start | bytes 12681220
  55.5 40.4 %collective-permute-start.3 = (f32[4,8,260,2]{2,1,3,0:T(8,128)}, f32[4,8,260,2]{2,1,3,0:T(8,128)}, u32[]{:S(2)}, u32[]{:S(2)}) collective-permute-start(f32[4,8,260,2]{2,1,3,0:T(8,128)} %copy.56), channel_id=1, source_target_pairs={{1,0},{2,1},{3,2},{4,3},{5,4},{6,5},{7,6},{8,7},{9,8},{10,9},{11,1... | collective-permute-start | bytes 199688 | tf_op jit(solution)/shard_map/ppermute | solution.py:24
  61.5 38.5 %collective-permute-start.2 = (f32[4,8,260,2]{2,1,3,0:T(8,128)}, f32[4,8,260,2]{2,1,3,0:T(8,128)}, u32[]{:S(2)}, u32[]{:S(2)}) collective-permute-start(f32[4,8,260,2]{2,1,3,0:T(8,128)} %copy.53), channel_id=1, source_target_pairs={{0,1},{1,2},{2,3},{3,4},{4,5},{5,6},{6,7},{7,8},{8,9},{9,10},{10,1... | collective-permute-start | bytes 199688 | tf_op jit(solution)/shard_map/ppermute | solution.py:23
  83.5 7.4 %copy-start.12 = (f32[8,128,128]{2,1,0:T(8,128)S(1)}, f32[8,128,128]{2,1,0:T(8,128)}, u32[]{:S(2)}) copy-start(f32[8,128,128]{2,1,0:T(8,128)} %param.31) | copy-start | bytes 1572868
  95.8 8.3 %copy-start.22 = (f32[8]{0:T(128)S(1)}, f32[8]{0:T(128)}, u32[]{:S(2)}) copy-start(f32[8]{0:T(128)} %get-tuple-element.45) | copy-start | bytes 100
  95.8 8.3 %copy-start.23 = (pred[8]{0:T(512)(128)(4,1)S(1)}, pred[8]{0:T(512)(128)(4,1)}, u32[]{:S(2)}) copy-start(pred[8]{0:T(512)(128)(4,1)} %get-tuple-element.46) | copy-start | bytes 28
  95.9 8.3 %copy-start.24 = (pred[8]{0:T(512)(128)(4,1)S(1)}, pred[8]{0:T(512)(128)(4,1)}, u32[]{:S(2)}) copy-start(pred[8]{0:T(512)(128)(4,1)} %get-tuple-element.47) | copy-start | bytes 28
  95.9 8.3 %copy-start.27 = (f32[4]{0:T(128)S(1)}, f32[4]{0:T(128)}, u32[]{:S(2)}) copy-start(f32[4]{0:T(128)} %param.22) | copy-start | bytes 52
  127.8 98.2 %copy-start.1 = (f32[4,8,256,128]{3,1,2,0:T(8,128)}, f32[4,8,256,128]{3,1,2,0:T(8,128)S(1)}, u32[]{:S(2)}) copy-start(f32[4,8,256,128]{3,1,2,0:T(8,128)S(1)} %fusion.3) | copy-start | bytes 12582916
  127.9 94.0 %collective-permute-start.6 = (f32[4,8,256,128]{3,1,2,0:T(8,128)S(1)}, f32[4,8,256,128]{3,1,2,0:T(8,128)S(1)}, u32[]{:S(2)}, u32[]{:S(2)}) collective-permute-start(f32[4,8,256,128]{3,1,2,0:T(8,128)S(1)} %fusion.3), channel_id=1, source_target_pairs={{16,0},{32,16},{48,32},{64,48},{80,64},{96,80},{112,96},{17,1},{33... | collective-permute-start | bytes 12582920 | tf_op jit(solution)/shard_map/ppermute | solution.py:13
  221.9 4.5 %copy-start.7 = (f32[4,8,256,128]{3,1,2,0:T(8,128)}, f32[4,8,256,128]{3,1,2,0:T(8,128)S(1)}, u32[]{:S(2)}) copy-start(f32[4,8,256,128]{3,1,2,0:T(8,128)S(1)} %collective-permute-done.6) | copy-start | bytes 12582916
  221.9 6.4 %copy-start.16 = (s32[16,16]{1,0:T(8,128)S(1)}, s32[16,16]{1,0:T(8,128)}, u32[]{:S(2)}) copy-start(s32[16,16]{1,0:T(8,128)} %param.24) | copy-start | bytes 3076
  221.9 6.4 %copy-start.17 = (s32[16,16]{1,0:T(8,128)S(1)}, s32[16,16]{1,0:T(8,128)}, u32[]{:S(2)}) copy-start(s32[16,16]{1,0:T(8,128)} %param.25) | copy-start | bytes 3076
  221.9 6.5 %copy-start.18 = (s32[16,16]{1,0:T(8,128)S(1)}, s32[16,16]{1,0:T(8,128)}, u32[]{:S(2)}) copy-start(s32[16,16]{1,0:T(8,128)} %param.26) | copy-start | bytes 3076
  226.4 96.0 %collective-permute-start.7 = (f32[2,4,8,256,128]{4,2,3,1,0:T(8,128)}, f32[2,4,8,256,128]{4,2,3,1,0:T(8,128)}, u32[]{:S(2)}, u32[]{:S(2)}) collective-permute-start(f32[2,4,8,256,128]{4,2,3,1,0:T(8,128)} %pad_maximum_fusion.1), channel_id=1, source_target_pairs={{1,0},{2,1},{3,2},{4,3},{5,4},{6,5},{7,6},{8,7},{9,8},{10,9},{11,1... | collective-permute-start | bytes 25165832 | tf_op jit(solution)/shard_map/ppermute | solution.py:13
  228.4 3.5 copy-start.2
  228.5 5.5 %copy-start.15 = (f32[256,128]{1,0:T(8,128)S(1)}, f32[256,128]{1,0:T(8,128)}, u32[]{:S(2)}) copy-start(f32[256,128]{1,0:T(8,128)} %param.19) | copy-start | bytes 393220
  228.5 93.9 %copy-start.8 = (f32[4,8,256,128]{3,1,2,0:T(8,128)S(1)}, f32[4,8,256,128]{3,1,2,0:T(8,128)}, u32[]{:S(2)}) copy-start(f32[4,8,256,128]{3,1,2,0:T(8,128)} %copy-done.7) | copy-start | bytes 12582916
  231.9 2.0 copy-start.10
  341.2 6.0 %copy-start = (f32[256,4,8,128]{3,2,1,0:T(8,128)S(1)}, f32[256,4,8,128]{3,2,1,0:T(8,128)}, u32[]{:S(2)}) copy-start(f32[256,4,8,128]{3,2,1,0:T(8,128)} %gather_fusion.1) | copy-start | bytes 12582916
  367.6 7.9 %copy-start.13 = (f32[8,128,128]{2,1,0:T(8,128)S(1)}, f32[8,128,128]{2,1,0:T(8,128)}, u32[]{:S(2)}) copy-start(f32[8,128,128]{2,1,0:T(8,128)} %param.27) | copy-start | bytes 1572868
  371.5 7.4 %copy-start.14 = (f32[4,8,16,128]{3,2,1,0:T(8,128)S(1)}, f32[4,8,16,128]{3,2,1,0:T(8,128)}, u32[]{:S(2)}) copy-start(f32[4,8,16,128]{3,2,1,0:T(8,128)} %param.17) | copy-start | bytes 786436
where the time goes:
time: 386 us; the launch traced here: 380 us
  waiting for transfers between devices  180 us (47%)
  local copies, waits for them, and re-layouts  67.2 us (17%)
  matrix products  63.6 us (16%)
  other arithmetic  40.1 us (10%)
  starting transfers between devices  27.9 us (7%)
    ppermute x4, waiting for transfers between devices, from_behind(): return lax.ppermute(value, axis, pairs)  180 us
    dot_general x8, matrix products, anterpolate(): jnp.einsum('pk,pkvzb->vzpb', chosen, picked, precision=precise_setting)  34.2 us
    select_n x1, other arithmetic, advance(): return jnp.where(building[None] == 1, 0.0, stepped)  23.7 us
    dot_general x8, matrix products, interpolate(): jnp.einsum('xk,xkvb->vxb', chosen, picked, precision=precise_setting)  20.1 us
    unnamed x63, local copies, waits for them, and re-layouts  18.9 us
    ppermute x4, starting transfers between devices, from_behind(): return lax.ppermute(value, axis, pairs)  13.7 us
    another operation x1, other arithmetic, local(): jnp.stack([nested_domain_states, child_east, child_pair[0], child_pair[1]])  10 us
    slice x2, local copies, waits for them, and re-layouts, extended(): last = lax.slice_in_dim(value, length - width, length, axis=dim)  9.22 us
  transfers between devices with their start and end apart: 8, of which 2 were waited for; matrix products, arithmetic and copies ran while one was open for 20% of the time, Pallas kernels for 0%

commit v1 on v0

v1 whole, which is shorter than its diff:
```python
import jax
import jax.numpy as jnp
from jax import lax
from jax.experimental import pallas as pl
from jax.experimental.pallas import tpu as pltpu
from jax.sharding import PartitionSpec as P

V, NZ, BLK, CX, K, KI, NOPS, PB = 4, 8, 128, 256, 16, 4, 8, 16
VZ = V * NZ
F32, BF16 = jnp.float32, jnp.bfloat16
PAD = 8
CHUNK = 64
VMEM_BYTES = 48 * 1024 * 1024

X_ROWS, X_PAR, X_IDX, X_ALL = 0, 64, 128, 144
Y_COLS, Y_PAR, Y_RELAY, Y_IDX, Y_RIDX, Y_ALL = 0, 128, 192, 256, 272, 288

ANY = pl.BlockSpec(memory_space=pl.ANY)
IN_VMEM = pl.BlockSpec(memory_space=pltpu.VMEM)
IN_SMEM = pl.BlockSpec(memory_space=pltpu.SMEM)
NT = (((1,), (1,)), ((), ()))
TN = (((0,), (0,)), ((), ()))


def exchange(value, axis, odd):
    pairs = []
    for a in range(odd, lax.axis_size(axis) - 1, 2):
        pairs += [(a, a + 1), (a + 1, a)]
    return lax.ppermute(value, axis, pairs)


def one_lower(value, axis):
    return lax.ppermute(value, axis, [(a, a - 1) for a in range(1, lax.axis_size(axis))])


def split(value):
    high = value.astype(BF16)
    return high, (value - high.astype(F32)).astype(BF16)


def lanes(shape):
    return lax.broadcasted_iota(jnp.int32, shape, len(shape) - 1)


def pack_kernel(parity, child, parent, tile, row, op, even, odd, to_next, to_prev, cells, stage, sems):
    copies = [pltpu.make_async_copy(child.at[pl.ds(NZ * v, NZ)], cells.at[pl.ds(NZ * v, NZ)], sems.at[v]) for v in range(V)]
    for c in copies:
        c.start()
    stage[...] = jnp.zeros_like(stage)
    stage[0, :, 0:K] = tile[...].astype(F32)
    stage[1, :, 0:K] = row[...].astype(F32)
    stage[2, :, 0:K] = op[...].astype(F32)
    index = stage[0] + pltpu.roll(stage[1], K, 1) + pltpu.roll(stage[2], 2 * K, 1)
    flag = parity[0] == 0
    for buffer in (even, odd):
        buffer[X_PAR:X_IDX] = parent[...]
        buffer[X_IDX:X_ALL] = index
    which = lanes((CX, BLK)) // 4
    edges = jnp.zeros((CX, BLK), F32)
    for v in range(V):
        copies[v].wait()
        for z in range(NZ):
            vz = NZ * v + z
            low, high = cells[vz, 0:2], cells[vz, CX - 2 : CX]
            even[2 * vz : 2 * vz + 2] = jnp.where(flag, high, low)
            odd[2 * vz : 2 * vz + 2] = jnp.where(flag, low, high)
            edges = jnp.where(which == vz, pltpu.roll(cells[vz], (4 * vz + 2) % BLK, 1), edges)
    half = CX // 2
    upper = lanes((half, BLK)) % 4 >= 2
    to_next[...] = jnp.where(upper, pltpu.roll(edges[half:], 2, 1), edges[:half])
    to_prev[...] = jnp.where(upper, edges[:half], pltpu.roll(edges[half:], BLK - 2, 1))


def join_kernel(parity, even_x, odd_x, own_even, to_next, to_prev, even, odd):
    flag_x, flag = parity[0] == 0, parity[1] == 0
    even[Y_COLS:Y_PAR] = jnp.where(flag, to_next[...], to_prev[...])
    odd[Y_COLS:Y_PAR] = jnp.where(flag, to_prev[...], to_next[...])
    relay = jnp.where(flag_x, odd_x[X_PAR:X_ALL], even_x[X_PAR:X_ALL])
    own = own_even[X_PAR:X_ALL]
    for buffer in (even, odd):
        buffer[Y_PAR:Y_RELAY] = own[:64]
        buffer[Y_RELAY:Y_IDX] = relay[:64]
        buffer[Y_IDX:Y_RIDX] = own[64:]
        buffer[Y_RIDX:Y_ALL] = relay[64:]


def main_kernel(
    parity, courant_x, courant_y, diffusion,
    child, building, own_x, even_x, odd_x, even_y, odd_y, fine_bank, coarse_bank, coarse_code, radiant,
    states, comfort, part_own, part_x, part_y,
    cells, new, walls, ground, halo, select, banks, ghost, table, fields, picked_high, picked_low, sems, out_sems,
):
    flag_x, flag_y = parity[0] == 0, parity[1] == 0
    walls_in = pltpu.make_async_copy(building, walls, sems.at[V])
    copies = [
        pltpu.make_async_copy(child.at[pl.ds(NZ * v, NZ)], cells.at[v, :, pl.ds(PAD, CX)], sems.at[v]) for v in range(V)
    ]
    copies[0].start()
    walls_in.start()
    for c in copies[1:]:
        c.start()

    prev_x = jnp.where(flag_x, odd_x[...], even_x[...])
    prev_y = jnp.where(flag_y, odd_y[...], even_y[...])
    parents = [own_x[X_PAR:X_IDX], prev_x[X_PAR:X_IDX], prev_y[Y_PAR:Y_RELAY], prev_y[Y_RELAY:Y_IDX]]
    indices = [own_x[X_IDX:X_ALL], prev_x[X_IDX:X_ALL], prev_y[Y_IDX:Y_RIDX], prev_y[Y_RIDX:Y_ALL]]

    next_x = jnp.where(flag_x, even_x[X_ROWS:X_PAR], odd_x[X_ROWS:X_PAR])
    for v in range(V):
        for z in range(NZ):
            vz = NZ * v + z
            cells[v, z, PAD - 2 : PAD] = prev_x[2 * vz : 2 * vz + 2]
            cells[v, z, PAD + CX : PAD + CX + 2] = next_x[2 * vz : 2 * vz + 2]
    half = CX // 2
    next_y = jnp.where(flag_y, even_y[Y_COLS:Y_PAR], odd_y[Y_COLS:Y_PAR])
    before = prev_y[Y_COLS:Y_PAR]
    upper = lanes((half, BLK)) % 4 >= 2
    halo[0:half] = jnp.where(upper, next_y, before)
    halo[half:CX] = jnp.where(upper, pltpu.roll(next_y, 2, 1), pltpu.roll(before, BLK - 2, 1))

    for o in range(NOPS):
        high, low = split(fine_bank[o])
        banks[0:BLK, BLK * o : BLK * (o + 1)] = high
        banks[BLK : 2 * BLK, BLK * o : BLK * (o + 1)] = low

    high, low = split(jnp.concatenate([parents[t][PB * v : PB * (v + 1)] for v in range(V) for t in range(4)], axis=0))
    for o in range(NOPS):
        bank_high, bank_low = split(coarse_bank[o])
        made = (
            lax.dot_general(high, bank_high, NT, preferred_element_type=F32)
            + lax.dot_general(high, bank_low, NT, preferred_element_type=F32)
            + lax.dot_general(low, bank_high, NT, preferred_element_type=F32)
        )
        made_high, made_low = split(made)
        for v in range(V):
            table[64 * o : 64 * (o + 1), BLK * v : BLK * (v + 1)] = made_high[64 * v : 64 * (v + 1)]
            table[512 + 64 * o : 512 + 64 * (o + 1), BLK * v : BLK * (v + 1)] = made_low[64 * v : 64 * (v + 1)]
    wanted = lax.broadcasted_iota(jnp.int32, (512, CX), 0)
    counts = jnp.zeros((512, CX), F32)
    for k in range(KI):
        counts = counts + jnp.where(coarse_code[k : k + 1, :] == wanted, 1.0, 0.0)
    counts = counts.T.astype(BF16)
    ghost[...] = jnp.dot(counts, table[0:512], preferred_element_type=F32) + jnp.dot(
        counts, table[512:1024], preferred_element_type=F32
    )

    codes = []
    for t in range(4):
        names = indices[t]
        rows = pltpu.roll(names, BLK - K, 1)
        ops = pltpu.roll(names, BLK - 2 * K, 1)
        codes.append(jnp.where(names == float(t), ops * float(CX) + rows, -1.0))
    codes = jnp.concatenate(codes, axis=0)
    spread = [jnp.broadcast_to(codes[:, k : k + 1], (64, CX)) for k in range(K)]
    place = lanes((64, CX)).astype(F32)
    for o in range(NOPS):
        total = jnp.zeros((64, CX), F32)
        for k in range(K):
            total = total + jnp.where(spread[k] == place + float(CX * o), 1.0, 0.0)
        total = total.astype(BF16)
        select[64 * o : 64 * (o + 1), 0:CX] = total
        select[64 * o : 64 * (o + 1), CX : 2 * CX] = total

    walls_in.wait()
    lane = lanes((CHUNK, BLK))

    def variable(v, carry):
        pltpu.make_async_copy(child.at[pl.ds(NZ * v, NZ)], cells.at[v, :, pl.ds(PAD, CX)], sems.at[v]).wait()
        d = diffusion[v]
        for z in range(NZ):
            sx, sy = courant_x[z], courant_y[z]
            mx, my = jnp.abs(sx), jnp.abs(sy)
            up_x, up_y = sx >= 0.0, sy >= 0.0
            near_x, near_y = 2.0 * mx - mx * mx, 2.0 * my - my * my
            far_x, far_y = 0.5 * mx * mx - 0.5 * mx, 0.5 * my * my - 0.5 * my
            own = 1.0 + (0.5 * mx * mx - 1.5 * mx) + (0.5 * my * my - 1.5 * my) - 6.0 * d
            low_x = d + jnp.where(up_x, near_x, 0.0)
            high_x = d + jnp.where(up_x, 0.0, near_x)
            low_y = d + jnp.where(up_y, near_y, 0.0)
            high_y = d + jnp.where(up_y, 0.0, near_y)
            low_far = jnp.where(up_x, far_x, 0.0)
            high_far = jnp.where(up_x, 0.0, far_x)
            first_far = jnp.where(up_y, BLK - 2, 0)
            turn_far = jnp.where(up_y, 2, BLK - 2)
            turn = BLK - 2 - (4 * (NZ * v + z)) % BLK
            turn = jnp.where(turn < 0, turn + BLK, turn)
            outside = (lane >= first_far) & (lane < first_far + 2)
            for r in range(0, CX, CHUNK):
                c = cells[v, z, PAD + r : PAD + r + CHUNK]
                edge = pltpu.roll(halo[r : r + CHUNK], turn, 1)
                total = own * c
                total = total + low_x * cells[v, z, PAD + r - 1 : PAD + r - 1 + CHUNK]
                total = total + high_x * cells[v, z, PAD + r + 1 : PAD + r + 1 + CHUNK]
                total = total + low_far * cells[v, z, PAD + r - 2 : PAD + r - 2 + CHUNK]
                total = total + high_far * cells[v, z, PAD + r + 2 : PAD + r + 2 + CHUNK]
                total = total + low_y * pltpu.roll(jnp.where(lane == BLK - 1, edge, c), 1, 1)
                total = total + high_y * pltpu.roll(jnp.where(lane == 0, edge, c), BLK - 1, 1)
                total = total + far_y * pltpu.roll(jnp.where(outside, edge, c), turn_far, 1)
                above = (
                    cells[v, z + 1, PAD + r : PAD + r + CHUNK]
                    if z < NZ - 1
                    else ghost[r : r + CHUNK, pl.ds(pl.multiple_of(BLK * v, BLK), BLK)]
                )
                if z > 0:
                    above = above + cells[v, z - 1, PAD + r : PAD + r + CHUNK]
                total = total + d * above
                total = jnp.where(walls[z, r : r + CHUNK] == 1, 0.0, total)
                new[v, z, r : r + CHUNK] = total
                high, low = split(total)
                fields[r : r + CHUNK, BLK * z : BLK * (z + 1)] = high
                fields[CX + r : CX + r + CHUNK, BLK * z : BLK * (z + 1)] = low
                if z == 0:
                    ground[v, r : r + CHUNK] = total
        pltpu.make_async_copy(new.at[v], states.at[pl.ds(NZ * v, NZ)], out_sems.at[v]).start()
        for z in range(0, NZ, 2):
            found = jnp.dot(select[...], fields[:, BLK * z : BLK * (z + 2)], preferred_element_type=F32)
            high, low = split(found)
            for o in range(NOPS):
                for e in range(2):
                    to = (slice(64 * (z + e), 64 * (z + e + 1)), slice(BLK * o, BLK * (o + 1)))
                    at = (slice(64 * o, 64 * (o + 1)), slice(BLK * e, BLK * (e + 1)))
                    picked_high[to] = high[at]
                    picked_low[to] = low[at]
        first = lax.dot_general(picked_high[...], banks[...], NT, preferred_element_type=F32)
        second = lax.dot_general(picked_low[...], banks[0:BLK], NT, preferred_element_type=F32)
        result = first[:, :BLK] + first[:, BLK:] + second
        for z in range(NZ):
            at = pl.ds(pl.multiple_of(PB * (NZ * v + z), PB), PB)
            part_own[at] = result[64 * z : 64 * z + 16]
            part_x[at] = result[64 * z + 16 : 64 * z + 32]
            part_y[0, at] = result[64 * z + 32 : 64 * z + 48]
            part_y[1, at] = result[64 * z + 48 : 64 * z + 64]
        return carry

    lax.fori_loop(0, V, variable, 0)

    for r in range(0, CX, CHUNK):
        u, w, t, h = (ground[v, r : r + CHUNK] for v in range(V))
        speed = jnp.sqrt(u * u + w * w + 0.25)
        excess = radiant[r : r + CHUNK] - t
        comfort[r : r + CHUNK] = (
            t + 0.3 * excess - 0.6 * (speed - 1.0) + 0.4 * h + 0.1 * t * excess - 0.15 * speed * excess
        )
    for v in range(V):
        pltpu.make_async_copy(new.at[v], states.at[pl.ds(NZ * v, NZ)], out_sems.at[v]).wait()


def shape(*dims):
    return jax.ShapeDtypeStruct(dims, F32)


def local(
    child_state, parent_slab, parent_above, radiative_mean_kelvin, courant_x, courant_y, diffusion, building,
    fine_tile, fine_row, fine_op, fine_bank, coarse_tile, coarse_row, coarse_op, coarse_bank,
):
    parity = jnp.stack([lax.axis_index("gx") % 2, lax.axis_index("gy") % 2]).astype(jnp.int32)
    child = child_state.reshape(VZ, CX, BLK)
    parent = parent_above.reshape(V * PB, BLK)
    params = pltpu.CompilerParams(vmem_limit_bytes=VMEM_BYTES)
    x_even, x_odd, to_next, to_prev = pl.pallas_call(
        pack_kernel,
        out_shape=(shape(X_ALL, BLK), shape(X_ALL, BLK), shape(CX // 2, BLK), shape(CX // 2, BLK)),
        in_specs=[IN_SMEM, ANY] + [IN_VMEM] * 4,
        out_specs=(IN_VMEM,) * 4,
        scratch_shapes=[
            pltpu.VMEM((VZ, CX, BLK), F32), pltpu.VMEM((3, PB, BLK), F32), pltpu.SemaphoreType.DMA((V,)),
        ],
        compiler_params=params,
    )(parity, child, parent, fine_tile, fine_row, fine_op)
    got_x_even = exchange(x_even, "gx", 0)
    got_x_odd = exchange(x_odd, "gx", 1)
    y_even, y_odd = pl.pallas_call(
        join_kernel,
        out_shape=(shape(Y_ALL, BLK), shape(Y_ALL, BLK)),
        in_specs=[IN_SMEM] + [IN_VMEM] * 5,
        out_specs=(IN_VMEM,) * 2,
        compiler_params=params,
    )(parity, got_x_even, got_x_odd, x_even, to_next, to_prev)
    got_y_odd = exchange(y_odd, "gy", 1)
    got_y_even = exchange(y_even, "gy", 0)
    coarse_code = (coarse_op * 64 + coarse_tile * PB + coarse_row).reshape(CX, KI).T
    states, comfort, part_own, part_x, part_y = pl.pallas_call(
        main_kernel,
        out_shape=(
            shape(VZ, CX, BLK), shape(CX, BLK), shape(VZ * PB, BLK), shape(VZ * PB, BLK), shape(2, VZ * PB, BLK),
        ),
        in_specs=[IN_SMEM] * 4 + [ANY] * 2 + [IN_VMEM] * 9,
        out_specs=(ANY,) + (IN_VMEM,) * 4,
        scratch_shapes=[
            pltpu.VMEM((V, NZ, CX + 2 * PAD, BLK), F32),
            pltpu.VMEM((V, NZ, CX, BLK), F32),
            pltpu.VMEM((NZ, CX, BLK), jnp.int32),
            pltpu.VMEM((V, CX, BLK), F32),
            pltpu.VMEM((CX, BLK), F32),
            pltpu.VMEM((512, 2 * CX), BF16),
            pltpu.VMEM((2 * BLK, NOPS * BLK), BF16),
            pltpu.VMEM((CX, V * BLK), F32),
            pltpu.VMEM((1024, V * BLK), BF16),
            pltpu.VMEM((2 * CX, NZ * BLK), BF16),
            pltpu.VMEM((512, NOPS * BLK), BF16),
            pltpu.VMEM((512, NOPS * BLK), BF16),
            pltpu.SemaphoreType.DMA((V + 1,)),
            pltpu.SemaphoreType.DMA((V,)),
        ],
        compiler_params=params,
    )(
        parity, courant_x, courant_y, diffusion,
        child, building, x_even, got_x_even, got_x_odd, got_y_even, got_y_odd, fine_bank, coarse_bank, coarse_code,
        radiative_mean_kelvin,
    )
    got_y = one_lower(part_y, "gy")
    got_x = one_lower(part_x + got_y[1], "gx")
    parent_new = 0.5 * parent_slab.reshape(VZ * PB, BLK) + 0.5 * ((part_own + got_y[0]) + got_x)
    return states.reshape(child_state.shape), parent_new.reshape(parent_slab.shape), comfort


def solution(mesh):
    placed = (
        P(None, None, "gx", "gy"),
        P(None, None, ("gx", "gy"), None),
        P(None, ("gx", "gy"), None),
        P("gx", "gy"),
        P(),
        P(),
        P(),
        P(None, "gx", "gy"),
        P(("gx", "gy"), None),
        P(("gx", "gy"), None),
        P(("gx", "gy"), None),
        P(),
        P("gx", "gy", None),
        P("gx", "gy", None),
        P("gx", "gy", None),
        P(),
    )
    return jax.shard_map(
        local,
        mesh=mesh,
        in_specs=placed,
        out_specs=(P(None, None, "gx", "gy"), P(None, None, ("gx", "gy"), None), P("gx", "gy")),
        check_vma=False,
    )
```

time: 386 us -> 67.2 us (0.17)
  the two profiles are of different devices: /device:TPU:45 before, /device:TPU:70 now
where the time goes in v1:
time: 67.2 us; the launch traced here: 66.1 us
  waiting for transfers between devices  26.3 us (39%)
  Pallas kernels  17.9 us (27%)
  starting transfers between devices  15.1 us (22%)
  local copies, waits for them, and re-layouts  5.08 us (8%)
  other arithmetic  0.87 us (1%)
  between operations  0.86 us (1%)
    pallas_call x1, Pallas kernels, local(): pl.pallas_call(main_kernel, out_shape=(shape(VZ, CX, BLK), shape(CX, BLK)...  15 us
    ppermute x2, waiting for transfers between devices, one_lower(): lax.ppermute(value, axis, [(a, a - 1) for a in range(1, lax.axis_size(axi...  14.4 us
    ppermute x4, waiting for transfers between devices, exchange(): return lax.ppermute(value, axis, pairs)  11.8 us
    ppermute x4, starting transfers between devices, exchange(): return lax.ppermute(value, axis, pairs)  7.89 us
    ppermute x2, starting transfers between devices, one_lower(): lax.ppermute(value, axis, [(a, a - 1) for a in range(1, lax.axis_size(axi...  7.24 us
    unnamed x32, local copies, waits for them, and re-layouts  5.08 us
    pallas_call x1, Pallas kernels, local(): pl.pallas_call(pack_kernel, out_shape=(shape(X_ALL, BLK), shape(X_ALL, BL...  2.38 us
  transfers between devices with their start and end apart: 6, of which 5 were waited for; matrix products, arithmetic and copies ran while one was open for 0% of the time, Pallas kernels for 0%

profile of v1, /device:TPU:70, one launch (start us, length us, event | category | flops | bytes accessed | tf_op | source)
XLA Modules:
  0.0 66.1 jit_solution(16764755151512575931)
XLA Ops:
  0.6 0.0 copy-start.15
  0.6 0.0 copy-start.13
  0.7 0.0 copy-start.14
  0.7 0.0 copy-start.11
  0.7 0.0 copy-start.10
  0.7 0.0 copy-start.9
  0.7 0.1 pad_add_fusion.parity
  0.8 0.0 copy-start
  0.8 2.2 %copy-done = f32[4,8,256,128]{3,2,1,0:T(8,128)S(1)} copy-done((f32[4,8,256,128]{3,2,1,0:T(8,128)S(1)}, f32[4,8,256,128]{3,2,1,0:T(8,128)}, u32[]{:S(2)}) %copy-start) | copy-done | bytes 4194328
  3.0 0.0 copy-start.5
  3.0 0.8 %copy-done.5 = f32[4,16,128]{2,1,0:T(8,128)S(1)} copy-done((f32[4,16,128]{2,1,0:T(8,128)S(1)}, f32[4,16,128]{2,1,0:T(8,128)}, u32[]{:S(2)}) %copy-start.5) | copy-done | bytes 32792
  3.7 0.0 copy-start.6
  3.7 0.7 %copy-done.6 = s32[16,16]{1,0:T(8,128)S(1)} copy-done((s32[16,16]{1,0:T(8,128)S(1)}, s32[16,16]{1,0:T(8,128)}, u32[]{:S(2)}) %copy-start.6) | copy-done | bytes 1048
  4.4 0.0 copy-start.7
  4.4 0.7 %copy-done.7 = s32[16,16]{1,0:T(8,128)S(1)} copy-done((s32[16,16]{1,0:T(8,128)S(1)}, s32[16,16]{1,0:T(8,128)}, u32[]{:S(2)}) %copy-start.7) | copy-done | bytes 1048
  5.1 0.0 copy-start.8
  5.1 0.7 %copy-done.8 = s32[16,16]{1,0:T(8,128)S(1)} copy-done((s32[16,16]{1,0:T(8,128)S(1)}, s32[16,16]{1,0:T(8,128)}, u32[]{:S(2)}) %copy-start.8) | copy-done | bytes 1048
  5.8 0.0 copy-start.1
  5.8 0.0 copy-start.2
  5.8 0.0 copy-start.3
  5.8 0.0 copy-start.4
  5.8 2.4 %shard_map.175 = (f32[144,128]{1,0:T(8,128)S(1)}, f32[144,128]{1,0:T(8,128)S(1)}, f32[128,128]{1,0:T(8,128)S(1)}, f32[128,128]{1,0:T(8,128)S(1)}) custom-call(s32[2]{0:T(128)S(1)} %pad_add_fusion.parity, f32[32,256,128]{2,1,0:T(8,128)S(1)} %bitcast.27, f32[64,128]{1,0:T(8,128)S(1)} %bitcast.28, s32[16,16]{1,0:T(8,128)S(1)} %copy-done.6, ...), custom_call_target="tpu_custom_call" | custom-call | tf_op jit(solution)/shard_map/pallas_call | solution.py:260
  8.2 0.0 copy-start.12
  8.2 5.5 %collective-permute-start.1 = (f32[144,128]{1,0:T(8,128)S(1)}, f32[144,128]{1,0:T(8,128)S(1)}, u32[]{:S(2)}, u32[]{:S(2)}) collective-permute-start(f32[144,128]{1,0:T(8,128)S(1)} %get-tuple-element.15), channel_id=1, source_target_pairs={{16,32},{32,16},{48,64},{64,48},{80,96},{96,80},{17,33},{33,17},{4... | collective-permute-start | bytes 221192 | tf_op jit(solution)/shard_map/ppermute | solution.py:29
  13.7 0.1 collective-permute-start
  13.8 3.2 %collective-permute-done.1.odd_x = f32[144,128]{1,0:T(8,128)S(1)} collective-permute-done((f32[144,128]{1,0:T(8,128)S(1)}, f32[144,128]{1,0:T(8,128)S(1)}, u32[]{:S(2)}, u32[]{:S(2)}) %collective-permute-start.1) | collective-permute-done | bytes 73760 | tf_op jit(solution)/shard_map/ppermute | solution.py:29
  17.0 2.7 %collective-permute-done.even_x = f32[144,128]{1,0:T(8,128)S(1)} collective-permute-done((f32[144,128]{1,0:T(8,128)S(1)}, f32[144,128]{1,0:T(8,128)S(1)}, u32[]{:S(2)}, u32[]{:S(2)}) %collective-permute-start) | collective-permute-done | bytes 73760 | tf_op jit(solution)/shard_map/ppermute | solution.py:29
  19.7 0.6 shard_map.176
  20.3 0.1 collective-permute-start.2
  20.3 2.2 %collective-permute-start.3 = (f32[288,128]{1,0:T(8,128)S(1)}, f32[288,128]{1,0:T(8,128)S(1)}, u32[]{:S(2)}, u32[]{:S(2)}) collective-permute-start(f32[288,128]{1,0:T(8,128)S(1)} %get-tuple-element.19), channel_id=1, source_target_pairs={{1,2},{2,1},{3,4},{4,3},{5,6},{6,5},{7,8},{8,7},{9,10},{10,9},{11,... | collective-permute-start | bytes 442376 | tf_op jit(solution)/shard_map/ppermute | solution.py:29
  22.6 0.0 copy-done.15
  22.6 0.0 copy-done.13
  22.6 0.0 copy-done.14
  22.6 0.0 collective-permute-done.2.even_y
  22.6 6.0 %collective-permute-done.3.odd_y = f32[288,128]{1,0:T(8,128)S(1)} collective-permute-done((f32[288,128]{1,0:T(8,128)S(1)}, f32[288,128]{1,0:T(8,128)S(1)}, u32[]{:S(2)}, u32[]{:S(2)}) %collective-permute-start.3) | collective-permute-done | bytes 147488 | tf_op jit(solution)/shard_map/ppermute | solution.py:29
  28.6 0.0 copy-done.11
  28.6 0.0 copy-done.10
  28.6 0.0 copy-done.9
  28.6 0.0 copy-done.1
  28.6 0.0 copy-done.2
  28.6 0.0 copy-done.3
  28.6 0.0 copy-done.4
  28.6 15.0 %shard_map.177 = (f32[32,256,128]{2,1,0:T(8,128)}, f32[256,128]{1,0:T(8,128)}, f32[512,128]{1,0:T(8,128)S(1)}, f32[512,128]{1,0:T(8,128)S(1)}, f32[2,512,128]{2,1,0:T(8,128)S(1)}) custom-call(s32[2]{0:T(128)S(1)} %pad_add_fusion.parity, f32[8]{0:T(128)S(1)} %copy-done.9, f32[8]{0:T(128)S(1)} %copy-done.10, f32[4]{0:T(128)S(1)} %copy-done.11, ...), custom_call_target="tpu_custom_call" | custom-call | tf_op jit(solution)/shard_map/pallas_call | solution.py:282
  43.6 2.7 %collective-permute-start.4 = (f32[2,512,128]{2,1,0:T(8,128)S(1)}, f32[2,512,128]{2,1,0:T(8,128)S(1)}, u32[]{:S(2)}, u32[]{:S(2)}) collective-permute-start(f32[2,512,128]{2,1,0:T(8,128)S(1)} %get-tuple-element.22), channel_id=1, source_target_pairs={{1,0},{2,1},{3,2},{4,3},{5,4},{6,5},{7,6},{8,7},{9,8},{10,9},{11,1... | collective-permute-start | bytes 1572872 | tf_op jit(solution)/shard_map/ppermute | solution.py:33
  46.3 6.7 %collective-permute-done.4 = f32[2,512,128]{2,1,0:T(8,128)S(1)} collective-permute-done((f32[2,512,128]{2,1,0:T(8,128)S(1)}, f32[2,512,128]{2,1,0:T(8,128)S(1)}, u32[]{:S(2)}, u32[]{:S(2)}) %collective-permute-start.4) | collective-permute-done | bytes 524320 | tf_op jit(solution)/shard_map/ppermute | solution.py:33
  53.1 4.5 %collective-permute-start.5 = (f32[512,128]{1,0:T(8,128)S(1)}, f32[512,128]{1,0:T(8,128)S(1)}, u32[]{:S(2)}, u32[]{:S(2)}) collective-permute-start(f32[512,128]{1,0:T(8,128)S(1)} %fusion), channel_id=1, source_target_pairs={{16,0},{32,16},{48,32},{64,48},{80,64},{96,80},{112,96},{17,1},{33... | collective-permute-start | bytes 786440 | tf_op jit(solution)/shard_map/ppermute | solution.py:33
  57.6 7.8 %collective-permute-done.5 = f32[512,128]{1,0:T(8,128)S(1)} collective-permute-done((f32[512,128]{1,0:T(8,128)S(1)}, f32[512,128]{1,0:T(8,128)S(1)}, u32[]{:S(2)}, u32[]{:S(2)}) %collective-permute-start.5) | collective-permute-done | bytes 262176 | tf_op jit(solution)/shard_map/ppermute | solution.py:33
  65.4 0.0 copy-done.12
  65.4 0.8 %fusion.4 = f32[512,128]{1,0:T(8,128)} fusion(f32[512,128]{1,0:T(8,128)S(1)} %collective-permute-done.5, f32[512,128]{1,0:T(8,128)S(1)} %get-tuple-element.21, f32[2,512,128]{2,1,0:T(8,128)S(1)} %collective-permute-done.4, f32[4,8,16,128]{3,2,1,0:T(8,128)S(1)} %copy-done.12), kind=kLoop, calls=%fused_computation.6 | loop fusion | flops 262144 | bytes 1310720 | tf_op jit(solution)/shard_map/add | solution.py:313
  (2 shorter events, 0.0 us)
Async XLA Ops:
  0.6 21.9 %copy-start.15 = (s32[256,1,4]{0,2,1:T(4,128)S(1)}, s32[256,1,4]{0,2,1:T(4,128)}, u32[]{:S(2)}) copy-start(s32[256,1,4]{0,2,1:T(4,128)} %param.30) | copy-start | bytes 12292
  0.6 21.9 %copy-start.13 = (s32[256,1,4]{0,2,1:T(4,128)S(1)}, s32[256,1,4]{0,2,1:T(4,128)}, u32[]{:S(2)}) copy-start(s32[256,1,4]{0,2,1:T(4,128)} %param.29) | copy-start | bytes 12292
  0.7 21.9 %copy-start.14 = (s32[256,1,4]{0,2,1:T(4,128)S(1)}, s32[256,1,4]{0,2,1:T(4,128)}, u32[]{:S(2)}) copy-start(s32[256,1,4]{0,2,1:T(4,128)} %param.28) | copy-start | bytes 12292
  0.7 27.9 %copy-start.11 = (f32[4]{0:T(128)S(1)}, f32[4]{0:T(128)}, u32[]{:S(2)}) copy-start(f32[4]{0:T(128)} %diffusion.1) | copy-start | bytes 52
  0.7 27.9 %copy-start.10 = (f32[8]{0:T(128)S(1)}, f32[8]{0:T(128)}, u32[]{:S(2)}) copy-start(f32[8]{0:T(128)} %courant_y.1) | copy-start | bytes 100
  0.7 27.9 %copy-start.9 = (f32[8]{0:T(128)S(1)}, f32[8]{0:T(128)}, u32[]{:S(2)}) copy-start(f32[8]{0:T(128)} %courant_x.1) | copy-start | bytes 100
  0.8 2.2 %copy-start = (f32[4,8,256,128]{3,2,1,0:T(8,128)S(1)}, f32[4,8,256,128]{3,2,1,0:T(8,128)}, u32[]{:S(2)}) copy-start(f32[4,8,256,128]{3,2,1,0:T(8,128)} %param.16) | copy-start | bytes 12582916
  3.0 0.8 %copy-start.5 = (f32[4,16,128]{2,1,0:T(8,128)S(1)}, f32[4,16,128]{2,1,0:T(8,128)}, u32[]{:S(2)}) copy-start(f32[4,16,128]{2,1,0:T(8,128)} %param.18) | copy-start | bytes 98308
  3.7 0.7 %copy-start.6 = (s32[16,16]{1,0:T(8,128)S(1)}, s32[16,16]{1,0:T(8,128)}, u32[]{:S(2)}) copy-start(s32[16,16]{1,0:T(8,128)} %tile.1) | copy-start | bytes 3076
  4.4 0.7 %copy-start.7 = (s32[16,16]{1,0:T(8,128)S(1)}, s32[16,16]{1,0:T(8,128)}, u32[]{:S(2)}) copy-start(s32[16,16]{1,0:T(8,128)} %row.1) | copy-start | bytes 3076
  5.1 0.7 %copy-start.8 = (s32[16,16]{1,0:T(8,128)S(1)}, s32[16,16]{1,0:T(8,128)}, u32[]{:S(2)}) copy-start(s32[16,16]{1,0:T(8,128)} %op.1) | copy-start | bytes 3076
  5.8 22.8 %copy-start.1 = (s32[8,256,128]{2,1,0:T(8,128)S(1)}, s32[8,256,128]{2,1,0:T(8,128)}, u32[]{:S(2)}) copy-start(s32[8,256,128]{2,1,0:T(8,128)} %building.1) | copy-start | bytes 3145732
  5.8 22.8 %copy-start.2 = (f32[8,128,128]{2,1,0:T(8,128)S(1)}, f32[8,128,128]{2,1,0:T(8,128)}, u32[]{:S(2)}) copy-start(f32[8,128,128]{2,1,0:T(8,128)} %fine_bank.1) | copy-start | bytes 1572868
  5.8 22.8 %copy-start.3 = (f32[8,128,128]{2,1,0:T(8,128)S(1)}, f32[8,128,128]{2,1,0:T(8,128)}, u32[]{:S(2)}) copy-start(f32[8,128,128]{2,1,0:T(8,128)} %coarse_bank.1) | copy-start | bytes 1572868
  5.8 22.8 %copy-start.4 = (f32[256,128]{1,0:T(8,128)S(1)}, f32[256,128]{1,0:T(8,128)}, u32[]{:S(2)}) copy-start(f32[256,128]{1,0:T(8,128)} %radiant.1) | copy-start | bytes 393220
  8.2 57.2 %copy-start.12 = (f32[4,8,16,128]{3,2,1,0:T(8,128)S(1)}, f32[4,8,16,128]{3,2,1,0:T(8,128)}, u32[]{:S(2)}) copy-start(f32[4,8,16,128]{3,2,1,0:T(8,128)} %param.17) | copy-start | bytes 786436
  8.2 8.8 %collective-permute-start.1 = (f32[144,128]{1,0:T(8,128)S(1)}, f32[144,128]{1,0:T(8,128)S(1)}, u32[]{:S(2)}, u32[]{:S(2)}) collective-permute-start(f32[144,128]{1,0:T(8,128)S(1)} %get-tuple-element.15), channel_id=1, source_target_pairs={{16,32},{32,16},{48,64},{64,48},{80,96},{96,80},{17,33},{33,17},{4... | collective-permute-start | bytes 221192 | tf_op jit(solution)/shard_map/ppermute | solution.py:29
  13.7 5.9 %collective-permute-start = (f32[144,128]{1,0:T(8,128)S(1)}, f32[144,128]{1,0:T(8,128)S(1)}, u32[]{:S(2)}, u32[]{:S(2)}) collective-permute-start(f32[144,128]{1,0:T(8,128)S(1)} %get-tuple-element.14.own_even.own_x), channel_id=1, source_target_pairs={{0,16},{16,0},{32,48},{48,32},{64,80},{80,64},{96,112},{112,96},{1... | collective-permute-start | bytes 221192 | tf_op jit(solution)/shard_map/ppermute | solution.py:29
  20.3 2.4 %collective-permute-start.2 = (f32[288,128]{1,0:T(8,128)S(1)}, f32[288,128]{1,0:T(8,128)S(1)}, u32[]{:S(2)}, u32[]{:S(2)}) collective-permute-start(f32[288,128]{1,0:T(8,128)S(1)} %get-tuple-element.18), channel_id=1, source_target_pairs={{0,1},{1,0},{2,3},{3,2},{4,5},{5,4},{6,7},{7,6},{8,9},{9,8},{10,11... | collective-permute-start | bytes 442376 | tf_op jit(solution)/shard_map/ppermute | solution.py:29
  20.3 8.2 %collective-permute-start.3 = (f32[288,128]{1,0:T(8,128)S(1)}, f32[288,128]{1,0:T(8,128)S(1)}, u32[]{:S(2)}, u32[]{:S(2)}) collective-permute-start(f32[288,128]{1,0:T(8,128)S(1)} %get-tuple-element.19), channel_id=1, source_target_pairs={{1,2},{2,1},{3,4},{4,3},{5,6},{6,5},{7,8},{8,7},{9,10},{10,9},{11,... | collective-permute-start | bytes 442376 | tf_op jit(solution)/shard_map/ppermute | solution.py:29
  43.6 9.4 %collective-permute-start.4 = (f32[2,512,128]{2,1,0:T(8,128)S(1)}, f32[2,512,128]{2,1,0:T(8,128)S(1)}, u32[]{:S(2)}, u32[]{:S(2)}) collective-permute-start(f32[2,512,128]{2,1,0:T(8,128)S(1)} %get-tuple-element.22), channel_id=1, source_target_pairs={{1,0},{2,1},{3,2},{4,3},{5,4},{6,5},{7,6},{8,7},{9,8},{10,9},{11,1... | collective-permute-start | bytes 1572872 | tf_op jit(solution)/shard_map/ppermute | solution.py:33
  53.1 12.3 %collective-permute-start.5 = (f32[512,128]{1,0:T(8,128)S(1)}, f32[512,128]{1,0:T(8,128)S(1)}, u32[]{:S(2)}, u32[]{:S(2)}) collective-permute-start(f32[512,128]{1,0:T(8,128)S(1)} %fusion), channel_id=1, source_target_pairs={{16,0},{32,16},{48,32},{64,48},{80,64},{96,80},{112,96},{17,1},{33... | collective-permute-start | bytes 786440 | tf_op jit(solution)/shard_map/ppermute | solution.py:33

commit v2 on v1

v2 whole, which is shorter than its diff:
```python
import jax
import jax.numpy as jnp
from jax import lax
from jax.experimental import pallas as pl
from jax.experimental.pallas import tpu as pltpu
from jax.sharding import PartitionSpec as P

V, NZ, BLK, CX, K, KI, NOPS, PB = 4, 8, 128, 256, 16, 4, 8, 16
VZ = V * NZ
F32, BF16 = jnp.float32, jnp.bfloat16
PAD = 8
CHUNK = 64
VMEM_BYTES = 32 * 1024 * 1024

X_ROWS, X_PAR, X_IDX, X_ALL = 0, 64, 128, 144
Y_COLS, Y_PAR, Y_RELAY, Y_IDX, Y_RIDX, Y_ALL = 0, 128, 192, 256, 272, 288

IN_HBM = pl.BlockSpec(memory_space=pltpu.HBM)
IN_VMEM = pl.BlockSpec(memory_space=pltpu.VMEM)
IN_SMEM = pl.BlockSpec(memory_space=pltpu.SMEM)
NT = (((1,), (1,)), ((), ()))
TN = (((0,), (0,)), ((), ()))


def exchange(value, axis, odd):
    pairs = []
    for a in range(odd, lax.axis_size(axis) - 1, 2):
        pairs += [(a, a + 1), (a + 1, a)]
    return lax.ppermute(value, axis, pairs)


def one_lower(value, axis):
    return lax.ppermute(value, axis, [(a, a - 1) for a in range(1, lax.axis_size(axis))])


def diagonal():
    nx, ny = lax.axis_size("gx"), lax.axis_size("gy")
    return [(i * ny + j, (i - 1) * ny + j - 1) for i in range(1, nx) for j in range(1, ny)]


def split(value):
    high = value.astype(BF16)
    return high, (value - high.astype(F32)).astype(BF16)


def lanes(shape):
    return lax.broadcasted_iota(jnp.int32, shape, len(shape) - 1)


def rows_kernel(parity, child, parent, tile, row, op, even, odd, first, last, blocks, names, stage, sems):
    copies = [
        pltpu.make_async_copy(child.at[:, pl.ds(0, 8)], first, sems.at[0]),
        pltpu.make_async_copy(child.at[:, pl.ds(CX - 8, 8)], last, sems.at[1]),
        pltpu.make_async_copy(parent, blocks, sems.at[2]),
    ] + [pltpu.make_async_copy(a, names.at[i], sems.at[3 + i]) for i, a in enumerate((tile, row, op))]
    for c in copies:
        c.start()
    stage[...] = jnp.zeros_like(stage)
    for c in copies:
        c.wait()
    for i in range(3):
        stage[i, :, 0:K] = names[i].astype(F32)
    index = stage[0] + pltpu.roll(stage[1], K, 1) + pltpu.roll(stage[2], 2 * K, 1)
    flag = parity[0] == 0
    for buffer in (even, odd):
        buffer[X_PAR:X_IDX] = blocks[...]
        buffer[X_IDX:X_ALL] = index
    for vz in range(VZ):
        low, high = first[vz, 0:2], last[vz, 6:8]
        even[2 * vz : 2 * vz + 2] = jnp.where(flag, high, low)
        odd[2 * vz : 2 * vz + 2] = jnp.where(flag, low, high)


def edges_kernel(child, fine_bank, coarse_bank, code, cells, to_next, to_prev, banks, coarse_banks, counts, fine, coarse, sems):
    copies = [
        pltpu.make_async_copy(child.at[pl.ds(NZ * v, NZ)], cells.at[pl.ds(NZ * v, NZ), pl.ds(PAD, CX)], sems.at[v])
        for v in range(V)
    ] + [pltpu.make_async_copy(fine_bank, fine, sems.at[V]), pltpu.make_async_copy(coarse_bank, coarse, sems.at[V + 1])]
    for c in copies:
        c.start()
    for vz in range(VZ):
        cells[vz, 0:PAD] = jnp.zeros((PAD, BLK), F32)
        cells[vz, PAD + CX : PAD + CX + PAD] = jnp.zeros((PAD, BLK), F32)
    wanted = lax.broadcasted_iota(jnp.int32, (512, CX), 0)
    total = jnp.zeros((512, CX), F32)
    for k in range(KI):
        total = total + jnp.where(code[k : k + 1, :] == wanted, 1.0, 0.0)
    counts[...] = total.T.astype(BF16)
    which = lanes((CX, BLK)) // 4
    edges = jnp.zeros((CX, BLK), F32)
    for v in range(V):
        copies[v].wait()
        for z in range(NZ):
            vz = NZ * v + z
            edges = jnp.where(which == vz, pltpu.roll(cells[vz, PAD : PAD + CX], (4 * vz + 2) % BLK, 1), edges)
    half = CX // 2
    upper = lanes((half, BLK)) % 4 >= 2
    to_next[...] = jnp.where(upper, pltpu.roll(edges[half:], 2, 1), edges[:half])
    to_prev[...] = jnp.where(upper, edges[:half], pltpu.roll(edges[half:], BLK - 2, 1))
    copies[V].wait()
    copies[V + 1].wait()
    for o in range(NOPS):
        high, low = split(fine[o])
        banks[0:BLK, BLK * o : BLK * (o + 1)] = high
        banks[BLK : 2 * BLK, BLK * o : BLK * (o + 1)] = low
        high, low = split(coarse[o])
        coarse_banks[0, BLK * o : BLK * (o + 1)] = high
        coarse_banks[1, BLK * o : BLK * (o + 1)] = low


def join_kernel(parity, even_x, odd_x, own_even, to_next, to_prev, even, odd):
    flag_x, flag = parity[0] == 0, parity[1] == 0
    even[Y_COLS:Y_PAR] = jnp.where(flag, to_next[...], to_prev[...])
    odd[Y_COLS:Y_PAR] = jnp.where(flag, to_prev[...], to_next[...])
    relay = jnp.where(flag_x, odd_x[X_PAR:X_ALL], even_x[X_PAR:X_ALL])
    own = own_even[X_PAR:X_ALL]
    for buffer in (even, odd):
        buffer[Y_PAR:Y_RELAY] = own[:64]
        buffer[Y_RELAY:Y_IDX] = relay[:64]
        buffer[Y_IDX:Y_RIDX] = own[64:]
        buffer[Y_RIDX:Y_ALL] = relay[64:]


def coefficients(courant):
    size = jnp.abs(courant)
    half = 0.5 * size
    return half * size - 1.5 * size, 2.0 * size - size * size, half * size - half


def inner_kernel(courant_x, courant_y, diffusion, cells, after, inner):
    del after
    lane = lanes((8, BLK))[0:1]

    def variable(v, carry):
        d = diffusion[v]
        for z in range(NZ):
            sx, sy = courant_x[z], courant_y[z]
            own_x, near_x, far_x = coefficients(sx)
            own_y, near_y, far_y = coefficients(sy)
            up_x, up_y = sx >= 0.0, sy >= 0.0
            own = 1.0 + own_x + own_y - 6.0 * d
            low_x = d + jnp.where(up_x, near_x, 0.0)
            high_x = d + jnp.where(up_x, 0.0, near_x)
            low_far = jnp.where(up_x, far_x, 0.0)
            high_far = jnp.where(up_x, 0.0, far_x)
            low_y = jnp.where(lane == 0, 0.0, d + jnp.where(up_y, near_y, 0.0))
            high_y = jnp.where(lane == BLK - 1, 0.0, d + jnp.where(up_y, 0.0, near_y))
            outside = jnp.where(up_y, 0, BLK - 2)
            far = jnp.where((lane >= outside) & (lane < outside + 2), 0.0, far_y)
            turn_far = jnp.where(up_y, 2, BLK - 2)
            vz = NZ * v + z
            for r in range(PAD, PAD + CX, CHUNK):
                c = cells[vz, r : r + CHUNK]
                total = own * c
                total = total + low_x * cells[vz, r - 1 : r - 1 + CHUNK]
                total = total + high_x * cells[vz, r + 1 : r + 1 + CHUNK]
                total = total + low_far * cells[vz, r - 2 : r - 2 + CHUNK]
                total = total + high_far * cells[vz, r + 2 : r + 2 + CHUNK]
                total = total + low_y * pltpu.roll(c, 1, 1)
                total = total + high_y * pltpu.roll(c, BLK - 1, 1)
                total = total + far * pltpu.roll(c, turn_far, 1)
                beside = None
                if z < NZ - 1:
                    beside = cells[vz + 1, r : r + CHUNK]
                if z > 0:
                    below = cells[vz - 1, r : r + CHUNK]
                    beside = below if beside is None else beside + below
                inner[vz, r - PAD : r - PAD + CHUNK] = total + d * beside
        return carry

    lax.fori_loop(0, V, variable, 0)


def per_level(values, level):
    out = jnp.zeros(level.shape, F32)
    for z in range(NZ):
        out = jnp.where(level == z, values[z], out)
    return out


def main_kernel(
    parity, courant_x, courant_y, diffusion,
    inner, building, own_x, even_x, odd_x, even_y, odd_y, banks, coarse_banks, counts,
    states, ground, part_own, part_x, part_y, part_both,
    new, walls, above_fix, below_fix, side_fix, select, ghost, table, fields, picked_high, picked_low, wall_sem, out_sems,
):
    flag_x, flag_y = parity[0] == 0, parity[1] == 0
    walls_in = pltpu.make_async_copy(building, walls, wall_sem)
    walls_in.start()

    prev_x = jnp.where(flag_x, odd_x[...], even_x[...])
    prev_y = jnp.where(flag_y, odd_y[...], even_y[...])
    parents = [own_x[X_PAR:X_IDX], prev_x[X_PAR:X_IDX], prev_y[Y_PAR:Y_RELAY], prev_y[Y_RELAY:Y_IDX]]
    indices = [own_x[X_IDX:X_ALL], prev_x[X_IDX:X_ALL], prev_y[Y_IDX:Y_RIDX], prev_y[Y_RIDX:Y_ALL]]

    def weights(courant, level, variable):
        d = jnp.zeros(level.shape, F32)
        for v in range(V):
            d = jnp.where(variable == v, diffusion[v], d)
        s = per_level(courant, level)
        _, near, far = coefficients(s)
        up = s >= 0.0
        return (
            d + jnp.where(up, near, 0.0), d + jnp.where(up, 0.0, near), jnp.where(up, far, 0.0), jnp.where(up, 0.0, far),
        )

    next_rows = jnp.where(flag_x, even_x[X_ROWS:X_PAR], odd_x[X_ROWS:X_PAR])
    prev_rows = prev_x[X_ROWS:X_PAR]
    line = lax.broadcasted_iota(jnp.int32, (2 * VZ, BLK), 0)
    low, high, low_far, high_far = weights(courant_x, (line // 2) % NZ, line // (2 * NZ))
    first = line % 2 == 0
    above_fix[...] = low_far * prev_rows + jnp.where(first, low * pltpu.roll(prev_rows, 2 * VZ - 1, 0), 0.0)
    below_fix[...] = high_far * next_rows + jnp.where(first, 0.0, high * pltpu.roll(next_rows, 1, 0))

    half = CX // 2
    next_y = jnp.where(flag_y, even_y[Y_COLS:Y_PAR], odd_y[Y_COLS:Y_PAR])
    before = prev_y[Y_COLS:Y_PAR]
    upper = lanes((half, BLK)) % 4 >= 2
    lane = lanes((8, BLK))
    low, high, low_far, high_far = (w[0:1] for w in weights(courant_y, (lane // 4) % NZ, lane // (4 * NZ)))
    place = lane[0:1] % 4
    by_minus_2 = jnp.where(place < 2, high_far, 0.0)
    by_minus_1 = jnp.where(place == 1, high, 0.0)
    by_plus_1 = jnp.where(place == 2, low, 0.0)
    by_plus_2 = jnp.where(place >= 2, low_far, 0.0)
    for part in range(2):
        if part == 0:
            columns = jnp.where(upper, next_y, before)
        else:
            columns = jnp.where(upper, pltpu.roll(next_y, 2, 1), pltpu.roll(before, BLK - 2, 1))
        side_fix[half * part : half * (part + 1)] = (
            by_minus_2 * pltpu.roll(columns, BLK - 2, 1)
            + by_minus_1 * pltpu.roll(columns, BLK - 1, 1)
            + by_plus_1 * pltpu.roll(columns, 1, 1)
            + by_plus_2 * pltpu.roll(columns, 2, 1)
        )

    high, low = split(jnp.concatenate([parents[t][PB * v : PB * (v + 1)] for v in range(V) for t in range(4)], axis=0))
    for o in range(NOPS):
        bank_high, bank_low = (coarse_banks[i, BLK * o : BLK * (o + 1)] for i in range(2))
        made = (
            lax.dot_general(high, bank_high, NT, preferred_element_type=F32)
            + lax.dot_general(high, bank_low, NT, preferred_element_type=F32)
            + lax.dot_general(low, bank_high, NT, preferred_element_type=F32)
        )
        made_high, made_low = split(made)
        for v in range(V):
            table[64 * o : 64 * (o + 1), BLK * v : BLK * (v + 1)] = made_high[64 * v : 64 * (v + 1)]
            table[512 + 64 * o : 512 + 64 * (o + 1), BLK * v : BLK * (v + 1)] = made_low[64 * v : 64 * (v + 1)]
    ghost[...] = jnp.dot(counts[...], table[0:512], preferred_element_type=F32) + jnp.dot(
        counts[...], table[512:1024], preferred_element_type=F32
    )

    codes = []
    for t in range(4):
        names = indices[t]
        rows = pltpu.roll(names, BLK - K, 1)
        ops = pltpu.roll(names, BLK - 2 * K, 1)
        codes.append(jnp.where(names == float(t), ops * float(CX) + rows, -1.0))
    codes = jnp.concatenate(codes, axis=0)
    spread = [jnp.broadcast_to(codes[:, k : k + 1], (64, CX)) for k in range(K)]
    cell = lanes((64, CX)).astype(F32)
    for o in range(NOPS):
        total = jnp.zeros((64, CX), F32)
        for k in range(K):
            total = total + jnp.where(spread[k] == cell + float(CX * o), 1.0, 0.0)
        total = total.astype(BF16)
        select[64 * o : 64 * (o + 1), 0:CX] = total
        select[64 * o : 64 * (o + 1), CX : 2 * CX] = total

    walls_in.wait()
    at_edge = (lanes((CHUNK, BLK)) + 2) % BLK < 4
    no_rows = jnp.zeros((6, BLK), F32)

    def variable(v, carry):
        d = diffusion[v]
        for z in range(NZ):
            vz = NZ * v + z
            turn = (2 * BLK - 2 - 4 * vz) % BLK
            for r in range(0, CX, CHUNK):
                total = inner[vz, r : r + CHUNK]
                total = total + jnp.where(at_edge, pltpu.roll(side_fix[r : r + CHUNK], turn, 1), 0.0)
                if z == NZ - 1:
                    total = total + d * ghost[r : r + CHUNK, pl.ds(pl.multiple_of(BLK * v, BLK), BLK)]
                if r == 0:
                    fix = jnp.concatenate([above_fix[pl.ds(2 * vz, 2)], no_rows], axis=0)
                    total = jnp.concatenate([total[:8] + fix, total[8:]], axis=0)
                if r == CX - CHUNK:
                    fix = jnp.concatenate([no_rows, below_fix[pl.ds(2 * vz, 2)]], axis=0)
                    total = jnp.concatenate([total[:-8], total[-8:] + fix], axis=0)
                total = jnp.where(walls[z, r : r + CHUNK] == 1, 0.0, total)
                new[vz, r : r + CHUNK] = total
                high, low = split(total)
                fields[r : r + CHUNK, BLK * z : BLK * (z + 1)] = high
                fields[CX + r : CX + r + CHUNK, BLK * z : BLK * (z + 1)] = low
                if z == 0:
                    ground[v, r : r + CHUNK] = total
        pltpu.make_async_copy(new.at[pl.ds(NZ * v, NZ)], states.at[pl.ds(NZ * v, NZ)], out_sems.at[v]).start()
        for z in range(0, NZ, 2):
            found = jnp.dot(select[...], fields[:, BLK * z : BLK * (z + 2)], preferred_element_type=F32)
            high, low = split(found)
            for o in range(NOPS):
                for e in range(2):
                    to = (slice(64 * (z + e), 64 * (z + e + 1)), slice(BLK * o, BLK * (o + 1)))
                    at = (slice(64 * o, 64 * (o + 1)), slice(BLK * e, BLK * (e + 1)))
                    picked_high[to] = high[at]
                    picked_low[to] = low[at]
        both = lax.dot_general(picked_high[...], banks[...], NT, preferred_element_type=F32)
        rest = lax.dot_general(picked_low[...], banks[0:BLK], NT, preferred_element_type=F32)
        result = both[:, :BLK] + both[:, BLK:] + rest
        for z in range(NZ):
            at = pl.ds(pl.multiple_of(PB * (NZ * v + z), PB), PB)
            for i, part in enumerate((part_own, part_x, part_y, part_both)):
                part[at] = result[64 * z + PB * i : 64 * z + PB * (i + 1)]
        return carry

    lax.fori_loop(0, V, variable, 0)
    for v in range(V):
        pltpu.make_async_copy(new.at[pl.ds(NZ * v, NZ)], states.at[pl.ds(NZ * v, NZ)], out_sems.at[v]).wait()


def comfort_kernel(ground, radiant, slab, part_own, comfort, so_far):
    u, w, t, h = (ground[v] for v in range(V))
    speed = jnp.sqrt(u * u + w * w + 0.25)
    excess = radiant[...] - t
    comfort[...] = t + 0.3 * excess - 0.6 * (speed - 1.0) + 0.4 * h + 0.1 * t * excess - 0.15 * speed * excess
    so_far[...] = 0.5 * slab[...] + 0.5 * part_own[...]


def shape(*dims, kind=F32):
    return jax.ShapeDtypeStruct(dims, kind)


def local(
    child_state, parent_slab, parent_above, radiative_mean_kelvin, courant_x, courant_y, diffusion, building,
    fine_tile, fine_row, fine_op, fine_bank, coarse_tile, coarse_row, coarse_op, coarse_bank,
):
    parity = jnp.stack([lax.axis_index("gx") % 2, lax.axis_index("gy") % 2]).astype(jnp.int32)
    child = child_state.reshape(VZ, CX, BLK)
    parent = parent_above.reshape(V * PB, BLK)
    params = pltpu.CompilerParams(vmem_limit_bytes=VMEM_BYTES)
    x_even, x_odd = pl.pallas_call(
        rows_kernel,
        out_shape=(shape(X_ALL, BLK), shape(X_ALL, BLK)),
        in_specs=[IN_SMEM] + [IN_HBM] * 5,
        out_specs=(IN_VMEM,) * 2,
        scratch_shapes=[
            pltpu.VMEM((VZ, 8, BLK), F32), pltpu.VMEM((VZ, 8, BLK), F32), pltpu.VMEM((V * PB, BLK), F32),
            pltpu.VMEM((3, PB, K), jnp.int32), pltpu.VMEM((3, PB, BLK), F32), pltpu.SemaphoreType.DMA((6,)),
        ],
        compiler_params=pltpu.CompilerParams(vmem_limit_bytes=56 * 1024 * 1024),
    )(parity, child, parent, fine_tile, fine_row, fine_op)
    got_x_even = exchange(x_even, "gx", 0)
    got_x_odd = exchange(x_odd, "gx", 1)
    coarse_code = (coarse_op * 64 + coarse_tile * PB + coarse_row).reshape(CX, KI).T
    cells, to_next, to_prev, banks, coarse_banks, counts = pl.pallas_call(
        edges_kernel,
        out_shape=(
            shape(VZ, CX + 2 * PAD, BLK), shape(CX // 2, BLK), shape(CX // 2, BLK),
            shape(2 * BLK, NOPS * BLK, kind=BF16), shape(2, NOPS * BLK, BLK, kind=BF16), shape(CX, 512, kind=BF16),
        ),
        in_specs=[IN_HBM] * 3 + [IN_VMEM],
        out_specs=(IN_VMEM,) * 6,
        scratch_shapes=[
            pltpu.VMEM((NOPS, BLK, BLK), F32), pltpu.VMEM((NOPS, BLK, BLK), F32), pltpu.SemaphoreType.DMA((V + 2,)),
        ],
        compiler_params=params,
    )(child, fine_bank, coarse_bank, coarse_code)
    y_even, y_odd = pl.pallas_call(
        join_kernel,
        out_shape=(shape(Y_ALL, BLK), shape(Y_ALL, BLK)),
        in_specs=[IN_SMEM] + [IN_VMEM] * 5,
        out_specs=(IN_VMEM,) * 2,
        compiler_params=params,
    )(parity, got_x_even, got_x_odd, x_even, to_next, to_prev)
    got_y_odd = exchange(y_odd, "gy", 1)
    got_y_even = exchange(y_even, "gy", 0)
    inner = pl.pallas_call(
        inner_kernel,
        out_shape=shape(VZ, CX, BLK),
        in_specs=[IN_SMEM] * 3 + [IN_VMEM, pl.BlockSpec(memory_space=pl.ANY)],
        out_specs=IN_VMEM,
        compiler_params=params,
    )(courant_x, courant_y, diffusion, cells, y_even)
    states, ground, part_own, part_x, part_y, part_both = pl.pallas_call(
        main_kernel,
        out_shape=(shape(VZ, CX, BLK), shape(V, CX, BLK)) + (shape(VZ * PB, BLK),) * 4,
        in_specs=[IN_SMEM] * 4 + [IN_VMEM, IN_HBM] + [IN_VMEM] * 8,
        out_specs=(IN_HBM,) + (IN_VMEM,) * 5,
        scratch_shapes=[
            pltpu.VMEM((VZ, CX, BLK), F32),
            pltpu.VMEM((NZ, CX, BLK), jnp.int32),
            pltpu.VMEM((2 * VZ, BLK), F32),
            pltpu.VMEM((2 * VZ, BLK), F32),
            pltpu.VMEM((CX, BLK), F32),
            pltpu.VMEM((512, 2 * CX), BF16),
            pltpu.VMEM((CX, V * BLK), F32),
            pltpu.VMEM((1024, V * BLK), BF16),
            pltpu.VMEM((2 * CX, NZ * BLK), BF16),
            pltpu.VMEM((512, NOPS * BLK), BF16),
            pltpu.VMEM((512, NOPS * BLK), BF16),
            pltpu.SemaphoreType.DMA,
            pltpu.SemaphoreType.DMA((V,)),
        ],
        compiler_params=params,
    )(
        parity, courant_x, courant_y, diffusion,
        inner, building, x_even, got_x_even, got_x_odd, got_y_even, got_y_odd, banks, coarse_banks, counts,
    )
    got_both = lax.ppermute(part_both, ("gx", "gy"), diagonal())
    got_x = one_lower(part_x, "gx")
    got_y = one_lower(part_y, "gy")
    comfort, so_far = pl.pallas_call(
        comfort_kernel,
        out_shape=(shape(CX, BLK), shape(VZ * PB, BLK)),
        in_specs=[IN_VMEM] * 4,
        out_specs=(IN_VMEM,) * 2,
        compiler_params=params,
    )(ground, radiative_mean_kelvin, parent_slab.reshape(VZ * PB, BLK), part_own)
    parent_new = so_far + 0.5 * (got_y + got_x + got_both)
    return states.reshape(child_state.shape), parent_new.reshape(parent_slab.shape), comfort


def solution(mesh):
    placed = (
        P(None, None, "gx", "gy"),
        P(None, None, ("gx", "gy"), None),
        P(None, ("gx", "gy"), None),
        P("gx", "gy"),
        P(),
        P(),
        P(),
        P(None, "gx", "gy"),
        P(("gx", "gy"), None),
        P(("gx", "gy"), None),
        P(("gx", "gy"), None),
        P(),
        P("gx", "gy", None),
        P("gx", "gy", None),
        P("gx", "gy", None),
        P(),
    )
    return jax.shard_map(
        local,
        mesh=mesh,
        in_specs=placed,
        out_specs=(P(None, None, "gx", "gy"), P(None, None, ("gx", "gy"), None), P("gx", "gy")),
        check_vma=False,
    )
```

time: 67.2 us -> 55.9 us (0.83)
  the two profiles are of different devices: /device:TPU:70 before, /device:TPU:25 now
where the time goes in v2:
time: 55.9 us; the launch traced here: 55.6 us
  Pallas kernels  20 us (36%)
  starting transfers between devices  16 us (29%)
  waiting for transfers between devices  15.1 us (27%)
  local copies, waits for them, and re-layouts  2.13 us (4%)
  other arithmetic  1.38 us (2%)
  between operations  0.93 us (2%)
    pallas_call x1, Pallas kernels, local(): pl.pallas_call(main_kernel, out_shape=(shape(VZ, CX, BLK), shape(V, CX, B...  9.69 us
    ppermute x4, starting transfers between devices, exchange(): return lax.ppermute(value, axis, pairs)  8.35 us
    ppermute x1, waiting for transfers between devices, local(): got_both = lax.ppermute(part_both, ('gx', 'gy'), diagonal())  7.31 us
    ppermute x2, waiting for transfers between devices, one_lower(): lax.ppermute(value, axis, [(a, a - 1) for a in range(1, lax.axis_size(axi...  6.1 us
    ppermute x2, starting transfers between devices, one_lower(): lax.ppermute(value, axis, [(a, a - 1) for a in range(1, lax.axis_size(axi...  5.77 us
    pallas_call x1, Pallas kernels, local(): pl.pallas_call(inner_kernel, out_shape=shape(VZ, CX, BLK), in_specs=[IN_S...  4.14 us
    pallas_call x1, Pallas kernels, local(): pl.pallas_call(rows_kernel, out_shape=(shape(X_ALL, BLK), shape(X_ALL, BL...  2.56 us
    pallas_call x1, Pallas kernels, local(): pl.pallas_call(edges_kernel, out_shape=(shape(VZ, CX + 2 * PAD, BLK), sha...  2.3 us
  transfers between devices with their start and end apart: 7, of which 4 were waited for; matrix products, arithmetic and copies ran while one was open for 0% of the time, Pallas kernels for 13%

profile of v2, /device:TPU:25, one launch (start us, length us, event | category | flops | bytes accessed | tf_op | source)
XLA Modules:
  0.0 55.6 jit_solution(3732524534452440436)
XLA Ops:
  0.6 0.0 copy-start.13
  0.6 0.0 copy-start.11
  0.7 0.0 copy-start.12
  0.7 0.0 copy-start
  0.7 0.6 %pad_add_fusion.parity = s32[2]{0:T(128)} fusion(s32[1]{0:T(128)} %bitcast.1, s32[1]{0:T(128)} %bitcast), kind=kLoop, calls=%fused_computation.2 | loop fusion | flops 2 | bytes 16 | tf_op jit(solution)/shard_map/stack | solution.py:338
  1.3 0.0 copy-start.7
  1.3 0.0 copy-start.8
  1.3 0.0 copy-start.9
  1.3 0.0 copy-start.10
  1.3 2.6 %shard_map.176 = (f32[144,128]{1,0:T(8,128)}, f32[144,128]{1,0:T(8,128)}) custom-call(s32[2]{0:T(128)} %pad_add_fusion.parity, f32[32,256,128]{2,1,0:T(8,128)} %bitcast.11, f32[64,128]{1,0:T(8,128)} %bitcast.15, s32[16,16]{1,0:T(8,128)} %tile.1, s32[16,16]{1,0:T(8,128)} %row.1, s32[16,16]{1,0:T(8,128)} %op.1), custom_call_target="tpu_custom_call" | custom-call | tf_op jit(solution)/shard_map/pallas_call | solution.py:342
  3.9 3.8 %collective-permute-start.1 = (f32[144,128]{1,0:T(8,128)}, f32[144,128]{1,0:T(8,128)S(1)}, u32[]{:S(2)}, u32[]{:S(2)}) collective-permute-start(f32[144,128]{1,0:T(8,128)} %get-tuple-element.23), channel_id=1, source_target_pairs={{16,32},{32,16},{48,64},{64,48},{80,96},{96,80},{17,33},{33,17},{4... | collective-permute-start | bytes 221192 | tf_op jit(solution)/shard_map/ppermute | solution.py:29
  7.7 0.1 collective-permute-start
  7.7 0.0 copy-done.13
  7.8 0.0 copy-done.11
  7.8 0.0 copy-done.12
  7.8 0.0 copy-done
  7.8 0.0 copy-start.2
  7.8 1.0 %copy-done.2 = f32[8,128,128]{2,1,0:T(8,128)S(1)} copy-done((f32[8,128,128]{2,1,0:T(8,128)S(1)}, f32[8,128,128]{2,1,0:T(8,128)}, u32[]{:S(2)}) %copy-start.2) | copy-done | bytes 524312
  8.8 0.0 copy-start.3
  8.8 1.0 %copy-done.3 = f32[8,128,128]{2,1,0:T(8,128)S(1)} copy-done((f32[8,128,128]{2,1,0:T(8,128)S(1)}, f32[8,128,128]{2,1,0:T(8,128)}, u32[]{:S(2)}) %copy-start.3) | copy-done | bytes 524312
  9.9 0.0 copy-start.4
  9.9 2.3 %shard_map.175 = (f32[32,272,128]{2,1,0:T(8,128)S(1)}, f32[128,128]{1,0:T(8,128)S(1)}, f32[128,128]{1,0:T(8,128)S(1)}, bf16[256,1024]{1,0:T(8,128)(2,1)S(1)}, bf...) custom-call(f32[32,256,128]{2,1,0:T(8,128)S(1)} %bitcast.12, f32[8,128,128]{2,1,0:T(8,128)S(1)} %copy-done.2, ...), custom_call_target="tpu_custom_call" | custom-call | tf_op jit(solution)/shard_map/pallas_call | solution.py:356
  12.2 0.0 collective-permute-done.1.odd_x
  12.2 1.6 %collective-permute-done.even_x = f32[144,128]{1,0:T(8,128)S(1)} collective-permute-done((f32[144,128]{1,0:T(8,128)}, f32[144,128]{1,0:T(8,128)S(1)}, u32[]{:S(2)}, u32[]{:S(2)}) %collective-permute-start) | collective-permute-done | bytes 73760 | tf_op jit(solution)/shard_map/ppermute | solution.py:29
  13.8 0.0 copy-done.7
  13.9 0.0 copy-done.4
  13.9 0.6 %shard_map.177 = (f32[288,128]{1,0:T(8,128)S(1)}, f32[288,128]{1,0:T(8,128)S(1)}) custom-call(s32[2]{0:T(128)S(1)} %copy-done.7, f32[144,128]{1,0:T(8,128)S(1)} %collective-permute-done.even_x, f32[144,128]{1,0:T(8,128)S(1)} %collective-permute-done.1.odd_x, f32[144,128]{1,0:T(8,128)S(1)} %copy-done.4, f32[128,128]{1,0:T(8,128)S(1)} %get-tuple-element.24.to_next, ...), custom_call_target="tpu_custom_call" | custom-call | tf_op jit(solution)/shard_map/pallas_call | solution.py:369
  14.4 4.4 %collective-permute-start.3 = (f32[288,128]{1,0:T(8,128)S(1)}, f32[288,128]{1,0:T(8,128)S(1)}, u32[]{:S(2)}, u32[]{:S(2)}) collective-permute-start(f32[288,128]{1,0:T(8,128)S(1)} %get-tuple-element.27), channel_id=1, source_target_pairs={{1,2},{2,1},{3,4},{4,3},{5,6},{6,5},{7,8},{8,7},{9,10},{10,9},{11,... | collective-permute-start | bytes 442376 | tf_op jit(solution)/shard_map/ppermute | solution.py:29
  18.8 0.1 collective-permute-start.2
  18.9 0.0 copy-done.8
  18.9 0.0 copy-done.9
  18.9 0.0 copy-done.10
  18.9 0.0 copy-start.1
  19.0 4.1 %shard_map.178.inner = f32[32,256,128]{2,1,0:T(8,128)S(1)} custom-call(f32[8]{0:T(128)S(1)} %copy-done.8, f32[8]{0:T(128)S(1)} %copy-done.9, f32[4]{0:T(128)S(1)} %copy-done.10, f32[32,272,128]{2,1,0:T(8,128)S(1)} %get-tuple-element.21.cells, f32[288,128]{1,0:T(8,128)S(1)} %get-tuple-element.26.after), custom_call_target="tpu_custom_call" | custom-call | tf_op jit(solution)/shard_map/pallas_call | solution.py:378
  23.1 0.0 copy-start.5
  23.1 0.0 copy-start.6
  23.1 0.0 collective-permute-done.3.odd_y
  23.1 0.0 collective-permute-done.2.even_y
  23.1 0.0 copy-done.1
  23.2 9.7 %shard_map.179 = (f32[32,256,128]{2,1,0:T(8,128)}, f32[4,256,128]{2,1,0:T(8,128)S(1)}, f32[512,128]{1,0:T(8,128)S(1)}, f32[512,128]{1,0:T(8,128)S(1)}, f32[512,128]{1,0:T(8,128)S(1)}, /*index=5*/f32[512,128]{1,0:T(8,128)S(1)}) custom-call(s32[2]{0:T(128)S(1)} %copy-done.7, f32[8]{0:T(128)S(1)} %copy-done.8, f32[8]{0:T(128)S(1)} %copy-done.9, ...), custom_call_target="tpu_custom_call" | custom-call | tf_op jit(solution)/shard_map/pallas_call | solution.py:385
  32.9 2.4 %collective-permute-start.4 = (f32[512,128]{1,0:T(8,128)S(1)}, f32[512,128]{1,0:T(8,128)S(1)}, u32[]{:S(2)}, u32[]{:S(2)}) collective-permute-start(f32[512,128]{1,0:T(8,128)S(1)} %get-tuple-element.35), channel_id=1, source_target_pairs={{1,0},{2,1},{3,2},{4,3},{5,4},{6,5},{7,6},{8,7},{9,8},{10,9},{11,1... | collective-permute-start | bytes 786440 | tf_op jit(solution)/shard_map/ppermute | solution.py:33
  35.2 3.4 %collective-permute-start.5 = (f32[512,128]{1,0:T(8,128)S(1)}, f32[512,128]{1,0:T(8,128)S(1)}, u32[]{:S(2)}, u32[]{:S(2)}) collective-permute-start(f32[512,128]{1,0:T(8,128)S(1)} %get-tuple-element.36), channel_id=1, source_target_pairs={{16,0},{32,16},{48,32},{64,48},{80,64},{96,80},{112,96},{17,1},{33... | collective-permute-start | bytes 786440 | tf_op jit(solution)/shard_map/ppermute | solution.py:33
  38.6 1.9 %collective-permute-start.6 = (f32[512,128]{1,0:T(8,128)S(1)}, f32[512,128]{1,0:T(8,128)S(1)}, u32[]{:S(2)}, u32[]{:S(2)}) collective-permute-start(f32[512,128]{1,0:T(8,128)S(1)} %get-tuple-element.37), channel_id=1, source_target_pairs={{17,0},{18,1},{19,2},{20,3},{21,4},{22,5},{23,6},{24,7},{25,8},{26... | collective-permute-start | bytes 786440 | tf_op jit(solution)/shard_map/ppermute | solution.py:410
  40.6 0.0 copy-done.5
  40.6 0.0 copy-done.6
  40.6 0.8 %shard_map.180 = (f32[256,128]{1,0:T(8,128)}, f32[512,128]{1,0:T(8,128)S(1)}) custom-call(f32[4,256,128]{2,1,0:T(8,128)S(1)} %get-tuple-element.32.ground, f32[256,128]{1,0:T(8,128)S(1)} %copy-done.6, f32[512,128]{1,0:T(8,128)S(1)} %bitcast.13, f32[512,128]{1,0:T(8,128)S(1)} %get-tuple-element.33.part_own), custom_call_target="tpu_custom_call" | custom-call | tf_op jit(solution)/shard_map/pallas_call | solution.py:413
  41.4 1.5 %collective-permute-done.4 = f32[512,128]{1,0:T(8,128)S(1)} collective-permute-done((f32[512,128]{1,0:T(8,128)S(1)}, f32[512,128]{1,0:T(8,128)S(1)}, u32[]{:S(2)}, u32[]{:S(2)}) %collective-permute-start.4) | collective-permute-done | bytes 262176 | tf_op jit(solution)/shard_map/ppermute | solution.py:33
  42.9 4.6 %collective-permute-done.5 = f32[512,128]{1,0:T(8,128)S(1)} collective-permute-done((f32[512,128]{1,0:T(8,128)S(1)}, f32[512,128]{1,0:T(8,128)S(1)}, u32[]{:S(2)}, u32[]{:S(2)}) %collective-permute-start.5) | collective-permute-done | bytes 262176 | tf_op jit(solution)/shard_map/ppermute | solution.py:33
  47.5 7.3 %collective-permute-done.6 = f32[512,128]{1,0:T(8,128)S(1)} collective-permute-done((f32[512,128]{1,0:T(8,128)S(1)}, f32[512,128]{1,0:T(8,128)S(1)}, u32[]{:S(2)}, u32[]{:S(2)}) %collective-permute-start.6) | collective-permute-done | bytes 262176 | tf_op jit(solution)/shard_map/ppermute | solution.py:410
  54.8 0.8 %multiply_add_fusion = f32[512,128]{1,0:T(8,128)} fusion(f32[512,128]{1,0:T(8,128)S(1)} %get-tuple-element.34, f32[512,128]{1,0:T(8,128)S(1)} %collective-permute-done.6, f32[512,128]{1,0:T(8,128)S(1)} %collective-permute-done.4, f32[512,128]{1,0:T(8,128)S(1)} %collective-permute-done.5), kind=kLoop, calls=%fused_computation | loop fusion | flops 262144 | bytes 1310720 | tf_op jit(solution)/shard_map/add | solution.py:420
  (1 shorter events, 0.0 us)
Async XLA Ops:
  0.6 7.1 %copy-start.13 = (s32[256,1,4]{0,2,1:T(4,128)S(1)}, s32[256,1,4]{0,2,1:T(4,128)}, u32[]{:S(2)}) copy-start(s32[256,1,4]{0,2,1:T(4,128)} %param.30) | copy-start | bytes 12292
  0.6 7.1 %copy-start.11 = (s32[256,1,4]{0,2,1:T(4,128)S(1)}, s32[256,1,4]{0,2,1:T(4,128)}, u32[]{:S(2)}) copy-start(s32[256,1,4]{0,2,1:T(4,128)} %param.29) | copy-start | bytes 12292
  0.7 7.1 %copy-start.12 = (s32[256,1,4]{0,2,1:T(4,128)S(1)}, s32[256,1,4]{0,2,1:T(4,128)}, u32[]{:S(2)}) copy-start(s32[256,1,4]{0,2,1:T(4,128)} %param.28) | copy-start | bytes 12292
  0.7 7.1 %copy-start = (f32[4,8,256,128]{3,2,1,0:T(8,128)S(1)}, f32[4,8,256,128]{3,2,1,0:T(8,128)}, u32[]{:S(2)}) copy-start(f32[4,8,256,128]{3,2,1,0:T(8,128)} %param.16) | copy-start | bytes 12582916
  1.3 12.6 %copy-start.7 = (s32[2]{0:T(128)S(1)}, s32[2]{0:T(128)}, u32[]{:S(2)}) copy-start(s32[2]{0:T(128)} %pad_add_fusion.parity) | copy-start | bytes 28
  1.3 17.6 %copy-start.8 = (f32[8]{0:T(128)S(1)}, f32[8]{0:T(128)}, u32[]{:S(2)}) copy-start(f32[8]{0:T(128)} %courant_x.3) | copy-start | bytes 100
  1.3 17.6 %copy-start.9 = (f32[8]{0:T(128)S(1)}, f32[8]{0:T(128)}, u32[]{:S(2)}) copy-start(f32[8]{0:T(128)} %courant_y.3) | copy-start | bytes 100
  1.3 17.7 %copy-start.10 = (f32[4]{0:T(128)S(1)}, f32[4]{0:T(128)}, u32[]{:S(2)}) copy-start(f32[4]{0:T(128)} %diffusion.3) | copy-start | bytes 52
  3.9 8.3 %collective-permute-start.1 = (f32[144,128]{1,0:T(8,128)}, f32[144,128]{1,0:T(8,128)S(1)}, u32[]{:S(2)}, u32[]{:S(2)}) collective-permute-start(f32[144,128]{1,0:T(8,128)} %get-tuple-element.23), channel_id=1, source_target_pairs={{16,32},{32,16},{48,64},{64,48},{80,96},{96,80},{17,33},{33,17},{4... | collective-permute-start | bytes 221192 | tf_op jit(solution)/shard_map/ppermute | solution.py:29
  7.7 6.2 %collective-permute-start = (f32[144,128]{1,0:T(8,128)}, f32[144,128]{1,0:T(8,128)S(1)}, u32[]{:S(2)}, u32[]{:S(2)}) collective-permute-start(f32[144,128]{1,0:T(8,128)} %get-tuple-element.22.own_even.own_x), channel_id=1, source_target_pairs={{0,16},{16,0},{32,48},{48,32},{64,80},{80,64},{96,112},{112,96},{1... | collective-permute-start | bytes 221192 | tf_op jit(solution)/shard_map/ppermute | solution.py:29
  7.8 1.0 %copy-start.2 = (f32[8,128,128]{2,1,0:T(8,128)S(1)}, f32[8,128,128]{2,1,0:T(8,128)}, u32[]{:S(2)}) copy-start(f32[8,128,128]{2,1,0:T(8,128)} %fine_bank.1) | copy-start | bytes 1572868
  8.8 1.0 %copy-start.3 = (f32[8,128,128]{2,1,0:T(8,128)S(1)}, f32[8,128,128]{2,1,0:T(8,128)}, u32[]{:S(2)}) copy-start(f32[8,128,128]{2,1,0:T(8,128)} %coarse_bank.1) | copy-start | bytes 1572868
  9.9 4.0 %copy-start.4 = (f32[144,128]{1,0:T(8,128)S(1)}, f32[144,128]{1,0:T(8,128)}, u32[]{:S(2)}) copy-start(f32[144,128]{1,0:T(8,128)} %get-tuple-element.22.own_even.own_x) | copy-start | bytes 221188
  14.4 8.7 %collective-permute-start.3 = (f32[288,128]{1,0:T(8,128)S(1)}, f32[288,128]{1,0:T(8,128)S(1)}, u32[]{:S(2)}, u32[]{:S(2)}) collective-permute-start(f32[288,128]{1,0:T(8,128)S(1)} %get-tuple-element.27), channel_id=1, source_target_pairs={{1,2},{2,1},{3,4},{4,3},{5,6},{6,5},{7,8},{8,7},{9,10},{10,9},{11,... | collective-permute-start | bytes 442376 | tf_op jit(solution)/shard_map/ppermute | solution.py:29
  18.8 4.3 %collective-permute-start.2 = (f32[288,128]{1,0:T(8,128)S(1)}, f32[288,128]{1,0:T(8,128)S(1)}, u32[]{:S(2)}, u32[]{:S(2)}) collective-permute-start(f32[288,128]{1,0:T(8,128)S(1)} %get-tuple-element.26.after), channel_id=1, source_target_pairs={{0,1},{1,0},{2,3},{3,2},{4,5},{5,4},{6,7},{7,6},{8,9},{9,8},{10,11... | collective-permute-start | bytes 442376 | tf_op jit(solution)/shard_map/ppermute | solution.py:29
  18.9 4.2 %copy-start.1 = (s32[8,256,128]{2,1,0:T(8,128)S(1)}, s32[8,256,128]{2,1,0:T(8,128)}, u32[]{:S(2)}) copy-start(s32[8,256,128]{2,1,0:T(8,128)} %building.1) | copy-start | bytes 3145732
  23.1 17.5 %copy-start.5 = (f32[4,8,16,128]{3,2,1,0:T(8,128)S(1)}, f32[4,8,16,128]{3,2,1,0:T(8,128)}, u32[]{:S(2)}) copy-start(f32[4,8,16,128]{3,2,1,0:T(8,128)} %param.17) | copy-start | bytes 786436
  23.1 17.5 %copy-start.6 = (f32[256,128]{1,0:T(8,128)S(1)}, f32[256,128]{1,0:T(8,128)}, u32[]{:S(2)}) copy-start(f32[256,128]{1,0:T(8,128)} %radiant.1) | copy-start | bytes 393220
  32.9 10.0 %collective-permute-start.4 = (f32[512,128]{1,0:T(8,128)S(1)}, f32[512,128]{1,0:T(8,128)S(1)}, u32[]{:S(2)}, u32[]{:S(2)}) collective-permute-start(f32[512,128]{1,0:T(8,128)S(1)} %get-tuple-element.35), channel_id=1, source_target_pairs={{1,0},{2,1},{3,2},{4,3},{5,4},{6,5},{7,6},{8,7},{9,8},{10,9},{11,1... | collective-permute-start | bytes 786440 | tf_op jit(solution)/shard_map/ppermute | solution.py:33
  35.2 12.2 %collective-permute-start.5 = (f32[512,128]{1,0:T(8,128)S(1)}, f32[512,128]{1,0:T(8,128)S(1)}, u32[]{:S(2)}, u32[]{:S(2)}) collective-permute-start(f32[512,128]{1,0:T(8,128)S(1)} %get-tuple-element.36), channel_id=1, source_target_pairs={{16,0},{32,16},{48,32},{64,48},{80,64},{96,80},{112,96},{17,1},{33... | collective-permute-start | bytes 786440 | tf_op jit(solution)/shard_map/ppermute | solution.py:33
  38.6 16.1 %collective-permute-start.6 = (f32[512,128]{1,0:T(8,128)S(1)}, f32[512,128]{1,0:T(8,128)S(1)}, u32[]{:S(2)}, u32[]{:S(2)}) collective-permute-start(f32[512,128]{1,0:T(8,128)S(1)} %get-tuple-element.37), channel_id=1, source_target_pairs={{17,0},{18,1},{19,2},{20,3},{21,4},{22,5},{23,6},{24,7},{25,8},{26... | collective-permute-start | bytes 786440 | tf_op jit(solution)/shard_map/ppermute | solution.py:410

commit v3 on v2

--- a/solution.py
+++ b/solution.py
@@ -33,11 +33,6 @@
     return lax.ppermute(value, axis, [(a, a - 1) for a in range(1, lax.axis_size(axis))])
 
 
-def diagonal():
-    nx, ny = lax.axis_size("gx"), lax.axis_size("gy")
-    return [(i * ny + j, (i - 1) * ny + j - 1) for i in range(1, nx) for j in range(1, ny)]
-
-
 def split(value):
     high = value.astype(BF16)
     return high, (value - high.astype(F32)).astype(BF16)
@@ -47,7 +42,7 @@
     return lax.broadcasted_iota(jnp.int32, shape, len(shape) - 1)
 
 
-def rows_kernel(parity, child, parent, tile, row, op, even, odd, first, last, blocks, names, stage, sems):
+def rows_kernel(child, parent, tile, row, op, even, odd, first, last, blocks, names, stage, sems):
     copies = [
         pltpu.make_async_copy(child.at[:, pl.ds(0, 8)], first, sems.at[0]),
         pltpu.make_async_copy(child.at[:, pl.ds(CX - 8, 8)], last, sems.at[1]),
@@ -61,7 +56,7 @@
     for i in range(3):
         stage[i, :, 0:K] = names[i].astype(F32)
     index = stage[0] + pltpu.roll(stage[1], K, 1) + pltpu.roll(stage[2], 2 * K, 1)
-    flag = parity[0] == 0
+    flag = lax.axis_index("gx") % 2 == 0
     for buffer in (even, odd):
         buffer[X_PAR:X_IDX] = blocks[...]
         buffer[X_IDX:X_ALL] = index
@@ -108,8 +103,8 @@
         coarse_banks[1, BLK * o : BLK * (o + 1)] = low
 
 
-def join_kernel(parity, even_x, odd_x, own_even, to_next, to_prev, even, odd):
-    flag_x, flag = parity[0] == 0, parity[1] == 0
+def join_kernel(even_x, odd_x, own_even, to_next, to_prev, even, odd):
+    flag_x, flag = lax.axis_index("gx") % 2 == 0, lax.axis_index("gy") % 2 == 0
     even[Y_COLS:Y_PAR] = jnp.where(flag, to_next[...], to_prev[...])
     odd[Y_COLS:Y_PAR] = jnp.where(flag, to_prev[...], to_next[...])
     relay = jnp.where(flag_x, odd_x[X_PAR:X_ALL], even_x[X_PAR:X_ALL])
@@ -178,20 +173,58 @@
     return out
 
 
-def main_kernel(
-    parity, courant_x, courant_y, diffusion,
-    inner, building, own_x, even_x, odd_x, even_y, odd_y, banks, coarse_banks, counts,
-    states, ground, part_own, part_x, part_y, part_both,
-    new, walls, above_fix, below_fix, side_fix, select, ghost, table, fields, picked_high, picked_low, wall_sem, out_sems,
+def choose(names, tile, select, at=0):
+    rows = pltpu.roll(names, BLK - K, 1)
+    ops = pltpu.roll(names, BLK - 2 * K, 1)
+    codes = jnp.where(names == float(tile), ops * float(CX) + rows, -1.0)
+    spread = [jnp.broadcast_to(codes[:, k : k + 1], (PB, CX)) for k in range(K)]
+    cell = lanes((PB, CX)).astype(F32)
+    for o in range(NOPS):
+        total = jnp.zeros((PB, CX), F32)
+        for k in range(K):
+            total = total + jnp.where(spread[k] == cell + float(CX * o), 1.0, 0.0)
+        total = total.astype(BF16)
+        row = (select.shape[0] // NOPS) * o + PB * at
+        select[row : row + PB, 0:CX] = total
+        select[row : row + PB, CX : 2 * CX] = total
+
+
+def gather(select, pair, vz, picked):
+    many = select.shape[0] // NOPS
+    found = jnp.dot(select[...], pair, preferred_element_type=F32)
+    for part, value in enumerate(split(found)):
+        for o in range(NOPS):
+            for e in range(2):
+                picked[part, pl.ds(pl.multiple_of(many * (vz + e), many), many), BLK * o : BLK * (o + 1)] = value[
+                    many * o : many * (o + 1), BLK * e : BLK * (e + 1)
+                ]
+
+
+def through_banks(picked, banks):
+    both = lax.dot_general(picked[0], banks[...], NT, preferred_element_type=F32)
+    rest = lax.dot_general(picked[1], banks[0:BLK], NT, preferred_element_type=F32)
+    return both[:, :BLK] + both[:, BLK:] + rest
+
+
+def gather_all(select, fields, picked):
+    def one_pair(i, carry):
+        gather(select, fields[:, pl.ds(pl.multiple_of(2 * BLK * i, 2 * BLK), 2 * BLK)], 2 * i, picked)
+        return carry
+
+    lax.fori_loop(0, VZ // 2, one_pair, 0, unroll=4)
+
+
+def update_kernel(
+    courant_x, courant_y, diffusion,
+    inner, walls, own_x, even_x, odd_x, even_y, odd_y, banks, coarse_banks, counts,
+    new, fields, part_both,
+    above_fix, below_fix, side_fix, select, ghost, table, picked,
 ):
-    flag_x, flag_y = parity[0] == 0, parity[1] == 0
-    walls_in = pltpu.make_async_copy(building, walls, wall_sem)
-    walls_in.start()
+    flag_x, flag_y = lax.axis_index("gx") % 2 == 0, lax.axis_index("gy") % 2 == 0
 
     prev_x = jnp.where(flag_x, odd_x[...], even_x[...])
     prev_y = jnp.where(flag_y, odd_y[...], even_y[...])
     parents = [own_x[X_PAR:X_IDX], prev_x[X_PAR:X_IDX], prev_y[Y_PAR:Y_RELAY], prev_y[Y_RELAY:Y_IDX]]
-    indices = [own_x[X_IDX:X_ALL], prev_x[X_IDX:X_ALL], prev_y[Y_IDX:Y_RIDX], prev_y[Y_RIDX:Y_ALL]]
 
     def weights(courant, level, variable):
         d = jnp.zeros(level.shape, F32)
@@ -251,24 +284,7 @@
         counts[...], table[512:1024], preferred_element_type=F32
     )
 
-    codes = []
-    for t in range(4):
-        names = indices[t]
-        rows = pltpu.roll(names, BLK - K, 1)
-        ops = pltpu.roll(names, BLK - 2 * K, 1)
-        codes.append(jnp.where(names == float(t), ops * float(CX) + rows, -1.0))
-    codes = jnp.concatenate(codes, axis=0)
-    spread = [jnp.broadcast_to(codes[:, k : k + 1], (64, CX)) for k in range(K)]
-    cell = lanes((64, CX)).astype(F32)
-    for o in range(NOPS):
-        total = jnp.zeros((64, CX), F32)
-        for k in range(K):
-            total = total + jnp.where(spread[k] == cell + float(CX * o), 1.0, 0.0)
-        total = total.astype(BF16)
-        select[64 * o : 64 * (o + 1), 0:CX] = total
-        select[64 * o : 64 * (o + 1), CX : 2 * CX] = total
-
-    walls_in.wait()
+    choose(prev_y[Y_RIDX:Y_ALL], 3, select)
     at_edge = (lanes((CHUNK, BLK)) + 2) % BLK < 4
     no_rows = jnp.zeros((6, BLK), F32)
 
@@ -291,40 +307,46 @@
                 total = jnp.where(walls[z, r : r + CHUNK] == 1, 0.0, total)
                 new[vz, r : r + CHUNK] = total
                 high, low = split(total)
-                fields[r : r + CHUNK, BLK * z : BLK * (z + 1)] = high
-                fields[CX + r : CX + r + CHUNK, BLK * z : BLK * (z + 1)] = low
-                if z == 0:
-                    ground[v, r : r + CHUNK] = total
-        pltpu.make_async_copy(new.at[pl.ds(NZ * v, NZ)], states.at[pl.ds(NZ * v, NZ)], out_sems.at[v]).start()
-        for z in range(0, NZ, 2):
-            found = jnp.dot(select[...], fields[:, BLK * z : BLK * (z + 2)], preferred_element_type=F32)
-            high, low = split(found)
-            for o in range(NOPS):
-                for e in range(2):
-                    to = (slice(64 * (z + e), 64 * (z + e + 1)), slice(BLK * o, BLK * (o + 1)))
-                    at = (slice(64 * o, 64 * (o + 1)), slice(BLK * e, BLK * (e + 1)))
-                    picked_high[to] = high[at]
-                    picked_low[to] = low[at]
-        both = lax.dot_general(picked_high[...], banks[...], NT, preferred_element_type=F32)
-        rest = lax.dot_general(picked_low[...], banks[0:BLK], NT, preferred_element_type=F32)
-        result = both[:, :BLK] + both[:, BLK:] + rest
-        for z in range(NZ):
-            at = pl.ds(pl.multiple_of(PB * (NZ * v + z), PB), PB)
-            for i, part in enumerate((part_own, part_x, part_y, part_both)):
-                part[at] = result[64 * z + PB * i : 64 * z + PB * (i + 1)]
+                columns = pl.ds(pl.multiple_of(BLK * vz, BLK), BLK)
+                fields[r : r + CHUNK, columns] = high
+                fields[CX + r : CX + r + CHUNK, columns] = low
+            if z % 2 == 1:
+                pair = pl.ds(pl.multiple_of(BLK * (vz - 1), BLK), 2 * BLK)
+                gather(select, fields[:, pair], vz - 1, picked)
         return carry
 
     lax.fori_loop(0, V, variable, 0)
-    for v in range(V):
-        pltpu.make_async_copy(new.at[pl.ds(NZ * v, NZ)], states.at[pl.ds(NZ * v, NZ)], out_sems.at[v]).wait()
-
-
-def comfort_kernel(ground, radiant, slab, part_own, comfort, so_far):
-    u, w, t, h = (ground[v] for v in range(V))
+    part_both[...] = through_banks(picked, banks)
+
+
+def sides_kernel(even_x, odd_x, even_y, odd_y, fields, banks, part_x, part_y, select, picked):
+    flag_x, flag_y = lax.axis_index("gx") % 2 == 0, lax.axis_index("gy") % 2 == 0
+    choose(jnp.where(flag_x, odd_x[X_IDX:X_ALL], even_x[X_IDX:X_ALL]), 1, select, 0)
+    choose(jnp.where(flag_y, odd_y[Y_IDX:Y_RIDX], even_y[Y_IDX:Y_RIDX]), 2, select, 1)
+    gather_all(select, fields, picked)
+    result = through_banks(picked, banks)
+    for vz in range(VZ):
+        part_x[PB * vz : PB * (vz + 1)] = result[2 * PB * vz : 2 * PB * vz + PB]
+        part_y[PB * vz : PB * (vz + 1)] = result[2 * PB * vz + PB : 2 * PB * (vz + 1)]
+
+
+def add_kernel(part_x, got_both, part_y, to_x, to_y):
+    to_x[...] = part_x[...] + got_both[...]
+    to_y[...] = part_y[...]
+
+
+def own_kernel(own_x, new, fields, banks, radiant, slab, after, states, comfort, so_far, select, picked, sem):
+    del after
+    out = pltpu.make_async_copy(new, states, sem)
+    out.start()
+    choose(own_x[X_IDX:X_ALL], 0, select)
+    gather_all(select, fields, picked)
+    so_far[...] = 0.5 * slab[...] + 0.5 * through_banks(picked, banks)
+    u, w, t, h = (new[NZ * v] for v in range(V))
     speed = jnp.sqrt(u * u + w * w + 0.25)
     excess = radiant[...] - t
     comfort[...] = t + 0.3 * excess - 0.6 * (speed - 1.0) + 0.4 * h + 0.1 * t * excess - 0.15 * speed * excess
-    so_far[...] = 0.5 * slab[...] + 0.5 * part_own[...]
+    out.wait()
 
 
 def shape(*dims, kind=F32):
@@ -335,21 +357,20 @@
     child_state, parent_slab, parent_above, radiative_mean_kelvin, courant_x, courant_y, diffusion, building,
     fine_tile, fine_row, fine_op, fine_bank, coarse_tile, coarse_row, coarse_op, coarse_bank,
 ):
-    parity = jnp.stack([lax.axis_index("gx") % 2, lax.axis_index("gy") % 2]).astype(jnp.int32)
     child = child_state.reshape(VZ, CX, BLK)
     parent = parent_above.reshape(V * PB, BLK)
     params = pltpu.CompilerParams(vmem_limit_bytes=VMEM_BYTES)
     x_even, x_odd = pl.pallas_call(
         rows_kernel,
         out_shape=(shape(X_ALL, BLK), shape(X_ALL, BLK)),
-        in_specs=[IN_SMEM] + [IN_HBM] * 5,
+        in_specs=[IN_HBM] * 5,
         out_specs=(IN_VMEM,) * 2,
         scratch_shapes=[
             pltpu.VMEM((VZ, 8, BLK), F32), pltpu.VMEM((VZ, 8, BLK), F32), pltpu.VMEM((V * PB, BLK), F32),
             pltpu.VMEM((3, PB, K), jnp.int32), pltpu.VMEM((3, PB, BLK), F32), pltpu.SemaphoreType.DMA((6,)),
         ],
         compiler_params=pltpu.CompilerParams(vmem_limit_bytes=56 * 1024 * 1024),
-    )(parity, child, parent, fine_tile, fine_row, fine_op)
+    )(child, parent, fine_tile, fine_row, fine_op)
     got_x_even = exchange(x_even, "gx", 0)
     got_x_odd = exchange(x_odd, "gx", 1)
     coarse_code = (coarse_op * 64 + coarse_tile * PB + coarse_row).reshape(CX, KI).T
@@ -369,10 +390,10 @@
     y_even, y_odd = pl.pallas_call(
         join_kernel,
         out_shape=(shape(Y_ALL, BLK), shape(Y_ALL, BLK)),
-        in_specs=[IN_SMEM] + [IN_VMEM] * 5,
+        in_specs=[IN_VMEM] * 5,
         out_specs=(IN_VMEM,) * 2,
         compiler_params=params,
-    )(parity, got_x_even, got_x_odd, x_even, to_next, to_prev)
+    )(got_x_even, got_x_odd, x_even, to_next, to_prev)
     got_y_odd = exchange(y_odd, "gy", 1)
     got_y_even = exchange(y_even, "gy", 0)
     inner = pl.pallas_call(
@@ -382,42 +403,48 @@
         out_specs=IN_VMEM,
         compiler_params=params,
     )(courant_x, courant_y, diffusion, cells, y_even)
-    states, ground, part_own, part_x, part_y, part_both = pl.pallas_call(
-        main_kernel,
-        out_shape=(shape(VZ, CX, BLK), shape(V, CX, BLK)) + (shape(VZ * PB, BLK),) * 4,
-        in_specs=[IN_SMEM] * 4 + [IN_VMEM, IN_HBM] + [IN_VMEM] * 8,
-        out_specs=(IN_HBM,) + (IN_VMEM,) * 5,
+    fields_shape = shape(2 * CX, VZ * BLK, kind=BF16)
+    select_and_picked = [pltpu.VMEM((NOPS * PB, 2 * CX), BF16), pltpu.VMEM((2, VZ * PB, NOPS * BLK), BF16)]
+    new, fields, part_both = pl.pallas_call(
+        update_kernel,
+        out_shape=(shape(VZ, CX, BLK), fields_shape, shape(VZ * PB, BLK)),
+        in_specs=[IN_SMEM] * 3 + [IN_VMEM] * 2 + [IN_VMEM] * 8,
+        out_specs=(IN_VMEM,) * 3,
+        input_output_aliases={3: 0},
         scratch_shapes=[
-            pltpu.VMEM((VZ, CX, BLK), F32),
-            pltpu.VMEM((NZ, CX, BLK), jnp.int32),
             pltpu.VMEM((2 * VZ, BLK), F32),
             pltpu.VMEM((2 * VZ, BLK), F32),
             pltpu.VMEM((CX, BLK), F32),
-            pltpu.VMEM((512, 2 * CX), BF16),
+            select_and_picked[0],
             pltpu.VMEM((CX, V * BLK), F32),
             pltpu.VMEM((1024, V * BLK), BF16),
-            pltpu.VMEM((2 * CX, NZ * BLK), BF16),
-            pltpu.VMEM((512, NOPS * BLK), BF16),
-            pltpu.VMEM((512, NOPS * BLK), BF16),
-            pltpu.SemaphoreType.DMA,
-            pltpu.SemaphoreType.DMA((V,)),
+            select_and_picked[1],
         ],
         compiler_params=params,
     )(
-        parity, courant_x, courant_y, diffusion,
+        courant_x, courant_y, diffusion,
         inner, building, x_even, got_x_even, got_x_odd, got_y_even, got_y_odd, banks, coarse_banks, counts,
     )
-    got_both = lax.ppermute(part_both, ("gx", "gy"), diagonal())
-    got_x = one_lower(part_x, "gx")
+    got_both = one_lower(part_both, "gy")
+    part_x, part_y = pl.pallas_call(
+        sides_kernel,
+        out_shape=(shape(VZ * PB, BLK),) * 2,
+        in_specs=[IN_VMEM] * 6,
+        out_specs=(IN_VMEM,) * 2,
+        scratch_shapes=[pltpu.VMEM((2 * NOPS * PB, 2 * CX), BF16), pltpu.VMEM((2, 2 * VZ * PB, NOPS * BLK), BF16)],
+        compiler_params=params,
+    )(got_x_even, got_x_odd, got_y_even, got_y_odd, fields, banks)
+    got_x = one_lower(part_x + got_both, "gx")
     got_y = one_lower(part_y, "gy")
-    comfort, so_far = pl.pallas_call(
-        comfort_kernel,
-        out_shape=(shape(CX, BLK), shape(VZ * PB, BLK)),
-        in_specs=[IN_VMEM] * 4,
-        out_specs=(IN_VMEM,) * 2,
-        compiler_params=params,
-    )(ground, radiative_mean_kelvin, parent_slab.reshape(VZ * PB, BLK), part_own)
-    parent_new = so_far + 0.5 * (got_y + got_x + got_both)
+    states, comfort, so_far = pl.pallas_call(
+        own_kernel,
+        out_shape=(shape(VZ, CX, BLK), shape(CX, BLK), shape(VZ * PB, BLK)),
+        in_specs=[IN_VMEM] * 6 + [pl.BlockSpec(memory_space=pl.ANY)],
+        out_specs=(IN_HBM, IN_VMEM, IN_VMEM),
+        scratch_shapes=select_and_picked + [pltpu.SemaphoreType.DMA],
+        compiler_params=params,
+    )(x_even, new, fields, banks, radiative_mean_kelvin, parent_slab.reshape(VZ * PB, BLK), part_y)
+    parent_new = so_far + 0.5 * (got_y + got_x)
     return states.reshape(child_state.shape), parent_new.reshape(parent_slab.shape), comfort
 
 

time: 55.9 us -> 50.3 us (0.90)
  the two profiles are of different devices: /device:TPU:25 before, /device:TPU:70 now
where the time goes in v3:
time: 50.3 us; the launch traced here: 50 us
  Pallas kernels  21.4 us (43%)
  starting transfers between devices  18.1 us (36%)
  waiting for transfers between devices  6.68 us (13%)
  local copies, waits for them, and re-layouts  2.13 us (4%)
  between operations  0.92 us (2%)
  other arithmetic  0.79 us (2%)
    ppermute x3, starting transfers between devices, one_lower(): lax.ppermute(value, axis, [(a, a - 1) for a in range(1, lax.axis_size(axi...  9.72 us
    ppermute x4, starting transfers between devices, exchange(): return lax.ppermute(value, axis, pairs)  8.37 us
    pallas_call x1, Pallas kernels, local(): pl.pallas_call(update_kernel, out_shape=(shape(VZ, CX, BLK), fields_shape...  5.75 us
    ppermute x3, waiting for transfers between devices, one_lower(): lax.ppermute(value, axis, [(a, a - 1) for a in range(1, lax.axis_size(axi...  4.65 us
    pallas_call x1, Pallas kernels, local(): pl.pallas_call(inner_kernel, out_shape=shape(VZ, CX, BLK), in_specs=[IN_S...  4.11 us
    pallas_call x1, Pallas kernels, local(): pl.pallas_call(sides_kernel, out_shape=(shape(VZ * PB, BLK),) * 2, in_spe...  3.98 us
    pallas_call x1, Pallas kernels, local(): pl.pallas_call(own_kernel, out_shape=(shape(VZ, CX, BLK), shape(CX, BLK),...  3.3 us
    pallas_call x1, Pallas kernels, local(): pl.pallas_call(edges_kernel, out_shape=(shape(VZ, CX + 2 * PAD, BLK), sha...  2.3 us
  transfers between devices with their start and end apart: 7, of which 3 were waited for; matrix products, arithmetic and copies ran while one was open for 0% of the time, Pallas kernels for 27%

profile of v3, /device:TPU:70, one launch (start us, length us, event | category | flops | bytes accessed | tf_op | source)
XLA Modules:
  0.0 50.0 jit_solution(14457193589611777276)
XLA Ops:
  0.6 0.0 copy-start
  0.6 0.0 copy-start.12
  0.7 0.0 copy-start.10
  0.7 0.0 copy-start.11
  0.7 0.0 copy-start.7
  0.7 0.0 copy-start.8
  0.7 0.0 copy-start.9
  0.7 1.9 %shard_map.175 = (f32[144,128]{1,0:T(8,128)}, f32[144,128]{1,0:T(8,128)}) custom-call(f32[32,256,128]{2,1,0:T(8,128)} %bitcast.9, f32[64,128]{1,0:T(8,128)} %bitcast.13, s32[16,16]{1,0:T(8,128)} %tile.1, s32[16,16]{1,0:T(8,128)} %row.1, s32[16,16]{1,0:T(8,128)} %op.1), custom_call_target="tpu_custom_call" | custom-call | tf_op jit(solution)/shard_map/pallas_call | solution.py:363
  2.6 0.0 copy-start.2
  2.6 5.5 %collective-permute-start.1 = (f32[144,128]{1,0:T(8,128)}, f32[144,128]{1,0:T(8,128)S(1)}, u32[]{:S(2)}, u32[]{:S(2)}) collective-permute-start(f32[144,128]{1,0:T(8,128)} %get-tuple-element.23), channel_id=1, source_target_pairs={{16,32},{32,16},{48,64},{64,48},{80,96},{96,80},{17,33},{33,17},{4... | collective-permute-start | bytes 221192 | tf_op jit(solution)/shard_map/ppermute | solution.py:29
  8.1 0.1 collective-permute-start
  8.2 0.0 copy-done.12
  8.2 0.0 copy-done.10
  8.3 0.0 copy-done.11
  8.3 0.0 copy-done
  8.3 0.0 copy-start.3
  8.3 1.0 %copy-done.3 = f32[8,128,128]{2,1,0:T(8,128)S(1)} copy-done((f32[8,128,128]{2,1,0:T(8,128)S(1)}, f32[8,128,128]{2,1,0:T(8,128)}, u32[]{:S(2)}) %copy-start.3) | copy-done | bytes 524312
  9.3 0.0 copy-start.4
  9.3 1.0 %copy-done.4 = f32[8,128,128]{2,1,0:T(8,128)S(1)} copy-done((f32[8,128,128]{2,1,0:T(8,128)S(1)}, f32[8,128,128]{2,1,0:T(8,128)}, u32[]{:S(2)}) %copy-start.4) | copy-done | bytes 524312
  10.4 2.3 %shard_map.176 = (f32[32,272,128]{2,1,0:T(8,128)S(1)}, f32[128,128]{1,0:T(8,128)S(1)}, f32[128,128]{1,0:T(8,128)S(1)}, bf16[256,1024]{1,0:T(8,128)(2,1)S(1)}, bf...) custom-call(f32[32,256,128]{2,1,0:T(8,128)S(1)} %bitcast.10, f32[8,128,128]{2,1,0:T(8,128)S(1)} %copy-done.3, ...), custom_call_target="tpu_custom_call" | custom-call | tf_op jit(solution)/shard_map/pallas_call | solution.py:377
  12.7 0.0 collective-permute-done.1.odd_x
  12.7 1.6 %collective-permute-done.even_x = f32[144,128]{1,0:T(8,128)S(1)} collective-permute-done((f32[144,128]{1,0:T(8,128)}, f32[144,128]{1,0:T(8,128)S(1)}, u32[]{:S(2)}, u32[]{:S(2)}) %collective-permute-start) | collective-permute-done | bytes 73760 | tf_op jit(solution)/shard_map/ppermute | solution.py:29
  14.3 0.0 copy-done.2
  14.3 1.9 %collective-permute-start.3 = (f32[288,128]{1,0:T(8,128)S(1)}, f32[288,128]{1,0:T(8,128)S(1)}, u32[]{:S(2)}, u32[]{:S(2)}) collective-permute-start(f32[288,128]{1,0:T(8,128)S(1)} %get-tuple-element.27), channel_id=1, source_target_pairs={{1,2},{2,1},{3,4},{4,3},{5,6},{6,5},{7,8},{8,7},{9,10},{10,9},{11,... | collective-permute-start | bytes 442376 | tf_op jit(solution)/shard_map/ppermute | solution.py:29
  16.3 0.9 %collective-permute-start.2 = (f32[288,128]{1,0:T(8,128)S(1)}, f32[288,128]{1,0:T(8,128)S(1)}, u32[]{:S(2)}, u32[]{:S(2)}) collective-permute-start(f32[288,128]{1,0:T(8,128)S(1)} %get-tuple-element.26.after), channel_id=1, source_target_pairs={{0,1},{1,0},{2,3},{3,2},{4,5},{5,4},{6,7},{7,6},{8,9},{9,8},{10,11... | collective-permute-start | bytes 442376 | tf_op jit(solution)/shard_map/ppermute | solution.py:29
  17.1 0.0 copy-done.7
  17.1 0.0 copy-done.8
  17.1 0.0 copy-done.9
  17.1 0.0 copy-start.1
  17.1 4.1 %shard_map.178.inner = f32[32,256,128]{2,1,0:T(8,128)S(1)} custom-call(f32[8]{0:T(128)S(1)} %copy-done.7, f32[8]{0:T(128)S(1)} %copy-done.8, f32[4]{0:T(128)S(1)} %copy-done.9, f32[32,272,128]{2,1,0:T(8,128)S(1)} %get-tuple-element.22.cells, f32[288,128]{1,0:T(8,128)S(1)} %get-tuple-element.26.after), custom_call_target="tpu_custom_call" | custom-call | tf_op jit(solution)/shard_map/pallas_call | solution.py:399
  21.3 0.4 collective-permute-done.3.odd_y
  21.7 0.0 collective-permute-done.2.even_y
  21.7 0.0 copy-done.1
  21.7 5.7 %shard_map.179 = (f32[32,256,128]{2,1,0:T(8,128)S(1)}, bf16[512,4096]{1,0:T(8,128)(2,1)S(1)}, f32[512,128]{1,0:T(8,128)S(1)}) custom-call(f32[8]{0:T(128)S(1)} %copy-done.7, f32[8]{0:T(128)S(1)} %copy-done.8, f32[4]{0:T(128)S(1)} %copy-done.9, f32[32,256,128]{2,1,0:T(8,128)S(1)} %shard_map.178.inner, ...), custom_call_target="tpu_custom_call", output_to_operand_aliasing={{0}: (3, {})} | custom-call | tf_op jit(solution)/shard_map/pallas_call | solution.py:408
  27.4 0.0 copy-start.5
  27.5 0.0 copy-start.6
  27.5 3.5 %collective-permute-start.5 = (f32[512,128]{1,0:T(8,128)S(1)}, f32[512,128]{1,0:T(8,128)S(1)}, u32[]{:S(2)}, u32[]{:S(2)}) collective-permute-start(f32[512,128]{1,0:T(8,128)S(1)} %get-tuple-element.37), channel_id=1, source_target_pairs={{1,0},{2,1},{3,2},{4,3},{5,4},{6,5},{7,6},{8,7},{9,8},{10,9},{11,1... | collective-permute-start | bytes 786440 | tf_op jit(solution)/shard_map/ppermute | solution.py:33
  31.0 4.0 %shard_map.180 = (f32[512,128]{1,0:T(8,128)S(1)}, f32[512,128]{1,0:T(8,128)S(1)}) custom-call(f32[144,128]{1,0:T(8,128)S(1)} %collective-permute-done.even_x, f32[144,128]{1,0:T(8,128)S(1)} %collective-permute-done.1.odd_x, f32[288,128]{1,0:T(8,128)S(1)} %collective-permute-done.2.even_y, f32[288,128]{1,0:T(8,128)S(1)} %collective-permute-done.3.odd_y, ...), custom_call_target="tpu_custom_call" | custom-call | tf_op jit(solution)/shard_map/pallas_call | solution.py:429
  35.0 2.4 %collective-permute-start.4 = (f32[512,128]{1,0:T(8,128)S(1)}, f32[512,128]{1,0:T(8,128)S(1)}, u32[]{:S(2)}, u32[]{:S(2)}) collective-permute-start(f32[512,128]{1,0:T(8,128)S(1)} %get-tuple-element.33.after), channel_id=1, source_target_pairs={{1,0},{2,1},{3,2},{4,3},{5,4},{6,5},{7,6},{8,7},{9,8},{10,9},{11,1... | collective-permute-start | bytes 786440 | tf_op jit(solution)/shard_map/ppermute | solution.py:33
  37.4 0.0 collective-permute-done.5
  37.4 3.8 %collective-permute-start.6 = (f32[512,128]{1,0:T(8,128)S(1)}, f32[512,128]{1,0:T(8,128)S(1)}, u32[]{:S(2)}, u32[]{:S(2)}) collective-permute-start(f32[512,128]{1,0:T(8,128)S(1)} %add.17), channel_id=1, source_target_pairs={{16,0},{32,16},{48,32},{64,48},{80,64},{96,80},{112,96},{17,1},{33... | collective-permute-start | bytes 786440 | tf_op jit(solution)/shard_map/ppermute | solution.py:33
  41.3 0.0 copy-done.5
  41.3 0.0 copy-done.6
  41.3 3.3 %shard_map.181 = (f32[32,256,128]{2,1,0:T(8,128)}, f32[256,128]{1,0:T(8,128)}, f32[512,128]{1,0:T(8,128)S(1)}) custom-call(f32[144,128]{1,0:T(8,128)S(1)} %copy-done.2, f32[32,256,128]{2,1,0:T(8,128)S(1)} %get-tuple-element.31.new, bf16[512,4096]{1,0:T(8,128)(2,1)S(1)} %get-tuple-element.32.fields, bf16[256,1024]{1,0:T(8,128)(2,1)S(1)} %get-tuple-element.28.banks, ...), custom_call_target="tpu_custom_call" | custom-call | tf_op jit(solution)/shard_map/pallas_call | solution.py:439
  44.6 0.0 collective-permute-done.4
  44.6 4.6 %collective-permute-done.6 = f32[512,128]{1,0:T(8,128)S(1)} collective-permute-done((f32[512,128]{1,0:T(8,128)S(1)}, f32[512,128]{1,0:T(8,128)S(1)}, u32[]{:S(2)}, u32[]{:S(2)}) %collective-permute-start.6) | collective-permute-done | bytes 262176 | tf_op jit(solution)/shard_map/ppermute | solution.py:33
  49.2 0.8 %multiply_add_fusion = f32[512,128]{1,0:T(8,128)} fusion(f32[512,128]{1,0:T(8,128)S(1)} %get-tuple-element.35, f32[512,128]{1,0:T(8,128)S(1)} %collective-permute-done.4, f32[512,128]{1,0:T(8,128)S(1)} %collective-permute-done.6), kind=kLoop, calls=%fused_computation | loop fusion | flops 196608 | bytes 1048576 | tf_op jit(solution)/shard_map/add | solution.py:447
  (3 shorter events, 0.1 us)
Async XLA Ops:
  0.6 7.7 %copy-start = (f32[4,8,256,128]{3,2,1,0:T(8,128)S(1)}, f32[4,8,256,128]{3,2,1,0:T(8,128)}, u32[]{:S(2)}) copy-start(f32[4,8,256,128]{3,2,1,0:T(8,128)} %param.16) | copy-start | bytes 12582916
  0.6 7.6 %copy-start.12 = (s32[256,1,4]{0,2,1:T(4,128)S(1)}, s32[256,1,4]{0,2,1:T(4,128)}, u32[]{:S(2)}) copy-start(s32[256,1,4]{0,2,1:T(4,128)} %param.30) | copy-start | bytes 12292
  0.7 7.6 %copy-start.10 = (s32[256,1,4]{0,2,1:T(4,128)S(1)}, s32[256,1,4]{0,2,1:T(4,128)}, u32[]{:S(2)}) copy-start(s32[256,1,4]{0,2,1:T(4,128)} %param.29) | copy-start | bytes 12292
  0.7 7.6 %copy-start.11 = (s32[256,1,4]{0,2,1:T(4,128)S(1)}, s32[256,1,4]{0,2,1:T(4,128)}, u32[]{:S(2)}) copy-start(s32[256,1,4]{0,2,1:T(4,128)} %param.28) | copy-start | bytes 12292
  0.7 16.4 %copy-start.7 = (f32[8]{0:T(128)S(1)}, f32[8]{0:T(128)}, u32[]{:S(2)}) copy-start(f32[8]{0:T(128)} %courant_x.3) | copy-start | bytes 100
  0.7 16.4 %copy-start.8 = (f32[8]{0:T(128)S(1)}, f32[8]{0:T(128)}, u32[]{:S(2)}) copy-start(f32[8]{0:T(128)} %courant_y.3) | copy-start | bytes 100
  0.7 16.4 %copy-start.9 = (f32[4]{0:T(128)S(1)}, f32[4]{0:T(128)}, u32[]{:S(2)}) copy-start(f32[4]{0:T(128)} %diffusion.3) | copy-start | bytes 52
  2.6 11.7 %copy-start.2 = (f32[144,128]{1,0:T(8,128)S(1)}, f32[144,128]{1,0:T(8,128)}, u32[]{:S(2)}) copy-start(f32[144,128]{1,0:T(8,128)} %get-tuple-element.21.own_even.own_x) | copy-start | bytes 221188
  2.6 10.1 %collective-permute-start.1 = (f32[144,128]{1,0:T(8,128)}, f32[144,128]{1,0:T(8,128)S(1)}, u32[]{:S(2)}, u32[]{:S(2)}) collective-permute-start(f32[144,128]{1,0:T(8,128)} %get-tuple-element.23), channel_id=1, source_target_pairs={{16,32},{32,16},{48,64},{64,48},{80,96},{96,80},{17,33},{33,17},{4... | collective-permute-start | bytes 221192 | tf_op jit(solution)/shard_map/ppermute | solution.py:29
  8.1 6.1 %collective-permute-start = (f32[144,128]{1,0:T(8,128)}, f32[144,128]{1,0:T(8,128)S(1)}, u32[]{:S(2)}, u32[]{:S(2)}) collective-permute-start(f32[144,128]{1,0:T(8,128)} %get-tuple-element.21.own_even.own_x), channel_id=1, source_target_pairs={{0,16},{16,0},{32,48},{48,32},{64,80},{80,64},{96,112},{112,96},{1... | collective-permute-start | bytes 221192 | tf_op jit(solution)/shard_map/ppermute | solution.py:29
  8.3 1.0 %copy-start.3 = (f32[8,128,128]{2,1,0:T(8,128)S(1)}, f32[8,128,128]{2,1,0:T(8,128)}, u32[]{:S(2)}) copy-start(f32[8,128,128]{2,1,0:T(8,128)} %fine_bank.1) | copy-start | bytes 1572868
  9.3 1.0 %copy-start.4 = (f32[8,128,128]{2,1,0:T(8,128)S(1)}, f32[8,128,128]{2,1,0:T(8,128)}, u32[]{:S(2)}) copy-start(f32[8,128,128]{2,1,0:T(8,128)} %coarse_bank.1) | copy-start | bytes 1572868
  14.3 7.4 %collective-permute-start.3 = (f32[288,128]{1,0:T(8,128)S(1)}, f32[288,128]{1,0:T(8,128)S(1)}, u32[]{:S(2)}, u32[]{:S(2)}) collective-permute-start(f32[288,128]{1,0:T(8,128)S(1)} %get-tuple-element.27), channel_id=1, source_target_pairs={{1,2},{2,1},{3,4},{4,3},{5,6},{6,5},{7,8},{8,7},{9,10},{10,9},{11,... | collective-permute-start | bytes 442376 | tf_op jit(solution)/shard_map/ppermute | solution.py:29
  16.3 5.4 %collective-permute-start.2 = (f32[288,128]{1,0:T(8,128)S(1)}, f32[288,128]{1,0:T(8,128)S(1)}, u32[]{:S(2)}, u32[]{:S(2)}) collective-permute-start(f32[288,128]{1,0:T(8,128)S(1)} %get-tuple-element.26.after), channel_id=1, source_target_pairs={{0,1},{1,0},{2,3},{3,2},{4,5},{5,4},{6,7},{7,6},{8,9},{9,8},{10,11... | collective-permute-start | bytes 442376 | tf_op jit(solution)/shard_map/ppermute | solution.py:29
  17.1 4.6 %copy-start.1 = (s32[8,256,128]{2,1,0:T(8,128)S(1)}, s32[8,256,128]{2,1,0:T(8,128)}, u32[]{:S(2)}) copy-start(s32[8,256,128]{2,1,0:T(8,128)} %walls.1) | copy-start | bytes 3145732
  27.4 13.8 %copy-start.5 = (f32[4,8,16,128]{3,2,1,0:T(8,128)S(1)}, f32[4,8,16,128]{3,2,1,0:T(8,128)}, u32[]{:S(2)}) copy-start(f32[4,8,16,128]{3,2,1,0:T(8,128)} %param.17) | copy-start | bytes 786436
  27.5 13.8 %copy-start.6 = (f32[256,128]{1,0:T(8,128)S(1)}, f32[256,128]{1,0:T(8,128)}, u32[]{:S(2)}) copy-start(f32[256,128]{1,0:T(8,128)} %radiant.1) | copy-start | bytes 393220
  27.5 9.9 %collective-permute-start.5 = (f32[512,128]{1,0:T(8,128)S(1)}, f32[512,128]{1,0:T(8,128)S(1)}, u32[]{:S(2)}, u32[]{:S(2)}) collective-permute-start(f32[512,128]{1,0:T(8,128)S(1)} %get-tuple-element.37), channel_id=1, source_target_pairs={{1,0},{2,1},{3,2},{4,3},{5,4},{6,5},{7,6},{8,7},{9,8},{10,9},{11,1... | collective-permute-start | bytes 786440 | tf_op jit(solution)/shard_map/ppermute | solution.py:33
  35.0 9.6 %collective-permute-start.4 = (f32[512,128]{1,0:T(8,128)S(1)}, f32[512,128]{1,0:T(8,128)S(1)}, u32[]{:S(2)}, u32[]{:S(2)}) collective-permute-start(f32[512,128]{1,0:T(8,128)S(1)} %get-tuple-element.33.after), channel_id=1, source_target_pairs={{1,0},{2,1},{3,2},{4,3},{5,4},{6,5},{7,6},{8,7},{9,8},{10,9},{11,1... | collective-permute-start | bytes 786440 | tf_op jit(solution)/shard_map/ppermute | solution.py:33
  37.4 11.8 %collective-permute-start.6 = (f32[512,128]{1,0:T(8,128)S(1)}, f32[512,128]{1,0:T(8,128)S(1)}, u32[]{:S(2)}, u32[]{:S(2)}) collective-permute-start(f32[512,128]{1,0:T(8,128)S(1)} %add.17), channel_id=1, source_target_pairs={{16,0},{32,16},{48,32},{64,48},{80,64},{96,80},{112,96},{17,1},{33... | collective-permute-start | bytes 786440 | tf_op jit(solution)/shard_map/ppermute | solution.py:33

commit v4 on v3

--- a/solution.py
+++ b/solution.py
@@ -10,6 +10,7 @@
 F32, BF16 = jnp.float32, jnp.bfloat16
 PAD = 8
 CHUNK = 64
+EARLY = 2
 VMEM_BYTES = 32 * 1024 * 1024
 
 X_ROWS, X_PAR, X_IDX, X_ALL = 0, 64, 128, 144
@@ -66,21 +67,16 @@
         odd[2 * vz : 2 * vz + 2] = jnp.where(flag, low, high)
 
 
-def edges_kernel(child, fine_bank, coarse_bank, code, cells, to_next, to_prev, banks, coarse_banks, counts, fine, coarse, sems):
+def edges_kernel(courant_x, courant_y, diffusion, child, cells, to_next, to_prev, inner, sems):
     copies = [
         pltpu.make_async_copy(child.at[pl.ds(NZ * v, NZ)], cells.at[pl.ds(NZ * v, NZ), pl.ds(PAD, CX)], sems.at[v])
         for v in range(V)
-    ] + [pltpu.make_async_copy(fine_bank, fine, sems.at[V]), pltpu.make_async_copy(coarse_bank, coarse, sems.at[V + 1])]
+    ]
     for c in copies:
         c.start()
     for vz in range(VZ):
         cells[vz, 0:PAD] = jnp.zeros((PAD, BLK), F32)
         cells[vz, PAD + CX : PAD + CX + PAD] = jnp.zeros((PAD, BLK), F32)
-    wanted = lax.broadcasted_iota(jnp.int32, (512, CX), 0)
-    total = jnp.zeros((512, CX), F32)
-    for k in range(KI):
-        total = total + jnp.where(code[k : k + 1, :] == wanted, 1.0, 0.0)
-    counts[...] = total.T.astype(BF16)
     which = lanes((CX, BLK)) // 4
     edges = jnp.zeros((CX, BLK), F32)
     for v in range(V):
@@ -92,15 +88,7 @@
     upper = lanes((half, BLK)) % 4 >= 2
     to_next[...] = jnp.where(upper, pltpu.roll(edges[half:], 2, 1), edges[:half])
     to_prev[...] = jnp.where(upper, edges[:half], pltpu.roll(edges[half:], BLK - 2, 1))
-    copies[V].wait()
-    copies[V + 1].wait()
-    for o in range(NOPS):
-        high, low = split(fine[o])
-        banks[0:BLK, BLK * o : BLK * (o + 1)] = high
-        banks[BLK : 2 * BLK, BLK * o : BLK * (o + 1)] = low
-        high, low = split(coarse[o])
-        coarse_banks[0, BLK * o : BLK * (o + 1)] = high
-        coarse_banks[1, BLK * o : BLK * (o + 1)] = low
+    step_inside(0, EARLY, courant_x, courant_y, diffusion, cells, inner)
 
 
 def join_kernel(even_x, odd_x, own_even, to_next, to_prev, even, odd):
@@ -122,8 +110,7 @@
     return half * size - 1.5 * size, 2.0 * size - size * size, half * size - half
 
 
-def inner_kernel(courant_x, courant_y, diffusion, cells, after, inner):
-    del after
+def step_inside(first, last, courant_x, courant_y, diffusion, cells, inner):
     lane = lanes((8, BLK))[0:1]
 
     def variable(v, carry):
@@ -163,7 +150,7 @@
                 inner[vz, r - PAD : r - PAD + CHUNK] = total + d * beside
         return carry
 
-    lax.fori_loop(0, V, variable, 0)
+    lax.fori_loop(first, last, variable, 0)
 
 
 def per_level(values, level):
@@ -214,17 +201,31 @@
     lax.fori_loop(0, VZ // 2, one_pair, 0, unroll=4)
 
 
-def update_kernel(
-    courant_x, courant_y, diffusion,
-    inner, walls, own_x, even_x, odd_x, even_y, odd_y, banks, coarse_banks, counts,
-    new, fields, part_both,
-    above_fix, below_fix, side_fix, select, ghost, table, picked,
+def ghost_part(blocks, coarse_banks, counts, table):
+    high, low = split(jnp.concatenate([blocks[t][PB * v : PB * (v + 1)] for v in range(V) for t in range(2)], axis=0))
+    for o in range(NOPS):
+        bank_high, bank_low = (coarse_banks[i, BLK * o : BLK * (o + 1)] for i in range(2))
+        made = (
+            lax.dot_general(high, bank_high, NT, preferred_element_type=F32)
+            + lax.dot_general(high, bank_low, NT, preferred_element_type=F32)
+            + lax.dot_general(low, bank_high, NT, preferred_element_type=F32)
+        )
+        made_high, made_low = split(made)
+        for v in range(V):
+            table[32 * o : 32 * (o + 1), BLK * v : BLK * (v + 1)] = made_high[32 * v : 32 * (v + 1)]
+            table[256 + 32 * o : 256 + 32 * (o + 1), BLK * v : BLK * (v + 1)] = made_low[32 * v : 32 * (v + 1)]
+    return jnp.dot(counts, table[0:256], preferred_element_type=F32) + jnp.dot(
+        counts, table[256:512], preferred_element_type=F32
+    )
+
+
+def middle_kernel(
+    courant_x, courant_y, diffusion, so_far, cells, fine, coarse, code, own_x, even_x, odd_x, after,
+    inner, banks, coarse_banks, counts_y, ghost, above_fix, below_fix, side_weights, table,
 ):
-    flag_x, flag_y = lax.axis_index("gx") % 2 == 0, lax.axis_index("gy") % 2 == 0
-
+    del so_far, after
+    flag_x = lax.axis_index("gx") % 2 == 0
     prev_x = jnp.where(flag_x, odd_x[...], even_x[...])
-    prev_y = jnp.where(flag_y, odd_y[...], even_y[...])
-    parents = [own_x[X_PAR:X_IDX], prev_x[X_PAR:X_IDX], prev_y[Y_PAR:Y_RELAY], prev_y[Y_RELAY:Y_IDX]]
 
     def weights(courant, level, variable):
         d = jnp.zeros(level.shape, F32)
@@ -245,17 +246,48 @@
     above_fix[...] = low_far * prev_rows + jnp.where(first, low * pltpu.roll(prev_rows, 2 * VZ - 1, 0), 0.0)
     below_fix[...] = high_far * next_rows + jnp.where(first, 0.0, high * pltpu.roll(next_rows, 1, 0))
 
+    lane = lanes((8, BLK))
+    low, high, low_far, high_far = weights(courant_y, (lane // 4) % NZ, lane // (4 * NZ))
+    place = lane % 4
+    side_weights[0:8] = jnp.where(place < 2, high_far, 0.0)
+    side_weights[8:16] = jnp.where(place == 1, high, 0.0)
+    side_weights[16:24] = jnp.where(place == 2, low, 0.0)
+    side_weights[24:32] = jnp.where(place >= 2, low_far, 0.0)
+    for v in range(V):
+        side_weights[32 + 8 * v : 40 + 8 * v] = jnp.full((8, BLK), diffusion[v], F32)
+
+    for o in range(NOPS):
+        high, low = split(fine[o])
+        banks[0:BLK, BLK * o : BLK * (o + 1)] = high
+        banks[BLK : 2 * BLK, BLK * o : BLK * (o + 1)] = low
+        high, low = split(coarse[o])
+        coarse_banks[0, BLK * o : BLK * (o + 1)] = high
+        coarse_banks[1, BLK * o : BLK * (o + 1)] = low
+
+    wanted = lax.broadcasted_iota(jnp.int32, (512, CX), 0)
+    total = jnp.zeros((512, CX), F32)
+    for k in range(KI):
+        total = total + jnp.where(code[k : k + 1, :] == wanted, 1.0, 0.0)
+    counts_y[...] = total[CX:].T.astype(BF16)
+    made = ghost_part([own_x[X_PAR:X_IDX], prev_x[X_PAR:X_IDX]], coarse_banks, total[:CX].T.astype(BF16), table)
+    for v in range(V):
+        ghost[:, BLK * v : BLK * (v + 1)] = diffusion[v] * made[:, BLK * v : BLK * (v + 1)]
+    step_inside(EARLY, V, courant_x, courant_y, diffusion, cells, inner)
+
+
+def update_kernel(
+    inner, walls, even_y, odd_y, banks, coarse_banks, counts_y, ghost_x, above_fix, below_fix, side_weights,
+    new, fields, part_both,
+    side_fix, select, ghost, table, picked,
+):
+    flag_y = lax.axis_index("gy") % 2 == 0
+    prev_y = jnp.where(flag_y, odd_y[...], even_y[...])
+
     half = CX // 2
     next_y = jnp.where(flag_y, even_y[Y_COLS:Y_PAR], odd_y[Y_COLS:Y_PAR])
     before = prev_y[Y_COLS:Y_PAR]
     upper = lanes((half, BLK)) % 4 >= 2
-    lane = lanes((8, BLK))
-    low, high, low_far, high_far = (w[0:1] for w in weights(courant_y, (lane // 4) % NZ, lane // (4 * NZ)))
-    place = lane[0:1] % 4
-    by_minus_2 = jnp.where(place < 2, high_far, 0.0)
-    by_minus_1 = jnp.where(place == 1, high, 0.0)
-    by_plus_1 = jnp.where(place == 2, low, 0.0)
-    by_plus_2 = jnp.where(place >= 2, low_far, 0.0)
+    by_minus_2, by_minus_1, by_plus_1, by_plus_2 = (side_weights[8 * i : 8 * i + 1] for i in range(4))
     for part in range(2):
         if part == 0:
             columns = jnp.where(upper, next_y, before)
@@ -268,28 +300,16 @@
             + by_plus_2 * pltpu.roll(columns, 2, 1)
         )
 
-    high, low = split(jnp.concatenate([parents[t][PB * v : PB * (v + 1)] for v in range(V) for t in range(4)], axis=0))
-    for o in range(NOPS):
-        bank_high, bank_low = (coarse_banks[i, BLK * o : BLK * (o + 1)] for i in range(2))
-        made = (
-            lax.dot_general(high, bank_high, NT, preferred_element_type=F32)
-            + lax.dot_general(high, bank_low, NT, preferred_element_type=F32)
-            + lax.dot_general(low, bank_high, NT, preferred_element_type=F32)
-        )
-        made_high, made_low = split(made)
-        for v in range(V):
-            table[64 * o : 64 * (o + 1), BLK * v : BLK * (v + 1)] = made_high[64 * v : 64 * (v + 1)]
-            table[512 + 64 * o : 512 + 64 * (o + 1), BLK * v : BLK * (v + 1)] = made_low[64 * v : 64 * (v + 1)]
-    ghost[...] = jnp.dot(counts[...], table[0:512], preferred_element_type=F32) + jnp.dot(
-        counts[...], table[512:1024], preferred_element_type=F32
-    )
+    made = ghost_part([prev_y[Y_PAR:Y_RELAY], prev_y[Y_RELAY:Y_IDX]], coarse_banks, counts_y[...], table)
+    for v in range(V):
+        at = (slice(None), slice(BLK * v, BLK * (v + 1)))
+        ghost[at] = ghost_x[at] + side_weights[32 + 8 * v : 33 + 8 * v] * made[at]
 
     choose(prev_y[Y_RIDX:Y_ALL], 3, select)
     at_edge = (lanes((CHUNK, BLK)) + 2) % BLK < 4
     no_rows = jnp.zeros((6, BLK), F32)
 
     def variable(v, carry):
-        d = diffusion[v]
         for z in range(NZ):
             vz = NZ * v + z
             turn = (2 * BLK - 2 - 4 * vz) % BLK
@@ -297,7 +317,7 @@
                 total = inner[vz, r : r + CHUNK]
                 total = total + jnp.where(at_edge, pltpu.roll(side_fix[r : r + CHUNK], turn, 1), 0.0)
                 if z == NZ - 1:
-                    total = total + d * ghost[r : r + CHUNK, pl.ds(pl.multiple_of(BLK * v, BLK), BLK)]
+                    total = total + ghost[r : r + CHUNK, pl.ds(pl.multiple_of(BLK * v, BLK), BLK)]
                 if r == 0:
                     fix = jnp.concatenate([above_fix[pl.ds(2 * vz, 2)], no_rows], axis=0)
                     total = jnp.concatenate([total[:8] + fix, total[8:]], axis=0)
@@ -373,20 +393,17 @@
     )(child, parent, fine_tile, fine_row, fine_op)
     got_x_even = exchange(x_even, "gx", 0)
     got_x_odd = exchange(x_odd, "gx", 1)
-    coarse_code = (coarse_op * 64 + coarse_tile * PB + coarse_row).reshape(CX, KI).T
-    cells, to_next, to_prev, banks, coarse_banks, counts = pl.pallas_call(
+    coarse_code = ((coarse_tile >> 1) * 256 + coarse_op * 32 + (coarse_tile & 1) * PB + coarse_row).reshape(CX, KI).T
+    cells, to_next, to_prev, inner = pl.pallas_call(
         edges_kernel,
         out_shape=(
-            shape(VZ, CX + 2 * PAD, BLK), shape(CX // 2, BLK), shape(CX // 2, BLK),
-            shape(2 * BLK, NOPS * BLK, kind=BF16), shape(2, NOPS * BLK, BLK, kind=BF16), shape(CX, 512, kind=BF16),
+            shape(VZ, CX + 2 * PAD, BLK), shape(CX // 2, BLK), shape(CX // 2, BLK), shape(VZ, CX, BLK),
         ),
-        in_specs=[IN_HBM] * 3 + [IN_VMEM],
-        out_specs=(IN_VMEM,) * 6,
-        scratch_shapes=[
-            pltpu.VMEM((NOPS, BLK, BLK), F32), pltpu.VMEM((NOPS, BLK, BLK), F32), pltpu.SemaphoreType.DMA((V + 2,)),
-        ],
-        compiler_params=params,
-    )(child, fine_bank, coarse_bank, coarse_code)
+        in_specs=[IN_SMEM] * 3 + [IN_HBM],
+        out_specs=(IN_VMEM,) * 4,
+        scratch_shapes=[pltpu.SemaphoreType.DMA((V,))],
+        compiler_params=params,
+    )(courant_x, courant_y, diffusion, child)
     y_even, y_odd = pl.pallas_call(
         join_kernel,
         out_shape=(shape(Y_ALL, BLK), shape(Y_ALL, BLK)),
@@ -396,34 +413,39 @@
     )(got_x_even, got_x_odd, x_even, to_next, to_prev)
     got_y_odd = exchange(y_odd, "gy", 1)
     got_y_even = exchange(y_even, "gy", 0)
-    inner = pl.pallas_call(
-        inner_kernel,
-        out_shape=shape(VZ, CX, BLK),
-        in_specs=[IN_SMEM] * 3 + [IN_VMEM, pl.BlockSpec(memory_space=pl.ANY)],
-        out_specs=IN_VMEM,
-        compiler_params=params,
-    )(courant_x, courant_y, diffusion, cells, y_even)
+    inner, banks, coarse_banks, counts_y, ghost, above_fix, below_fix, side_weights = pl.pallas_call(
+        middle_kernel,
+        out_shape=(
+            shape(VZ, CX, BLK), shape(2 * BLK, NOPS * BLK, kind=BF16), shape(2, NOPS * BLK, BLK, kind=BF16),
+            shape(CX, CX, kind=BF16), shape(CX, V * BLK), shape(2 * VZ, BLK), shape(2 * VZ, BLK), shape(64, BLK),
+        ),
+        in_specs=[IN_SMEM] * 3 + [IN_VMEM] * 8 + [pl.BlockSpec(memory_space=pl.ANY)],
+        out_specs=(IN_VMEM,) * 8,
+        input_output_aliases={3: 0},
+        scratch_shapes=[pltpu.VMEM((512, V * BLK), BF16)],
+        compiler_params=params,
+    )(
+        courant_x, courant_y, diffusion, inner, cells, fine_bank, coarse_bank, coarse_code, x_even, got_x_even, got_x_odd,
+        y_even,
+    )
     fields_shape = shape(2 * CX, VZ * BLK, kind=BF16)
     select_and_picked = [pltpu.VMEM((NOPS * PB, 2 * CX), BF16), pltpu.VMEM((2, VZ * PB, NOPS * BLK), BF16)]
     new, fields, part_both = pl.pallas_call(
         update_kernel,
         out_shape=(shape(VZ, CX, BLK), fields_shape, shape(VZ * PB, BLK)),
-        in_specs=[IN_SMEM] * 3 + [IN_VMEM] * 2 + [IN_VMEM] * 8,
+        in_specs=[IN_VMEM] * 11,
         out_specs=(IN_VMEM,) * 3,
-        input_output_aliases={3: 0},
+        input_output_aliases={0: 0},
         scratch_shapes=[
-            pltpu.VMEM((2 * VZ, BLK), F32),
-            pltpu.VMEM((2 * VZ, BLK), F32),
             pltpu.VMEM((CX, BLK), F32),
             select_and_picked[0],
             pltpu.VMEM((CX, V * BLK), F32),
-            pltpu.VMEM((1024, V * BLK), BF16),
+            pltpu.VMEM((512, V * BLK), BF16),
             select_and_picked[1],
         ],
         compiler_params=params,
     )(
-        courant_x, courant_y, diffusion,
-        inner, building, x_even, got_x_even, got_x_odd, got_y_even, got_y_odd, banks, coarse_banks, counts,
+        inner, building, got_y_even, got_y_odd, banks, coarse_banks, counts_y, ghost, above_fix, below_fix, side_weights,
     )
     got_both = one_lower(part_both, "gy")
     part_x, part_y = pl.pallas_call(

time: 50.3 us -> 49.6 us (0.986)
  local copies, waits for them, and re-layouts: 2.13 us -> 0.06 us
  waiting for transfers between devices: 6.68 us -> 7.91 us
  Pallas kernels: 21.4 us -> 22.1 us
    unnamed x26, local copies, waits for them, and re-layouts: 2.13 us -> 0.06 us
    pallas_call x1, Pallas kernels: 2.3 us -> 4.08 us  [local(): pl.pallas_call(edges_kernel, out_shape=(shape(VZ, CX + 2 * PAD, BLK), sha...]
    ppermute x4, waiting for transfers between devices: 2.04 us -> 2.89 us  [exchange(): return lax.ppermute(value, axis, pairs)]
    pallas_call x1, Pallas kernels: 4.11 us -> 3.54 us  [local(): pl.pallas_call(middle_kernel, out_shape=(shape(VZ, CX, BLK), shape(2 * BL...]
    pallas_call x1, Pallas kernels: 5.75 us -> 5.22 us  [local(): pl.pallas_call(update_kernel, out_shape=(shape(VZ, CX, BLK), fields_shape...]
    ppermute x3, starting transfers between devices: 9.72 us -> 9.2 us  [one_lower(): lax.ppermute(value, axis, [(a, a - 1) for a in range(1, lax.axis_size(axi...]
  transfers between devices with their start and end apart: 7 -> 7, of which waited for: 3 -> 3; matrix products, arithmetic and copies ran while one was open for 0% -> 0% of each run, Pallas kernels for 27% -> 30%
where the time goes in v4:
time: 49.6 us; the launch traced here: 49.3 us
  Pallas kernels  22.1 us (45%)
  starting transfers between devices  17.6 us (35%)
  waiting for transfers between devices  7.91 us (16%)
  between operations  0.93 us (2%)
  other arithmetic  0.81 us (2%)
    ppermute x3, starting transfers between devices, one_lower(): lax.ppermute(value, axis, [(a, a - 1) for a in range(1, lax.axis_size(axi...  9.2 us
    ppermute x4, starting transfers between devices, exchange(): return lax.ppermute(value, axis, pairs)  8.37 us
    pallas_call x1, Pallas kernels, local(): pl.pallas_call(update_kernel, out_shape=(shape(VZ, CX, BLK), fields_shape...  5.22 us
    ppermute x3, waiting for transfers between devices, one_lower(): lax.ppermute(value, axis, [(a, a - 1) for a in range(1, lax.axis_size(axi...  5.02 us
    pallas_call x1, Pallas kernels, local(): pl.pallas_call(edges_kernel, out_shape=(shape(VZ, CX + 2 * PAD, BLK), sha...  4.08 us
    pallas_call x1, Pallas kernels, local(): pl.pallas_call(sides_kernel, out_shape=(shape(VZ * PB, BLK),) * 2, in_spe...  3.97 us
    pallas_call x1, Pallas kernels, local(): pl.pallas_call(middle_kernel, out_shape=(shape(VZ, CX, BLK), shape(2 * BL...  3.54 us
    pallas_call x1, Pallas kernels, local(): pl.pallas_call(own_kernel, out_shape=(shape(VZ, CX, BLK), shape(CX, BLK),...  3.31 us
  transfers between devices with their start and end apart: 7, of which 3 were waited for; matrix products, arithmetic and copies ran while one was open for 0% of the time, Pallas kernels for 30%

profile of v4, /device:TPU:70, one launch (start us, length us, event | category | flops | bytes accessed | tf_op | source)
XLA Modules:
  0.0 49.3 jit_solution(12699942596945706699)
XLA Ops:
  0.6 0.0 copy-start
  0.6 0.0 copy-start.9
  0.7 0.0 copy-start.8
  0.7 0.0 copy-start.7
  0.7 0.0 copy-start.10
  0.7 0.0 copy-start.11
  0.7 0.0 copy-start.12
  0.7 0.0 copy-start.3
  0.7 0.0 copy-start.4
  0.7 1.9 %shard_map.175 = (f32[144,128]{1,0:T(8,128)}, f32[144,128]{1,0:T(8,128)}) custom-call(f32[32,256,128]{2,1,0:T(8,128)} %bitcast.9, f32[64,128]{1,0:T(8,128)} %bitcast.13, s32[16,16]{1,0:T(8,128)} %tile.1, s32[16,16]{1,0:T(8,128)} %row.1, s32[16,16]{1,0:T(8,128)} %op.1), custom_call_target="tpu_custom_call" | custom-call | tf_op jit(solution)/shard_map/pallas_call | solution.py:383
  2.6 0.0 copy-start.2
  2.7 5.5 %collective-permute-start.1 = (f32[144,128]{1,0:T(8,128)}, f32[144,128]{1,0:T(8,128)S(1)}, u32[]{:S(2)}, u32[]{:S(2)}) collective-permute-start(f32[144,128]{1,0:T(8,128)} %get-tuple-element.30), channel_id=1, source_target_pairs={{16,32},{32,16},{48,64},{64,48},{80,96},{96,80},{17,33},{33,17},{4... | collective-permute-start | bytes 221192 | tf_op jit(solution)/shard_map/ppermute | solution.py:30
  8.2 0.1 collective-permute-start
  8.3 0.0 copy-done
  8.3 0.0 copy-done.9
  8.3 0.0 copy-done.8
  8.3 0.0 copy-done.7
  8.3 4.1 %shard_map.176 = (f32[32,272,128]{2,1,0:T(8,128)S(1)}, f32[128,128]{1,0:T(8,128)S(1)}, f32[128,128]{1,0:T(8,128)S(1)}, f32[32,256,128]{2,1,0:T(8,128)S(1)}) custom-call(f32[8]{0:T(128)S(1)} %copy-done.7, f32[8]{0:T(128)S(1)} %copy-done.8, f32[4]{0:T(128)S(1)} %copy-done.9, f32[32,256,128]{2,1,0:T(8,128)S(1)} %bitcast.10), custom_call_target="tpu_custom_call" | custom-call | tf_op jit(solution)/shard_map/pallas_call | solution.py:397
  12.4 0.0 collective-permute-done.1.odd_x
  12.4 1.9 %collective-permute-done.even_x = f32[144,128]{1,0:T(8,128)S(1)} collective-permute-done((f32[144,128]{1,0:T(8,128)}, f32[144,128]{1,0:T(8,128)S(1)}, u32[]{:S(2)}, u32[]{:S(2)}) %collective-permute-start) | collective-permute-done | bytes 73760 | tf_op jit(solution)/shard_map/ppermute | solution.py:30
  14.3 0.0 copy-done.2
  14.4 1.9 %collective-permute-start.3 = (f32[288,128]{1,0:T(8,128)S(1)}, f32[288,128]{1,0:T(8,128)S(1)}, u32[]{:S(2)}, u32[]{:S(2)}) collective-permute-start(f32[288,128]{1,0:T(8,128)S(1)} %get-tuple-element.35), channel_id=1, source_target_pairs={{1,2},{2,1},{3,4},{4,3},{5,6},{6,5},{7,8},{8,7},{9,10},{10,9},{11,... | collective-permute-start | bytes 442376 | tf_op jit(solution)/shard_map/ppermute | solution.py:30
  16.3 0.9 %collective-permute-start.2 = (f32[288,128]{1,0:T(8,128)S(1)}, f32[288,128]{1,0:T(8,128)S(1)}, u32[]{:S(2)}, u32[]{:S(2)}) collective-permute-start(f32[288,128]{1,0:T(8,128)S(1)} %get-tuple-element.33.after), channel_id=1, source_target_pairs={{0,1},{1,0},{2,3},{3,2},{4,5},{5,4},{6,7},{7,6},{8,9},{9,8},{10,11... | collective-permute-start | bytes 442376 | tf_op jit(solution)/shard_map/ppermute | solution.py:30
  17.1 0.0 copy-done.10
  17.1 0.0 copy-done.11
  17.1 0.0 copy-done.12
  17.2 0.0 copy-done.3
  17.2 0.0 copy-done.4
  17.2 0.0 copy-start.1
  17.2 3.5 %shard_map.178 = (f32[32,256,128]{2,1,0:T(8,128)S(1)}, bf16[256,1024]{1,0:T(8,128)(2,1)S(1)}, bf16[2,1024,128]{2,1,0:T(8,128)(2,1)S(1)}, bf16[256,256]{1,0:T(8,1...) custom-call(f32[8]{0:T(128)S(1)} %copy-done.7, ...), custom_call_target="tpu_custom_call", output_to_operand_aliasing={{0}: (3, {})} | custom-call | tf_op jit(solution)/shard_map/pallas_call | solution.py:416
  20.7 1.0 %collective-permute-done.3.odd_y = f32[288,128]{1,0:T(8,128)S(1)} collective-permute-done((f32[288,128]{1,0:T(8,128)S(1)}, f32[288,128]{1,0:T(8,128)S(1)}, u32[]{:S(2)}, u32[]{:S(2)}) %collective-permute-start.3) | collective-permute-done | bytes 147488 | tf_op jit(solution)/shard_map/ppermute | solution.py:30
  21.7 0.0 collective-permute-done.2.even_y
  21.7 0.0 copy-done.1
  21.7 5.2 %shard_map.179 = (f32[32,256,128]{2,1,0:T(8,128)S(1)}, bf16[512,4096]{1,0:T(8,128)(2,1)S(1)}, f32[512,128]{1,0:T(8,128)S(1)}) custom-call(f32[32,256,128]{2,1,0:T(8,128)S(1)} %get-tuple-element.34.inner, s32[8,256,128]{2,1,0:T(8,128)S(1)} %copy-done.1, f32[288,128]{1,0:T(8,128)S(1)} %collective-permute-done.2.even_y, ...), custom_call_target="tpu_custom_call", output_to_operand_aliasing={{0}: (0, {})} | custom-call | tf_op jit(solution)/shard_map/pallas_call | solution.py:433
  26.9 0.0 copy-start.5
  27.0 0.0 copy-start.6
  27.0 3.5 %collective-permute-start.5 = (f32[512,128]{1,0:T(8,128)S(1)}, f32[512,128]{1,0:T(8,128)S(1)}, u32[]{:S(2)}, u32[]{:S(2)}) collective-permute-start(f32[512,128]{1,0:T(8,128)S(1)} %get-tuple-element.49), channel_id=1, source_target_pairs={{1,0},{2,1},{3,2},{4,3},{5,4},{6,5},{7,6},{8,7},{9,8},{10,9},{11,1... | collective-permute-start | bytes 786440 | tf_op jit(solution)/shard_map/ppermute | solution.py:34
  30.5 4.0 %shard_map.180 = (f32[512,128]{1,0:T(8,128)S(1)}, f32[512,128]{1,0:T(8,128)S(1)}) custom-call(f32[144,128]{1,0:T(8,128)S(1)} %collective-permute-done.even_x, f32[144,128]{1,0:T(8,128)S(1)} %collective-permute-done.1.odd_x, f32[288,128]{1,0:T(8,128)S(1)} %collective-permute-done.2.even_y, f32[288,128]{1,0:T(8,128)S(1)} %collective-permute-done.3.odd_y, ...), custom_call_target="tpu_custom_call" | custom-call | tf_op jit(solution)/shard_map/pallas_call | solution.py:451
  34.5 1.9 %collective-permute-start.4 = (f32[512,128]{1,0:T(8,128)S(1)}, f32[512,128]{1,0:T(8,128)S(1)}, u32[]{:S(2)}, u32[]{:S(2)}) collective-permute-start(f32[512,128]{1,0:T(8,128)S(1)} %get-tuple-element.45.after), channel_id=1, source_target_pairs={{1,0},{2,1},{3,2},{4,3},{5,4},{6,5},{7,6},{8,7},{9,8},{10,9},{11,1... | collective-permute-start | bytes 786440 | tf_op jit(solution)/shard_map/ppermute | solution.py:34
  36.4 0.0 collective-permute-done.5
  36.5 3.7 %collective-permute-start.6 = (f32[512,128]{1,0:T(8,128)S(1)}, f32[512,128]{1,0:T(8,128)S(1)}, u32[]{:S(2)}, u32[]{:S(2)}) collective-permute-start(f32[512,128]{1,0:T(8,128)S(1)} %add.21), channel_id=1, source_target_pairs={{16,0},{32,16},{48,32},{64,48},{80,64},{96,80},{112,96},{17,1},{33... | collective-permute-start | bytes 786440 | tf_op jit(solution)/shard_map/ppermute | solution.py:34
  40.2 0.0 copy-done.5
  40.2 0.0 copy-done.6
  40.2 3.3 %shard_map.181 = (f32[32,256,128]{2,1,0:T(8,128)}, f32[256,128]{1,0:T(8,128)}, f32[512,128]{1,0:T(8,128)S(1)}) custom-call(f32[144,128]{1,0:T(8,128)S(1)} %copy-done.2, f32[32,256,128]{2,1,0:T(8,128)S(1)} %get-tuple-element.43.new, bf16[512,4096]{1,0:T(8,128)(2,1)S(1)} %get-tuple-element.44.fields, bf16[256,1024]{1,0:T(8,128)(2,1)S(1)} %get-tuple-element.36.banks, ...), custom_call_target="tpu_custom_call" | custom-call | tf_op jit(solution)/shard_map/pallas_call | solution.py:461
  43.6 0.0 collective-permute-done.4
  43.6 5.0 %collective-permute-done.6 = f32[512,128]{1,0:T(8,128)S(1)} collective-permute-done((f32[512,128]{1,0:T(8,128)S(1)}, f32[512,128]{1,0:T(8,128)S(1)}, u32[]{:S(2)}, u32[]{:S(2)}) %collective-permute-start.6) | collective-permute-done | bytes 262176 | tf_op jit(solution)/shard_map/ppermute | solution.py:34
  48.6 0.8 %multiply_add_fusion = f32[512,128]{1,0:T(8,128)} fusion(f32[512,128]{1,0:T(8,128)S(1)} %get-tuple-element.47, f32[512,128]{1,0:T(8,128)S(1)} %collective-permute-done.4, f32[512,128]{1,0:T(8,128)S(1)} %collective-permute-done.6), kind=kLoop, calls=%fused_computation | loop fusion | flops 196608 | bytes 1048576 | tf_op jit(solution)/shard_map/add | solution.py:469
  (3 shorter events, 0.1 us)
Async XLA Ops:
  0.6 7.6 %copy-start = (f32[4,8,256,128]{3,2,1,0:T(8,128)S(1)}, f32[4,8,256,128]{3,2,1,0:T(8,128)}, u32[]{:S(2)}) copy-start(f32[4,8,256,128]{3,2,1,0:T(8,128)} %param.16) | copy-start | bytes 12582916
  0.6 7.6 %copy-start.9 = (f32[4]{0:T(128)S(1)}, f32[4]{0:T(128)}, u32[]{:S(2)}) copy-start(f32[4]{0:T(128)} %diffusion.3) | copy-start | bytes 52
  0.7 7.6 %copy-start.8 = (f32[8]{0:T(128)S(1)}, f32[8]{0:T(128)}, u32[]{:S(2)}) copy-start(f32[8]{0:T(128)} %courant_y.3) | copy-start | bytes 100
  0.7 7.6 %copy-start.7 = (f32[8]{0:T(128)S(1)}, f32[8]{0:T(128)}, u32[]{:S(2)}) copy-start(f32[8]{0:T(128)} %courant_x.3) | copy-start | bytes 100
  0.7 16.5 %copy-start.10 = (s32[256,1,4]{0,2,1:T(4,128)S(1)}, s32[256,1,4]{0,2,1:T(4,128)}, u32[]{:S(2)}) copy-start(s32[256,1,4]{0,2,1:T(4,128)} %param.29) | copy-start | bytes 12292
  0.7 16.5 %copy-start.11 = (s32[256,1,4]{0,2,1:T(4,128)S(1)}, s32[256,1,4]{0,2,1:T(4,128)}, u32[]{:S(2)}) copy-start(s32[256,1,4]{0,2,1:T(4,128)} %param.28) | copy-start | bytes 12292
  0.7 16.5 %copy-start.12 = (s32[256,1,4]{0,2,1:T(4,128)S(1)}, s32[256,1,4]{0,2,1:T(4,128)}, u32[]{:S(2)}) copy-start(s32[256,1,4]{0,2,1:T(4,128)} %param.30) | copy-start | bytes 12292
  0.7 16.5 %copy-start.3 = (f32[8,128,128]{2,1,0:T(8,128)S(1)}, f32[8,128,128]{2,1,0:T(8,128)}, u32[]{:S(2)}) copy-start(f32[8,128,128]{2,1,0:T(8,128)} %fine.1) | copy-start | bytes 1572868
  0.7 16.5 %copy-start.4 = (f32[8,128,128]{2,1,0:T(8,128)S(1)}, f32[8,128,128]{2,1,0:T(8,128)}, u32[]{:S(2)}) copy-start(f32[8,128,128]{2,1,0:T(8,128)} %coarse.1) | copy-start | bytes 1572868
  2.6 11.7 %copy-start.2 = (f32[144,128]{1,0:T(8,128)S(1)}, f32[144,128]{1,0:T(8,128)}, u32[]{:S(2)}) copy-start(f32[144,128]{1,0:T(8,128)} %get-tuple-element.27.own_even.own_x) | copy-start | bytes 221188
  2.7 9.7 %collective-permute-start.1 = (f32[144,128]{1,0:T(8,128)}, f32[144,128]{1,0:T(8,128)S(1)}, u32[]{:S(2)}, u32[]{:S(2)}) collective-permute-start(f32[144,128]{1,0:T(8,128)} %get-tuple-element.30), channel_id=1, source_target_pairs={{16,32},{32,16},{48,64},{64,48},{80,96},{96,80},{17,33},{33,17},{4... | collective-permute-start | bytes 221192 | tf_op jit(solution)/shard_map/ppermute | solution.py:30
  8.2 6.1 %collective-permute-start = (f32[144,128]{1,0:T(8,128)}, f32[144,128]{1,0:T(8,128)S(1)}, u32[]{:S(2)}, u32[]{:S(2)}) collective-permute-start(f32[144,128]{1,0:T(8,128)} %get-tuple-element.27.own_even.own_x), channel_id=1, source_target_pairs={{0,16},{16,0},{32,48},{48,32},{64,80},{80,64},{96,112},{112,96},{1... | collective-permute-start | bytes 221192 | tf_op jit(solution)/shard_map/ppermute | solution.py:30
  14.4 7.4 %collective-permute-start.3 = (f32[288,128]{1,0:T(8,128)S(1)}, f32[288,128]{1,0:T(8,128)S(1)}, u32[]{:S(2)}, u32[]{:S(2)}) collective-permute-start(f32[288,128]{1,0:T(8,128)S(1)} %get-tuple-element.35), channel_id=1, source_target_pairs={{1,2},{2,1},{3,4},{4,3},{5,6},{6,5},{7,8},{8,7},{9,10},{10,9},{11,... | collective-permute-start | bytes 442376 | tf_op jit(solution)/shard_map/ppermute | solution.py:30
  16.3 5.4 %collective-permute-start.2 = (f32[288,128]{1,0:T(8,128)S(1)}, f32[288,128]{1,0:T(8,128)S(1)}, u32[]{:S(2)}, u32[]{:S(2)}) collective-permute-start(f32[288,128]{1,0:T(8,128)S(1)} %get-tuple-element.33.after), channel_id=1, source_target_pairs={{0,1},{1,0},{2,3},{3,2},{4,5},{5,4},{6,7},{7,6},{8,9},{9,8},{10,11... | collective-permute-start | bytes 442376 | tf_op jit(solution)/shard_map/ppermute | solution.py:30
  17.2 4.5 %copy-start.1 = (s32[8,256,128]{2,1,0:T(8,128)S(1)}, s32[8,256,128]{2,1,0:T(8,128)}, u32[]{:S(2)}) copy-start(s32[8,256,128]{2,1,0:T(8,128)} %walls.1) | copy-start | bytes 3145732
  26.9 13.3 %copy-start.5 = (f32[4,8,16,128]{3,2,1,0:T(8,128)S(1)}, f32[4,8,16,128]{3,2,1,0:T(8,128)}, u32[]{:S(2)}) copy-start(f32[4,8,16,128]{3,2,1,0:T(8,128)} %param.17) | copy-start | bytes 786436
  27.0 13.3 %copy-start.6 = (f32[256,128]{1,0:T(8,128)S(1)}, f32[256,128]{1,0:T(8,128)}, u32[]{:S(2)}) copy-start(f32[256,128]{1,0:T(8,128)} %radiant.1) | copy-start | bytes 393220
  27.0 9.5 %collective-permute-start.5 = (f32[512,128]{1,0:T(8,128)S(1)}, f32[512,128]{1,0:T(8,128)S(1)}, u32[]{:S(2)}, u32[]{:S(2)}) collective-permute-start(f32[512,128]{1,0:T(8,128)S(1)} %get-tuple-element.49), channel_id=1, source_target_pairs={{1,0},{2,1},{3,2},{4,3},{5,4},{6,5},{7,6},{8,7},{9,8},{10,9},{11,1... | collective-permute-start | bytes 786440 | tf_op jit(solution)/shard_map/ppermute | solution.py:34
  34.5 9.1 %collective-permute-start.4 = (f32[512,128]{1,0:T(8,128)S(1)}, f32[512,128]{1,0:T(8,128)S(1)}, u32[]{:S(2)}, u32[]{:S(2)}) collective-permute-start(f32[512,128]{1,0:T(8,128)S(1)} %get-tuple-element.45.after), channel_id=1, source_target_pairs={{1,0},{2,1},{3,2},{4,3},{5,4},{6,5},{7,6},{8,7},{9,8},{10,9},{11,1... | collective-permute-start | bytes 786440 | tf_op jit(solution)/shard_map/ppermute | solution.py:34
  36.5 12.1 %collective-permute-start.6 = (f32[512,128]{1,0:T(8,128)S(1)}, f32[512,128]{1,0:T(8,128)S(1)}, u32[]{:S(2)}, u32[]{:S(2)}) collective-permute-start(f32[512,128]{1,0:T(8,128)S(1)} %add.21), channel_id=1, source_target_pairs={{16,0},{32,16},{48,32},{64,48},{80,64},{96,80},{112,96},{17,1},{33... | collective-permute-start | bytes 786440 | tf_op jit(solution)/shard_map/ppermute | solution.py:34

commit v5 on v4

--- a/solution.py
+++ b/solution.py
@@ -10,7 +10,7 @@
 F32, BF16 = jnp.float32, jnp.bfloat16
 PAD = 8
 CHUNK = 64
-EARLY = 2
+EARLY = 3
 VMEM_BYTES = 32 * 1024 * 1024
 
 X_ROWS, X_PAR, X_IDX, X_ALL = 0, 64, 128, 144
@@ -176,15 +176,12 @@
         select[row : row + PB, CX : 2 * CX] = total
 
 
-def gather(select, pair, vz, picked):
-    many = select.shape[0] // NOPS
-    found = jnp.dot(select[...], pair, preferred_element_type=F32)
-    for part, value in enumerate(split(found)):
-        for o in range(NOPS):
-            for e in range(2):
-                picked[part, pl.ds(pl.multiple_of(many * (vz + e), many), many), BLK * o : BLK * (o + 1)] = value[
-                    many * o : many * (o + 1), BLK * e : BLK * (e + 1)
-                ]
+def turn_of(vz):
+    return (2 * BLK - 2 - 4 * vz) % BLK
+
+
+def at_edges(rows):
+    return (lanes((rows, BLK)) + 2) % BLK < 4
 
 
 def through_banks(picked, banks):
@@ -193,9 +190,23 @@
     return both[:, :BLK] + both[:, BLK:] + rest
 
 
-def gather_all(select, fields, picked):
+def gather_all(select, fields, side, edge, picked):
+    rows = select.shape[0]
+    many = rows // NOPS
+    edge[...] = jnp.dot(select[...], side[...], preferred_element_type=F32)
+    near = at_edges(rows)
+
     def one_pair(i, carry):
-        gather(select, fields[:, pl.ds(pl.multiple_of(2 * BLK * i, 2 * BLK), 2 * BLK)], 2 * i, picked)
+        pair = fields[:, pl.ds(pl.multiple_of(2 * BLK * i, 2 * BLK), 2 * BLK)]
+        found = jnp.dot(select[...], pair, preferred_element_type=F32)
+        for e in range(2):
+            vz = 2 * i + e
+            whole = found[:, BLK * e : BLK * (e + 1)] + jnp.where(near, pltpu.roll(edge[...], turn_of(vz), 1), 0.0)
+            for part, value in enumerate(split(whole)):
+                for o in range(NOPS):
+                    picked[part, pl.ds(pl.multiple_of(many * vz, many), many), BLK * o : BLK * (o + 1)] = value[
+                        many * o : many * (o + 1)
+                    ]
         return carry
 
     lax.fori_loop(0, VZ // 2, one_pair, 0, unroll=4)
@@ -220,8 +231,8 @@
 
 
 def middle_kernel(
-    courant_x, courant_y, diffusion, so_far, cells, fine, coarse, code, own_x, even_x, odd_x, after,
-    inner, banks, coarse_banks, counts_y, ghost, above_fix, below_fix, side_weights, table,
+    courant_x, courant_y, diffusion, so_far, cells, walls, fine, coarse, code, own_x, even_x, odd_x, after,
+    inner, fields, banks, coarse_banks, counts_y, side_weights, open_sides, ghost, above_fix, below_fix, table,
 ):
     del so_far, after
     flag_x = lax.axis_index("gx") % 2 == 0
@@ -274,48 +285,24 @@
         ghost[:, BLK * v : BLK * (v + 1)] = diffusion[v] * made[:, BLK * v : BLK * (v + 1)]
     step_inside(EARLY, V, courant_x, courant_y, diffusion, cells, inner)
 
-
-def update_kernel(
-    inner, walls, even_y, odd_y, banks, coarse_banks, counts_y, ghost_x, above_fix, below_fix, side_weights,
-    new, fields, part_both,
-    side_fix, select, ghost, table, picked,
-):
-    flag_y = lax.axis_index("gy") % 2 == 0
-    prev_y = jnp.where(flag_y, odd_y[...], even_y[...])
-
-    half = CX // 2
-    next_y = jnp.where(flag_y, even_y[Y_COLS:Y_PAR], odd_y[Y_COLS:Y_PAR])
-    before = prev_y[Y_COLS:Y_PAR]
-    upper = lanes((half, BLK)) % 4 >= 2
-    by_minus_2, by_minus_1, by_plus_1, by_plus_2 = (side_weights[8 * i : 8 * i + 1] for i in range(4))
-    for part in range(2):
-        if part == 0:
-            columns = jnp.where(upper, next_y, before)
-        else:
-            columns = jnp.where(upper, pltpu.roll(next_y, 2, 1), pltpu.roll(before, BLK - 2, 1))
-        side_fix[half * part : half * (part + 1)] = (
-            by_minus_2 * pltpu.roll(columns, BLK - 2, 1)
-            + by_minus_1 * pltpu.roll(columns, BLK - 1, 1)
-            + by_plus_1 * pltpu.roll(columns, 1, 1)
-            + by_plus_2 * pltpu.roll(columns, 2, 1)
-        )
-
-    made = ghost_part([prev_y[Y_PAR:Y_RELAY], prev_y[Y_RELAY:Y_IDX]], coarse_banks, counts_y[...], table)
-    for v in range(V):
-        at = (slice(None), slice(BLK * v, BLK * (v + 1)))
-        ghost[at] = ghost_x[at] + side_weights[32 + 8 * v : 33 + 8 * v] * made[at]
-
-    choose(prev_y[Y_RIDX:Y_ALL], 3, select)
-    at_edge = (lanes((CHUNK, BLK)) + 2) % BLK < 4
+    for r in range(0, CX, CHUNK):
+        level = lanes((CHUNK, BLK)) // 4
+        marks = jnp.zeros((CHUNK, BLK), F32)
+        for z in range(NZ):
+            wall = jnp.where(walls[z, r : r + CHUNK] == 1, 0.0, 1.0)
+            marks = jnp.where(level == z, pltpu.roll(wall, 4 * z + 2, 1), marks)
+        total = marks
+        for v in range(1, V):
+            total = total + pltpu.roll(marks, 4 * NZ * v, 1)
+        open_sides[r : r + CHUNK] = total
+
     no_rows = jnp.zeros((6, BLK), F32)
 
     def variable(v, carry):
         for z in range(NZ):
             vz = NZ * v + z
-            turn = (2 * BLK - 2 - 4 * vz) % BLK
             for r in range(0, CX, CHUNK):
                 total = inner[vz, r : r + CHUNK]
-                total = total + jnp.where(at_edge, pltpu.roll(side_fix[r : r + CHUNK], turn, 1), 0.0)
                 if z == NZ - 1:
                     total = total + ghost[r : r + CHUNK, pl.ds(pl.multiple_of(BLK * v, BLK), BLK)]
                 if r == 0:
@@ -325,25 +312,65 @@
                     fix = jnp.concatenate([no_rows, below_fix[pl.ds(2 * vz, 2)]], axis=0)
                     total = jnp.concatenate([total[:-8], total[-8:] + fix], axis=0)
                 total = jnp.where(walls[z, r : r + CHUNK] == 1, 0.0, total)
-                new[vz, r : r + CHUNK] = total
+                inner[vz, r : r + CHUNK] = total
                 high, low = split(total)
                 columns = pl.ds(pl.multiple_of(BLK * vz, BLK), BLK)
                 fields[r : r + CHUNK, columns] = high
                 fields[CX + r : CX + r + CHUNK, columns] = low
-            if z % 2 == 1:
-                pair = pl.ds(pl.multiple_of(BLK * (vz - 1), BLK), 2 * BLK)
-                gather(select, fields[:, pair], vz - 1, picked)
         return carry
 
     lax.fori_loop(0, V, variable, 0)
+
+
+def update_kernel(
+    old, old_fields, walls, even_y, odd_y, banks, coarse_banks, counts_y, side_weights, open_sides,
+    new, fields, side_fix, side, part_both,
+    select, edge, table, picked,
+):
+    del old, old_fields
+    flag_y = lax.axis_index("gy") % 2 == 0
+    prev_y = jnp.where(flag_y, odd_y[...], even_y[...])
+
+    half = CX // 2
+    next_y = jnp.where(flag_y, even_y[Y_COLS:Y_PAR], odd_y[Y_COLS:Y_PAR])
+    before = prev_y[Y_COLS:Y_PAR]
+    upper = lanes((half, BLK)) % 4 >= 2
+    by_minus_2, by_minus_1, by_plus_1, by_plus_2 = (side_weights[8 * i : 8 * i + 1] for i in range(4))
+    for part in range(2):
+        at = slice(half * part, half * (part + 1))
+        if part == 0:
+            columns = jnp.where(upper, next_y, before)
+        else:
+            columns = jnp.where(upper, pltpu.roll(next_y, 2, 1), pltpu.roll(before, BLK - 2, 1))
+        total = (
+            by_minus_2 * pltpu.roll(columns, BLK - 2, 1)
+            + by_minus_1 * pltpu.roll(columns, BLK - 1, 1)
+            + by_plus_1 * pltpu.roll(columns, 1, 1)
+            + by_plus_2 * pltpu.roll(columns, 2, 1)
+        )
+        total = jnp.where(open_sides[at] > 0.5, total, 0.0)
+        side_fix[at] = total
+        side[at], side[CX + half * part : CX + half * (part + 1)] = split(total)
+
+    made = ghost_part([prev_y[Y_PAR:Y_RELAY], prev_y[Y_RELAY:Y_IDX]], coarse_banks, counts_y[...], table)
+    for v in range(V):
+        vz = NZ * v + NZ - 1
+        added = side_weights[32 + 8 * v : 33 + 8 * v] * made[:, BLK * v : BLK * (v + 1)]
+        total = new[vz] + jnp.where(walls[NZ - 1] == 1, 0.0, added)
+        new[vz] = total
+        columns = slice(BLK * vz, BLK * (vz + 1))
+        fields[0:CX, columns], fields[CX : 2 * CX, columns] = split(total)
+
+    choose(prev_y[Y_RIDX:Y_ALL], 3, select)
+    gather_all(select, fields, side, edge, picked)
     part_both[...] = through_banks(picked, banks)
 
 
-def sides_kernel(even_x, odd_x, even_y, odd_y, fields, banks, part_x, part_y, select, picked):
+def sides_kernel(even_x, odd_x, even_y, odd_y, fields, side, banks, part_x, part_y, select, edge, picked):
     flag_x, flag_y = lax.axis_index("gx") % 2 == 0, lax.axis_index("gy") % 2 == 0
     choose(jnp.where(flag_x, odd_x[X_IDX:X_ALL], even_x[X_IDX:X_ALL]), 1, select, 0)
     choose(jnp.where(flag_y, odd_y[Y_IDX:Y_RIDX], even_y[Y_IDX:Y_RIDX]), 2, select, 1)
-    gather_all(select, fields, picked)
+    gather_all(select, fields, side, edge, picked)
     result = through_banks(picked, banks)
     for vz in range(VZ):
         part_x[PB * vz : PB * (vz + 1)] = result[2 * PB * vz : 2 * PB * vz + PB]
@@ -355,18 +382,33 @@
     to_y[...] = part_y[...]
 
 
-def own_kernel(own_x, new, fields, banks, radiant, slab, after, states, comfort, so_far, select, picked, sem):
+def own_kernel(
+    own_x, new, side_fix, fields, side, banks, radiant, slab, after,
+    states, comfort, so_far,
+    whole, select, edge, picked, sems,
+):
     del after
-    out = pltpu.make_async_copy(new, states, sem)
-    out.start()
-    choose(own_x[X_IDX:X_ALL], 0, select)
-    gather_all(select, fields, picked)
-    so_far[...] = 0.5 * slab[...] + 0.5 * through_banks(picked, banks)
-    u, w, t, h = (new[NZ * v] for v in range(V))
+    near = at_edges(CHUNK)
+
+    def variable(v, carry):
+        for z in range(NZ):
+            vz = NZ * v + z
+            for r in range(0, CX, CHUNK):
+                turned = pltpu.roll(side_fix[r : r + CHUNK], turn_of(vz), 1)
+                whole[vz, r : r + CHUNK] = new[vz, r : r + CHUNK] + jnp.where(near, turned, 0.0)
+        pltpu.make_async_copy(whole.at[pl.ds(NZ * v, NZ)], states.at[pl.ds(NZ * v, NZ)], sems.at[v]).start()
+        return carry
+
+    lax.fori_loop(0, V, variable, 0)
+    u, w, t, h = (whole[NZ * v] for v in range(V))
     speed = jnp.sqrt(u * u + w * w + 0.25)
     excess = radiant[...] - t
     comfort[...] = t + 0.3 * excess - 0.6 * (speed - 1.0) + 0.4 * h + 0.1 * t * excess - 0.15 * speed * excess
-    out.wait()
+    choose(own_x[X_IDX:X_ALL], 0, select)
+    gather_all(select, fields, side, edge, picked)
+    so_far[...] = 0.5 * slab[...] + 0.5 * through_banks(picked, banks)
+    for v in range(V):
+        pltpu.make_async_copy(whole.at[pl.ds(NZ * v, NZ)], states.at[pl.ds(NZ * v, NZ)], sems.at[v]).wait()
 
 
 def shape(*dims, kind=F32):
@@ -389,8 +431,8 @@
             pltpu.VMEM((VZ, 8, BLK), F32), pltpu.VMEM((VZ, 8, BLK), F32), pltpu.VMEM((V * PB, BLK), F32),
             pltpu.VMEM((3, PB, K), jnp.int32), pltpu.VMEM((3, PB, BLK), F32), pltpu.SemaphoreType.DMA((6,)),
         ],
-        compiler_params=pltpu.CompilerParams(vmem_limit_bytes=56 * 1024 * 1024),
-    )(child, parent, fine_tile, fine_row, fine_op)
+        compiler_params=params,
+    )(*(pltpu.with_memory_space_constraint(a, pltpu.HBM) for a in (child, parent, fine_tile, fine_row, fine_op)))
     got_x_even = exchange(x_even, "gx", 0)
     got_x_odd = exchange(x_odd, "gx", 1)
     coarse_code = ((coarse_tile >> 1) * 256 + coarse_op * 32 + (coarse_tile & 1) * PB + coarse_row).reshape(CX, KI).T
@@ -413,59 +455,73 @@
     )(got_x_even, got_x_odd, x_even, to_next, to_prev)
     got_y_odd = exchange(y_odd, "gy", 1)
     got_y_even = exchange(y_even, "gy", 0)
-    inner, banks, coarse_banks, counts_y, ghost, above_fix, below_fix, side_weights = pl.pallas_call(
+    fields_shape = shape(2 * CX, VZ * BLK, kind=BF16)
+    inner, fields, banks, coarse_banks, counts_y, side_weights, open_sides = pl.pallas_call(
         middle_kernel,
         out_shape=(
-            shape(VZ, CX, BLK), shape(2 * BLK, NOPS * BLK, kind=BF16), shape(2, NOPS * BLK, BLK, kind=BF16),
-            shape(CX, CX, kind=BF16), shape(CX, V * BLK), shape(2 * VZ, BLK), shape(2 * VZ, BLK), shape(64, BLK),
+            shape(VZ, CX, BLK), fields_shape, shape(2 * BLK, NOPS * BLK, kind=BF16), shape(2, NOPS * BLK, BLK, kind=BF16),
+            shape(CX, CX, kind=BF16), shape(64, BLK), shape(CX, BLK),
         ),
-        in_specs=[IN_SMEM] * 3 + [IN_VMEM] * 8 + [pl.BlockSpec(memory_space=pl.ANY)],
-        out_specs=(IN_VMEM,) * 8,
+        in_specs=[IN_SMEM] * 3 + [IN_VMEM] * 9 + [pl.BlockSpec(memory_space=pl.ANY)],
+        out_specs=(IN_VMEM,) * 7,
         input_output_aliases={3: 0},
-        scratch_shapes=[pltpu.VMEM((512, V * BLK), BF16)],
+        scratch_shapes=[
+            pltpu.VMEM((CX, V * BLK), F32),
+            pltpu.VMEM((2 * VZ, BLK), F32),
+            pltpu.VMEM((2 * VZ, BLK), F32),
+            pltpu.VMEM((512, V * BLK), BF16),
+        ],
         compiler_params=params,
     )(
-        courant_x, courant_y, diffusion, inner, cells, fine_bank, coarse_bank, coarse_code, x_even, got_x_even, got_x_odd,
-        y_even,
+        courant_x, courant_y, diffusion, inner, cells, building, fine_bank, coarse_bank, coarse_code,
+        x_even, got_x_even, got_x_odd, y_even,
     )
-    fields_shape = shape(2 * CX, VZ * BLK, kind=BF16)
-    select_and_picked = [pltpu.VMEM((NOPS * PB, 2 * CX), BF16), pltpu.VMEM((2, VZ * PB, NOPS * BLK), BF16)]
-    new, fields, part_both = pl.pallas_call(
+
+    def choosing(tiles):
+        rows = tiles * NOPS * PB
+        return [
+            pltpu.VMEM((rows, 2 * CX), BF16),
+            pltpu.VMEM((rows, BLK), F32),
+        ]
+
+    new, fields, side_fix, side, part_both = pl.pallas_call(
         update_kernel,
-        out_shape=(shape(VZ, CX, BLK), fields_shape, shape(VZ * PB, BLK)),
-        in_specs=[IN_VMEM] * 11,
-        out_specs=(IN_VMEM,) * 3,
-        input_output_aliases={0: 0},
-        scratch_shapes=[
-            pltpu.VMEM((CX, BLK), F32),
-            select_and_picked[0],
-            pltpu.VMEM((CX, V * BLK), F32),
+        out_shape=(
+            shape(VZ, CX, BLK), fields_shape, shape(CX, BLK), shape(2 * CX, BLK, kind=BF16), shape(VZ * PB, BLK),
+        ),
+        in_specs=[IN_VMEM] * 10,
+        out_specs=(IN_VMEM,) * 5,
+        input_output_aliases={0: 0, 1: 1},
+        scratch_shapes=choosing(1) + [
             pltpu.VMEM((512, V * BLK), BF16),
-            select_and_picked[1],
+            pltpu.VMEM((2, VZ * PB, NOPS * BLK), BF16),
         ],
         compiler_params=params,
-    )(
-        inner, building, got_y_even, got_y_odd, banks, coarse_banks, counts_y, ghost, above_fix, below_fix, side_weights,
-    )
+    )(inner, fields, building, got_y_even, got_y_odd, banks, coarse_banks, counts_y, side_weights, open_sides)
     got_both = one_lower(part_both, "gy")
     part_x, part_y = pl.pallas_call(
         sides_kernel,
         out_shape=(shape(VZ * PB, BLK),) * 2,
-        in_specs=[IN_VMEM] * 6,
+        in_specs=[IN_VMEM] * 7,
         out_specs=(IN_VMEM,) * 2,
-        scratch_shapes=[pltpu.VMEM((2 * NOPS * PB, 2 * CX), BF16), pltpu.VMEM((2, 2 * VZ * PB, NOPS * BLK), BF16)],
-        compiler_params=params,
-    )(got_x_even, got_x_odd, got_y_even, got_y_odd, fields, banks)
+        scratch_shapes=choosing(2) + [pltpu.VMEM((2, 2 * VZ * PB, NOPS * BLK), BF16)],
+        compiler_params=params,
+    )(got_x_even, got_x_odd, got_y_even, got_y_odd, fields, side, banks)
     got_x = one_lower(part_x + got_both, "gx")
     got_y = one_lower(part_y, "gy")
     states, comfort, so_far = pl.pallas_call(
         own_kernel,
         out_shape=(shape(VZ, CX, BLK), shape(CX, BLK), shape(VZ * PB, BLK)),
-        in_specs=[IN_VMEM] * 6 + [pl.BlockSpec(memory_space=pl.ANY)],
+        in_specs=[IN_VMEM] * 8 + [pl.BlockSpec(memory_space=pl.ANY)],
         out_specs=(IN_HBM, IN_VMEM, IN_VMEM),
-        scratch_shapes=select_and_picked + [pltpu.SemaphoreType.DMA],
-        compiler_params=params,
-    )(x_even, new, fields, banks, radiative_mean_kelvin, parent_slab.reshape(VZ * PB, BLK), part_y)
+        scratch_shapes=[pltpu.VMEM((VZ, CX, BLK), F32)] + choosing(1) + [
+            pltpu.VMEM((2, VZ * PB, NOPS * BLK), BF16),
+            pltpu.SemaphoreType.DMA((V,)),
+        ],
+        compiler_params=params,
+    )(
+        x_even, new, side_fix, fields, side, banks, radiative_mean_kelvin, parent_slab.reshape(VZ * PB, BLK), part_y,
+    )
     parent_new = so_far + 0.5 * (got_y + got_x)
     return states.reshape(child_state.shape), parent_new.reshape(parent_slab.shape), comfort
 

time: 49.6 us -> 48.3 us (0.974)
  waiting for transfers between devices: 7.91 us -> 4.24 us
  starting transfers between devices: 17.6 us -> 18.9 us
  Pallas kernels: 22.1 us -> 23.1 us
    ppermute x3, waiting for transfers between devices: 5.02 us -> 3.09 us  [one_lower(): lax.ppermute(value, axis, [(a, a - 1) for a in range(1, lax.axis_size(axi...]
    pallas_call x1, Pallas kernels: 5.22 us -> 3.31 us  [local(): pl.pallas_call(update_kernel, out_shape=(shape(VZ, CX, BLK), fields_shape...]
    ppermute x4, waiting for transfers between devices: 2.89 us -> 1.15 us  [exchange(): return lax.ppermute(value, axis, pairs)]
    pallas_call x1, Pallas kernels: 3.31 us -> 4.88 us  [local(): pl.pallas_call(own_kernel, out_shape=(shape(VZ, CX, BLK), shape(CX, BLK),...]
    ppermute x3, starting transfers between devices: 9.2 us -> 10.6 us  [one_lower(): lax.ppermute(value, axis, [(a, a - 1) for a in range(1, lax.axis_size(axi...]
    pallas_call x1, Pallas kernels: 4.08 us -> 4.99 us  [local(): pl.pallas_call(edges_kernel, out_shape=(shape(VZ, CX + 2 * PAD, BLK), sha...]
    pallas_call x1, Pallas kernels: 1.92 us -> 1.26 us  [local(): pl.pallas_call(rows_kernel, out_shape=(shape(X_ALL, BLK), shape(X_ALL, BL...]
    pallas_call x1, Pallas kernels: 3.54 us -> 4.16 us  [local(): pl.pallas_call(middle_kernel, out_shape=(shape(VZ, CX, BLK), fields_shape...]
  transfers between devices with their start and end apart: 7 -> 7, of which waited for: 3 -> 3; matrix products, arithmetic and copies ran while one was open for 0% -> 0% of each run, Pallas kernels for 30% -> 38%
where the time goes in v5:
time: 48.3 us; the launch traced here: 48.1 us
  Pallas kernels  23.1 us (48%)
  starting transfers between devices  18.9 us (39%)
  waiting for transfers between devices  4.24 us (9%)
  between operations  0.93 us (2%)
  other arithmetic  0.81 us (2%)
    ppermute x3, starting transfers between devices, one_lower(): lax.ppermute(value, axis, [(a, a - 1) for a in range(1, lax.axis_size(axi...  10.6 us
    ppermute x4, starting transfers between devices, exchange(): return lax.ppermute(value, axis, pairs)  8.37 us
    pallas_call x1, Pallas kernels, local(): pl.pallas_call(edges_kernel, out_shape=(shape(VZ, CX + 2 * PAD, BLK), sha...  4.99 us
    pallas_call x1, Pallas kernels, local(): pl.pallas_call(own_kernel, out_shape=(shape(VZ, CX, BLK), shape(CX, BLK),...  4.88 us
    pallas_call x1, Pallas kernels, local(): pl.pallas_call(sides_kernel, out_shape=(shape(VZ * PB, BLK),) * 2, in_spe...  4.45 us
    pallas_call x1, Pallas kernels, local(): pl.pallas_call(middle_kernel, out_shape=(shape(VZ, CX, BLK), fields_shape...  4.16 us
    pallas_call x1, Pallas kernels, local(): pl.pallas_call(update_kernel, out_shape=(shape(VZ, CX, BLK), fields_shape...  3.31 us
    ppermute x3, waiting for transfers between devices, one_lower(): lax.ppermute(value, axis, [(a, a - 1) for a in range(1, lax.axis_size(axi...  3.09 us
  transfers between devices with their start and end apart: 7, of which 3 were waited for; matrix products, arithmetic and copies ran while one was open for 0% of the time, Pallas kernels for 38%

profile of v5, /device:TPU:70, one launch (start us, length us, event | category | flops | bytes accessed | tf_op | source)
XLA Modules:
  0.0 48.1 jit_solution(3682635006501487920)
XLA Ops:
  0.6 0.0 copy-start
  0.6 0.0 copy-start.8
  0.7 0.0 copy-start.7
  0.7 0.0 copy-start.6
  0.7 0.0 copy-start.9
  0.7 0.0 copy-start.10
  0.7 0.0 copy-start.11
  0.7 0.0 copy-start.1
  0.7 0.0 copy-start.2
  0.7 0.0 copy-start.3
  0.7 1.3 %shard_map.175 = (f32[144,128]{1,0:T(8,128)S(1)}, f32[144,128]{1,0:T(8,128)S(1)}) custom-call(f32[32,256,128]{2,1,0:T(8,128)} %bitcast.9, f32[64,128]{1,0:T(8,128)} %bitcast.13, s32[16,16]{1,0:T(8,128)} %tile.1, s32[16,16]{1,0:T(8,128)} %row.1, s32[16,16]{1,0:T(8,128)} %op.1), custom_call_target="tpu_custom_call" | custom-call | tf_op jit(solution)/shard_map/pallas_call | solution.py:425
  2.0 5.5 %collective-permute-start.1 = (f32[144,128]{1,0:T(8,128)S(1)}, f32[144,128]{1,0:T(8,128)S(1)}, u32[]{:S(2)}, u32[]{:S(2)}) collective-permute-start(f32[144,128]{1,0:T(8,128)S(1)} %get-tuple-element.31), channel_id=1, source_target_pairs={{16,32},{32,16},{48,64},{64,48},{80,96},{96,80},{17,33},{33,17},{4... | collective-permute-start | bytes 221192 | tf_op jit(solution)/shard_map/ppermute | solution.py:30
  7.5 0.1 collective-permute-start
  7.6 0.0 copy-done
  7.6 0.0 copy-done.8
  7.6 0.0 copy-done.7
  7.6 0.0 copy-done.6
  7.6 5.0 %shard_map.176 = (f32[32,272,128]{2,1,0:T(8,128)S(1)}, f32[128,128]{1,0:T(8,128)S(1)}, f32[128,128]{1,0:T(8,128)S(1)}, f32[32,256,128]{2,1,0:T(8,128)S(1)}) custom-call(f32[8]{0:T(128)S(1)} %copy-done.6, f32[8]{0:T(128)S(1)} %copy-done.7, f32[4]{0:T(128)S(1)} %copy-done.8, f32[32,256,128]{2,1,0:T(8,128)S(1)} %bitcast.10), custom_call_target="tpu_custom_call" | custom-call | tf_op jit(solution)/shard_map/pallas_call | solution.py:439
  12.6 0.0 collective-permute-done.1.odd_x
  12.7 0.8 %collective-permute-done.even_x = f32[144,128]{1,0:T(8,128)S(1)} collective-permute-done((f32[144,128]{1,0:T(8,128)S(1)}, f32[144,128]{1,0:T(8,128)S(1)}, u32[]{:S(2)}, u32[]{:S(2)}) %collective-permute-start) | collective-permute-done | bytes 73760 | tf_op jit(solution)/shard_map/ppermute | solution.py:30
  13.5 1.9 %collective-permute-start.3 = (f32[288,128]{1,0:T(8,128)S(1)}, f32[288,128]{1,0:T(8,128)S(1)}, u32[]{:S(2)}, u32[]{:S(2)}) collective-permute-start(f32[288,128]{1,0:T(8,128)S(1)} %get-tuple-element.37), channel_id=1, source_target_pairs={{1,2},{2,1},{3,4},{4,3},{5,6},{6,5},{7,8},{8,7},{9,10},{10,9},{11,... | collective-permute-start | bytes 442376 | tf_op jit(solution)/shard_map/ppermute | solution.py:30
  15.4 0.9 %collective-permute-start.2 = (f32[288,128]{1,0:T(8,128)S(1)}, f32[288,128]{1,0:T(8,128)S(1)}, u32[]{:S(2)}, u32[]{:S(2)}) collective-permute-start(f32[288,128]{1,0:T(8,128)S(1)} %get-tuple-element.34.after), channel_id=1, source_target_pairs={{0,1},{1,0},{2,3},{3,2},{4,5},{5,4},{6,7},{7,6},{8,9},{9,8},{10,11... | collective-permute-start | bytes 442376 | tf_op jit(solution)/shard_map/ppermute | solution.py:30
  16.3 0.0 copy-done.9
  16.3 0.0 copy-done.10
  16.3 0.0 copy-done.11
  16.3 0.0 copy-done.1
  16.3 0.0 copy-done.2
  16.3 0.0 copy-done.3
  16.3 4.2 %shard_map.178 = (f32[32,256,128]{2,1,0:T(8,128)S(1)}, bf16[512,4096]{1,0:T(8,128)(2,1)S(1)}, bf16[256,1024]{1,0:T(8,128)(2,1)S(1)}, bf16[2,1024,128]{2,1,0:T(8,...) custom-call(f32[8]{0:T(128)S(1)} %copy-done.6, ...), custom_call_target="tpu_custom_call", output_to_operand_aliasing={{0}: (3, {})} | custom-call | tf_op jit(solution)/shard_map/pallas_call | solution.py:459
  20.5 0.4 collective-permute-done.3.odd_y
  20.8 0.0 collective-permute-done.2.even_y
  20.8 3.3 %shard_map.179 = (f32[32,256,128]{2,1,0:T(8,128)S(1)}, bf16[512,4096]{1,0:T(8,128)(2,1)S(1)}, f32[256,128]{1,0:T(8,128)S(1)}, bf16[512,128]{1,0:T(8,128)(2,1)S(1)}, f32[512,128]{1,0:T(8,128)S(1)}) custom-call(f32[32,256,128]{2,1,0:T(8,128)S(1)} %get-tuple-element.35.old, ...), custom_call_target="tpu_custom_call", output_to_operand_aliasing={{0}: (0, {}), {1}: (1, {})} | custom-call | tf_op jit(solution)/shard_map/pallas_call | solution.py:487
  24.2 0.0 copy-start.4
  24.2 0.0 copy-start.5
  24.2 3.6 %collective-permute-start.5 = (f32[512,128]{1,0:T(8,128)S(1)}, f32[512,128]{1,0:T(8,128)S(1)}, u32[]{:S(2)}, u32[]{:S(2)}) collective-permute-start(f32[512,128]{1,0:T(8,128)S(1)} %get-tuple-element.51), channel_id=1, source_target_pairs={{1,0},{2,1},{3,2},{4,3},{5,4},{6,5},{7,6},{8,7},{9,8},{10,9},{11,1... | collective-permute-start | bytes 786440 | tf_op jit(solution)/shard_map/ppermute | solution.py:34
  27.8 4.4 %shard_map.180 = (f32[512,128]{1,0:T(8,128)S(1)}, f32[512,128]{1,0:T(8,128)S(1)}) custom-call(f32[144,128]{1,0:T(8,128)S(1)} %collective-permute-done.even_x, f32[144,128]{1,0:T(8,128)S(1)} %collective-permute-done.1.odd_x, f32[288,128]{1,0:T(8,128)S(1)} %collective-permute-done.2.even_y, f32[288,128]{1,0:T(8,128)S(1)} %collective-permute-done.3.odd_y, ...), custom_call_target="tpu_custom_call" | custom-call | tf_op jit(solution)/shard_map/pallas_call | solution.py:502
  32.2 2.4 %collective-permute-start.4 = (f32[512,128]{1,0:T(8,128)S(1)}, f32[512,128]{1,0:T(8,128)S(1)}, u32[]{:S(2)}, u32[]{:S(2)}) collective-permute-start(f32[512,128]{1,0:T(8,128)S(1)} %get-tuple-element.47.after), channel_id=1, source_target_pairs={{1,0},{2,1},{3,2},{4,3},{5,4},{6,5},{7,6},{8,7},{9,8},{10,9},{11,1... | collective-permute-start | bytes 786440 | tf_op jit(solution)/shard_map/ppermute | solution.py:34
  34.6 0.0 collective-permute-done.5
  34.7 4.6 %collective-permute-start.6 = (f32[512,128]{1,0:T(8,128)S(1)}, f32[512,128]{1,0:T(8,128)S(1)}, u32[]{:S(2)}, u32[]{:S(2)}) collective-permute-start(f32[512,128]{1,0:T(8,128)S(1)} %add.21), channel_id=1, source_target_pairs={{16,0},{32,16},{48,32},{64,48},{80,64},{96,80},{112,96},{17,1},{33... | collective-permute-start | bytes 786440 | tf_op jit(solution)/shard_map/ppermute | solution.py:34
  39.3 0.0 copy-done.4
  39.3 0.0 copy-done.5
  39.3 4.9 %shard_map.181 = (f32[32,256,128]{2,1,0:T(8,128)}, f32[256,128]{1,0:T(8,128)}, f32[512,128]{1,0:T(8,128)S(1)}) custom-call(f32[144,128]{1,0:T(8,128)S(1)} %get-tuple-element.28.own_even.own_x, f32[32,256,128]{2,1,0:T(8,128)S(1)} %get-tuple-element.43.new, f32[256,128]{1,0:T(8,128)S(1)} %get-tuple-element.44.side_fix, ...), custom_call_target="tpu_custom_call" | custom-call | tf_op jit(solution)/shard_map/pallas_call | solution.py:512
  44.2 0.0 collective-permute-done.4
  44.2 3.1 %collective-permute-done.6 = f32[512,128]{1,0:T(8,128)S(1)} collective-permute-done((f32[512,128]{1,0:T(8,128)S(1)}, f32[512,128]{1,0:T(8,128)S(1)}, u32[]{:S(2)}, u32[]{:S(2)}) %collective-permute-start.6) | collective-permute-done | bytes 262176 | tf_op jit(solution)/shard_map/ppermute | solution.py:34
  47.3 0.8 %multiply_add_fusion = f32[512,128]{1,0:T(8,128)} fusion(f32[512,128]{1,0:T(8,128)S(1)} %get-tuple-element.49, f32[512,128]{1,0:T(8,128)S(1)} %collective-permute-done.4, f32[512,128]{1,0:T(8,128)S(1)} %collective-permute-done.6), kind=kLoop, calls=%fused_computation | loop fusion | flops 196608 | bytes 1048576 | tf_op jit(solution)/shard_map/add | solution.py:525
  (3 shorter events, 0.1 us)
Async XLA Ops:
  0.6 7.0 %copy-start = (f32[4,8,256,128]{3,2,1,0:T(8,128)S(1)}, f32[4,8,256,128]{3,2,1,0:T(8,128)}, u32[]{:S(2)}) copy-start(f32[4,8,256,128]{3,2,1,0:T(8,128)} %param.16) | copy-start | bytes 12582916
  0.6 7.0 %copy-start.8 = (f32[4]{0:T(128)S(1)}, f32[4]{0:T(128)}, u32[]{:S(2)}) copy-start(f32[4]{0:T(128)} %diffusion.3) | copy-start | bytes 52
  0.7 7.0 %copy-start.7 = (f32[8]{0:T(128)S(1)}, f32[8]{0:T(128)}, u32[]{:S(2)}) copy-start(f32[8]{0:T(128)} %courant_y.3) | copy-start | bytes 100
  0.7 7.0 %copy-start.6 = (f32[8]{0:T(128)S(1)}, f32[8]{0:T(128)}, u32[]{:S(2)}) copy-start(f32[8]{0:T(128)} %courant_x.3) | copy-start | bytes 100
  0.7 15.6 %copy-start.9 = (s32[256,1,4]{0,2,1:T(4,128)S(1)}, s32[256,1,4]{0,2,1:T(4,128)}, u32[]{:S(2)}) copy-start(s32[256,1,4]{0,2,1:T(4,128)} %param.29) | copy-start | bytes 12292
  0.7 15.6 %copy-start.10 = (s32[256,1,4]{0,2,1:T(4,128)S(1)}, s32[256,1,4]{0,2,1:T(4,128)}, u32[]{:S(2)}) copy-start(s32[256,1,4]{0,2,1:T(4,128)} %param.28) | copy-start | bytes 12292
  0.7 15.6 %copy-start.11 = (s32[256,1,4]{0,2,1:T(4,128)S(1)}, s32[256,1,4]{0,2,1:T(4,128)}, u32[]{:S(2)}) copy-start(s32[256,1,4]{0,2,1:T(4,128)} %param.30) | copy-start | bytes 12292
  0.7 15.6 %copy-start.1 = (s32[8,256,128]{2,1,0:T(8,128)S(1)}, s32[8,256,128]{2,1,0:T(8,128)}, u32[]{:S(2)}) copy-start(s32[8,256,128]{2,1,0:T(8,128)} %walls.3) | copy-start | bytes 3145732
  0.7 15.6 %copy-start.2 = (f32[8,128,128]{2,1,0:T(8,128)S(1)}, f32[8,128,128]{2,1,0:T(8,128)}, u32[]{:S(2)}) copy-start(f32[8,128,128]{2,1,0:T(8,128)} %fine.1) | copy-start | bytes 1572868
  0.7 15.6 %copy-start.3 = (f32[8,128,128]{2,1,0:T(8,128)S(1)}, f32[8,128,128]{2,1,0:T(8,128)}, u32[]{:S(2)}) copy-start(f32[8,128,128]{2,1,0:T(8,128)} %coarse.1) | copy-start | bytes 1572868
  2.0 10.6 %collective-permute-start.1 = (f32[144,128]{1,0:T(8,128)S(1)}, f32[144,128]{1,0:T(8,128)S(1)}, u32[]{:S(2)}, u32[]{:S(2)}) collective-permute-start(f32[144,128]{1,0:T(8,128)S(1)} %get-tuple-element.31), channel_id=1, source_target_pairs={{16,32},{32,16},{48,64},{64,48},{80,96},{96,80},{17,33},{33,17},{4... | collective-permute-start | bytes 221192 | tf_op jit(solution)/shard_map/ppermute | solution.py:30
  7.5 5.9 %collective-permute-start = (f32[144,128]{1,0:T(8,128)S(1)}, f32[144,128]{1,0:T(8,128)S(1)}, u32[]{:S(2)}, u32[]{:S(2)}) collective-permute-start(f32[144,128]{1,0:T(8,128)S(1)} %get-tuple-element.28.own_even.own_x), channel_id=1, source_target_pairs={{0,16},{16,0},{32,48},{48,32},{64,80},{80,64},{96,112},{112,96},{1... | collective-permute-start | bytes 221192 | tf_op jit(solution)/shard_map/ppermute | solution.py:30
  13.5 7.4 %collective-permute-start.3 = (f32[288,128]{1,0:T(8,128)S(1)}, f32[288,128]{1,0:T(8,128)S(1)}, u32[]{:S(2)}, u32[]{:S(2)}) collective-permute-start(f32[288,128]{1,0:T(8,128)S(1)} %get-tuple-element.37), channel_id=1, source_target_pairs={{1,2},{2,1},{3,4},{4,3},{5,6},{6,5},{7,8},{8,7},{9,10},{10,9},{11,... | collective-permute-start | bytes 442376 | tf_op jit(solution)/shard_map/ppermute | solution.py:30
  15.4 5.4 %collective-permute-start.2 = (f32[288,128]{1,0:T(8,128)S(1)}, f32[288,128]{1,0:T(8,128)S(1)}, u32[]{:S(2)}, u32[]{:S(2)}) collective-permute-start(f32[288,128]{1,0:T(8,128)S(1)} %get-tuple-element.34.after), channel_id=1, source_target_pairs={{0,1},{1,0},{2,3},{3,2},{4,5},{5,4},{6,7},{7,6},{8,9},{9,8},{10,11... | collective-permute-start | bytes 442376 | tf_op jit(solution)/shard_map/ppermute | solution.py:30
  24.2 15.1 %copy-start.4 = (f32[4,8,16,128]{3,2,1,0:T(8,128)S(1)}, f32[4,8,16,128]{3,2,1,0:T(8,128)}, u32[]{:S(2)}) copy-start(f32[4,8,16,128]{3,2,1,0:T(8,128)} %param.17) | copy-start | bytes 786436
  24.2 15.1 %copy-start.5 = (f32[256,128]{1,0:T(8,128)S(1)}, f32[256,128]{1,0:T(8,128)}, u32[]{:S(2)}) copy-start(f32[256,128]{1,0:T(8,128)} %radiant.1) | copy-start | bytes 393220
  24.2 10.5 %collective-permute-start.5 = (f32[512,128]{1,0:T(8,128)S(1)}, f32[512,128]{1,0:T(8,128)S(1)}, u32[]{:S(2)}, u32[]{:S(2)}) collective-permute-start(f32[512,128]{1,0:T(8,128)S(1)} %get-tuple-element.51), channel_id=1, source_target_pairs={{1,0},{2,1},{3,2},{4,3},{5,4},{6,5},{7,6},{8,7},{9,8},{10,9},{11,1... | collective-permute-start | bytes 786440 | tf_op jit(solution)/shard_map/ppermute | solution.py:34
  32.2 11.9 %collective-permute-start.4 = (f32[512,128]{1,0:T(8,128)S(1)}, f32[512,128]{1,0:T(8,128)S(1)}, u32[]{:S(2)}, u32[]{:S(2)}) collective-permute-start(f32[512,128]{1,0:T(8,128)S(1)} %get-tuple-element.47.after), channel_id=1, source_target_pairs={{1,0},{2,1},{3,2},{4,3},{5,4},{6,5},{7,6},{8,7},{9,8},{10,9},{11,1... | collective-permute-start | bytes 786440 | tf_op jit(solution)/shard_map/ppermute | solution.py:34
  34.7 12.6 %collective-permute-start.6 = (f32[512,128]{1,0:T(8,128)S(1)}, f32[512,128]{1,0:T(8,128)S(1)}, u32[]{:S(2)}, u32[]{:S(2)}) collective-permute-start(f32[512,128]{1,0:T(8,128)S(1)} %add.21), channel_id=1, source_target_pairs={{16,0},{32,16},{48,32},{64,48},{80,64},{96,80},{112,96},{17,1},{33... | collective-permute-start | bytes 786440 | tf_op jit(solution)/shard_map/ppermute | solution.py:34

commit v6 on v5

--- a/solution.py
+++ b/solution.py
@@ -209,7 +209,7 @@
                     ]
         return carry
 
-    lax.fori_loop(0, VZ // 2, one_pair, 0, unroll=4)
+    lax.fori_loop(0, VZ // 2, one_pair, 0, unroll=True)
 
 
 def ghost_part(blocks, coarse_banks, counts, table):

time: 48.3 us -> 46.6 us (0.965)
  Pallas kernels: 23.1 us -> 20.6 us
  waiting for transfers between devices: 4.24 us -> 5.06 us
    pallas_call x1, Pallas kernels: 3.31 us -> 2.46 us  [local(): pl.pallas_call(update_kernel, out_shape=(shape(VZ, CX, BLK), fields_shape...]
    pallas_call x1, Pallas kernels: 4.45 us -> 3.61 us  [local(): pl.pallas_call(sides_kernel, out_shape=(shape(VZ * PB, BLK),) * 2, in_spe...]
    ppermute x3, waiting for transfers between devices: 3.09 us -> 3.9 us  [one_lower(): lax.ppermute(value, axis, [(a, a - 1) for a in range(1, lax.axis_size(axi...]
    pallas_call x1, Pallas kernels: 4.88 us -> 4.07 us  [local(): pl.pallas_call(own_kernel, out_shape=(shape(VZ, CX, BLK), shape(CX, BLK),...]
  transfers between devices with their start and end apart: 7 -> 7, of which waited for: 3 -> 3; matrix products, arithmetic and copies ran while one was open for 0% -> 0% of each run, Pallas kernels for 38% -> 36%
where the time goes in v6:
time: 46.6 us; the launch traced here: 46.4 us
  Pallas kernels  20.6 us (44%)
  starting transfers between devices  18.9 us (41%)
  waiting for transfers between devices  5.06 us (11%)
  between operations  0.93 us (2%)
  other arithmetic  0.81 us (2%)
    ppermute x3, starting transfers between devices, one_lower(): lax.ppermute(value, axis, [(a, a - 1) for a in range(1, lax.axis_size(axi...  10.6 us
    ppermute x4, starting transfers between devices, exchange(): return lax.ppermute(value, axis, pairs)  8.37 us
    pallas_call x1, Pallas kernels, local(): pl.pallas_call(edges_kernel, out_shape=(shape(VZ, CX + 2 * PAD, BLK), sha...  4.99 us
    pallas_call x1, Pallas kernels, local(): pl.pallas_call(middle_kernel, out_shape=(shape(VZ, CX, BLK), fields_shape...  4.16 us
    pallas_call x1, Pallas kernels, local(): pl.pallas_call(own_kernel, out_shape=(shape(VZ, CX, BLK), shape(CX, BLK),...  4.07 us
    ppermute x3, waiting for transfers between devices, one_lower(): lax.ppermute(value, axis, [(a, a - 1) for a in range(1, lax.axis_size(axi...  3.9 us
    pallas_call x1, Pallas kernels, local(): pl.pallas_call(sides_kernel, out_shape=(shape(VZ * PB, BLK),) * 2, in_spe...  3.61 us
    pallas_call x1, Pallas kernels, local(): pl.pallas_call(update_kernel, out_shape=(shape(VZ, CX, BLK), fields_shape...  2.46 us
  transfers between devices with their start and end apart: 7, of which 3 were waited for; matrix products, arithmetic and copies ran while one was open for 0% of the time, Pallas kernels for 36%

profile of v6, /device:TPU:70, one launch (start us, length us, event | category | flops | bytes accessed | tf_op | source)
XLA Modules:
  0.0 46.4 jit_solution(18265698254560500781)
XLA Ops:
  0.6 0.0 copy-start
  0.6 0.0 copy-start.8
  0.7 0.0 copy-start.7
  0.7 0.0 copy-start.6
  0.7 0.0 copy-start.9
  0.7 0.0 copy-start.10
  0.7 0.0 copy-start.11
  0.7 0.0 copy-start.1
  0.7 0.0 copy-start.2
  0.7 0.0 copy-start.3
  0.7 1.3 %shard_map.175 = (f32[144,128]{1,0:T(8,128)S(1)}, f32[144,128]{1,0:T(8,128)S(1)}) custom-call(f32[32,256,128]{2,1,0:T(8,128)} %bitcast.9, f32[64,128]{1,0:T(8,128)} %bitcast.13, s32[16,16]{1,0:T(8,128)} %tile.1, s32[16,16]{1,0:T(8,128)} %row.1, s32[16,16]{1,0:T(8,128)} %op.1), custom_call_target="tpu_custom_call" | custom-call | tf_op jit(solution)/shard_map/pallas_call | solution.py:425
  2.0 5.5 %collective-permute-start.1 = (f32[144,128]{1,0:T(8,128)S(1)}, f32[144,128]{1,0:T(8,128)S(1)}, u32[]{:S(2)}, u32[]{:S(2)}) collective-permute-start(f32[144,128]{1,0:T(8,128)S(1)} %get-tuple-element.31), channel_id=1, source_target_pairs={{16,32},{32,16},{48,64},{64,48},{80,96},{96,80},{17,33},{33,17},{4... | collective-permute-start | bytes 221192 | tf_op jit(solution)/shard_map/ppermute | solution.py:30
  7.5 0.1 collective-permute-start
  7.6 0.0 copy-done
  7.6 0.0 copy-done.8
  7.6 0.0 copy-done.7
  7.6 0.0 copy-done.6
  7.6 5.0 %shard_map.176 = (f32[32,272,128]{2,1,0:T(8,128)S(1)}, f32[128,128]{1,0:T(8,128)S(1)}, f32[128,128]{1,0:T(8,128)S(1)}, f32[32,256,128]{2,1,0:T(8,128)S(1)}) custom-call(f32[8]{0:T(128)S(1)} %copy-done.6, f32[8]{0:T(128)S(1)} %copy-done.7, f32[4]{0:T(128)S(1)} %copy-done.8, f32[32,256,128]{2,1,0:T(8,128)S(1)} %bitcast.10), custom_call_target="tpu_custom_call" | custom-call | tf_op jit(solution)/shard_map/pallas_call | solution.py:439
  12.6 0.0 collective-permute-done.1.odd_x
  12.7 0.8 %collective-permute-done.even_x = f32[144,128]{1,0:T(8,128)S(1)} collective-permute-done((f32[144,128]{1,0:T(8,128)S(1)}, f32[144,128]{1,0:T(8,128)S(1)}, u32[]{:S(2)}, u32[]{:S(2)}) %collective-permute-start) | collective-permute-done | bytes 73760 | tf_op jit(solution)/shard_map/ppermute | solution.py:30
  13.5 1.9 %collective-permute-start.3 = (f32[288,128]{1,0:T(8,128)S(1)}, f32[288,128]{1,0:T(8,128)S(1)}, u32[]{:S(2)}, u32[]{:S(2)}) collective-permute-start(f32[288,128]{1,0:T(8,128)S(1)} %get-tuple-element.37), channel_id=1, source_target_pairs={{1,2},{2,1},{3,4},{4,3},{5,6},{6,5},{7,8},{8,7},{9,10},{10,9},{11,... | collective-permute-start | bytes 442376 | tf_op jit(solution)/shard_map/ppermute | solution.py:30
  15.4 0.9 %collective-permute-start.2 = (f32[288,128]{1,0:T(8,128)S(1)}, f32[288,128]{1,0:T(8,128)S(1)}, u32[]{:S(2)}, u32[]{:S(2)}) collective-permute-start(f32[288,128]{1,0:T(8,128)S(1)} %get-tuple-element.34.after), channel_id=1, source_target_pairs={{0,1},{1,0},{2,3},{3,2},{4,5},{5,4},{6,7},{7,6},{8,9},{9,8},{10,11... | collective-permute-start | bytes 442376 | tf_op jit(solution)/shard_map/ppermute | solution.py:30
  16.3 0.0 copy-done.9
  16.3 0.0 copy-done.10
  16.3 0.0 copy-done.11
  16.3 0.0 copy-done.1
  16.3 0.0 copy-done.2
  16.3 0.0 copy-done.3
  16.3 4.2 %shard_map.178 = (f32[32,256,128]{2,1,0:T(8,128)S(1)}, bf16[512,4096]{1,0:T(8,128)(2,1)S(1)}, bf16[256,1024]{1,0:T(8,128)(2,1)S(1)}, bf16[2,1024,128]{2,1,0:T(8,...) custom-call(f32[8]{0:T(128)S(1)} %copy-done.6, ...), custom_call_target="tpu_custom_call", output_to_operand_aliasing={{0}: (3, {})} | custom-call | tf_op jit(solution)/shard_map/pallas_call | solution.py:459
  20.5 0.4 collective-permute-done.3.odd_y
  20.8 0.0 collective-permute-done.2.even_y
  20.8 2.5 %shard_map.179 = (f32[32,256,128]{2,1,0:T(8,128)S(1)}, bf16[512,4096]{1,0:T(8,128)(2,1)S(1)}, f32[256,128]{1,0:T(8,128)S(1)}, bf16[512,128]{1,0:T(8,128)(2,1)S(1)}, f32[512,128]{1,0:T(8,128)S(1)}) custom-call(f32[32,256,128]{2,1,0:T(8,128)S(1)} %get-tuple-element.35.old, ...), custom_call_target="tpu_custom_call", output_to_operand_aliasing={{0}: (0, {}), {1}: (1, {})} | custom-call | tf_op jit(solution)/shard_map/pallas_call | solution.py:487
  23.3 0.0 copy-start.4
  23.3 0.0 copy-start.5
  23.3 3.6 %collective-permute-start.5 = (f32[512,128]{1,0:T(8,128)S(1)}, f32[512,128]{1,0:T(8,128)S(1)}, u32[]{:S(2)}, u32[]{:S(2)}) collective-permute-start(f32[512,128]{1,0:T(8,128)S(1)} %get-tuple-element.51), channel_id=1, source_target_pairs={{1,0},{2,1},{3,2},{4,3},{5,4},{6,5},{7,6},{8,7},{9,8},{10,9},{11,1... | collective-permute-start | bytes 786440 | tf_op jit(solution)/shard_map/ppermute | solution.py:34
  26.9 3.6 %shard_map.180 = (f32[512,128]{1,0:T(8,128)S(1)}, f32[512,128]{1,0:T(8,128)S(1)}) custom-call(f32[144,128]{1,0:T(8,128)S(1)} %collective-permute-done.even_x, f32[144,128]{1,0:T(8,128)S(1)} %collective-permute-done.1.odd_x, f32[288,128]{1,0:T(8,128)S(1)} %collective-permute-done.2.even_y, f32[288,128]{1,0:T(8,128)S(1)} %collective-permute-done.3.odd_y, ...), custom_call_target="tpu_custom_call" | custom-call | tf_op jit(solution)/shard_map/pallas_call | solution.py:502
  30.6 2.4 %collective-permute-start.4 = (f32[512,128]{1,0:T(8,128)S(1)}, f32[512,128]{1,0:T(8,128)S(1)}, u32[]{:S(2)}, u32[]{:S(2)}) collective-permute-start(f32[512,128]{1,0:T(8,128)S(1)} %get-tuple-element.47.after), channel_id=1, source_target_pairs={{1,0},{2,1},{3,2},{4,3},{5,4},{6,5},{7,6},{8,7},{9,8},{10,9},{11,1... | collective-permute-start | bytes 786440 | tf_op jit(solution)/shard_map/ppermute | solution.py:34
  33.0 0.0 collective-permute-done.5
  33.0 4.6 %collective-permute-start.6 = (f32[512,128]{1,0:T(8,128)S(1)}, f32[512,128]{1,0:T(8,128)S(1)}, u32[]{:S(2)}, u32[]{:S(2)}) collective-permute-start(f32[512,128]{1,0:T(8,128)S(1)} %add.21), channel_id=1, source_target_pairs={{16,0},{32,16},{48,32},{64,48},{80,64},{96,80},{112,96},{17,1},{33... | collective-permute-start | bytes 786440 | tf_op jit(solution)/shard_map/ppermute | solution.py:34
  37.6 0.0 copy-done.4
  37.6 0.0 copy-done.5
  37.6 4.1 %shard_map.181 = (f32[32,256,128]{2,1,0:T(8,128)}, f32[256,128]{1,0:T(8,128)}, f32[512,128]{1,0:T(8,128)S(1)}) custom-call(f32[144,128]{1,0:T(8,128)S(1)} %get-tuple-element.28.own_even.own_x, f32[32,256,128]{2,1,0:T(8,128)S(1)} %get-tuple-element.43.new, f32[256,128]{1,0:T(8,128)S(1)} %get-tuple-element.44.side_fix, ...), custom_call_target="tpu_custom_call" | custom-call | tf_op jit(solution)/shard_map/pallas_call | solution.py:512
  41.7 0.0 collective-permute-done.4
  41.7 3.9 %collective-permute-done.6 = f32[512,128]{1,0:T(8,128)S(1)} collective-permute-done((f32[512,128]{1,0:T(8,128)S(1)}, f32[512,128]{1,0:T(8,128)S(1)}, u32[]{:S(2)}, u32[]{:S(2)}) %collective-permute-start.6) | collective-permute-done | bytes 262176 | tf_op jit(solution)/shard_map/ppermute | solution.py:34
  45.6 0.8 %multiply_add_fusion = f32[512,128]{1,0:T(8,128)} fusion(f32[512,128]{1,0:T(8,128)S(1)} %get-tuple-element.49, f32[512,128]{1,0:T(8,128)S(1)} %collective-permute-done.4, f32[512,128]{1,0:T(8,128)S(1)} %collective-permute-done.6), kind=kLoop, calls=%fused_computation | loop fusion | flops 196608 | bytes 1048576 | tf_op jit(solution)/shard_map/add | solution.py:525
  (3 shorter events, 0.1 us)
Async XLA Ops:
  0.6 7.0 %copy-start = (f32[4,8,256,128]{3,2,1,0:T(8,128)S(1)}, f32[4,8,256,128]{3,2,1,0:T(8,128)}, u32[]{:S(2)}) copy-start(f32[4,8,256,128]{3,2,1,0:T(8,128)} %param.16) | copy-start | bytes 12582916
  0.6 7.0 %copy-start.8 = (f32[4]{0:T(128)S(1)}, f32[4]{0:T(128)}, u32[]{:S(2)}) copy-start(f32[4]{0:T(128)} %diffusion.3) | copy-start | bytes 52
  0.7 7.0 %copy-start.7 = (f32[8]{0:T(128)S(1)}, f32[8]{0:T(128)}, u32[]{:S(2)}) copy-start(f32[8]{0:T(128)} %courant_y.3) | copy-start | bytes 100
  0.7 7.0 %copy-start.6 = (f32[8]{0:T(128)S(1)}, f32[8]{0:T(128)}, u32[]{:S(2)}) copy-start(f32[8]{0:T(128)} %courant_x.3) | copy-start | bytes 100
  0.7 15.6 %copy-start.9 = (s32[256,1,4]{0,2,1:T(4,128)S(1)}, s32[256,1,4]{0,2,1:T(4,128)}, u32[]{:S(2)}) copy-start(s32[256,1,4]{0,2,1:T(4,128)} %param.29) | copy-start | bytes 12292
  0.7 15.6 %copy-start.10 = (s32[256,1,4]{0,2,1:T(4,128)S(1)}, s32[256,1,4]{0,2,1:T(4,128)}, u32[]{:S(2)}) copy-start(s32[256,1,4]{0,2,1:T(4,128)} %param.28) | copy-start | bytes 12292
  0.7 15.6 %copy-start.11 = (s32[256,1,4]{0,2,1:T(4,128)S(1)}, s32[256,1,4]{0,2,1:T(4,128)}, u32[]{:S(2)}) copy-start(s32[256,1,4]{0,2,1:T(4,128)} %param.30) | copy-start | bytes 12292
  0.7 15.6 %copy-start.1 = (s32[8,256,128]{2,1,0:T(8,128)S(1)}, s32[8,256,128]{2,1,0:T(8,128)}, u32[]{:S(2)}) copy-start(s32[8,256,128]{2,1,0:T(8,128)} %walls.3) | copy-start | bytes 3145732
  0.7 15.6 %copy-start.2 = (f32[8,128,128]{2,1,0:T(8,128)S(1)}, f32[8,128,128]{2,1,0:T(8,128)}, u32[]{:S(2)}) copy-start(f32[8,128,128]{2,1,0:T(8,128)} %fine.1) | copy-start | bytes 1572868
  0.7 15.6 %copy-start.3 = (f32[8,128,128]{2,1,0:T(8,128)S(1)}, f32[8,128,128]{2,1,0:T(8,128)}, u32[]{:S(2)}) copy-start(f32[8,128,128]{2,1,0:T(8,128)} %coarse.1) | copy-start | bytes 1572868
  2.0 10.6 %collective-permute-start.1 = (f32[144,128]{1,0:T(8,128)S(1)}, f32[144,128]{1,0:T(8,128)S(1)}, u32[]{:S(2)}, u32[]{:S(2)}) collective-permute-start(f32[144,128]{1,0:T(8,128)S(1)} %get-tuple-element.31), channel_id=1, source_target_pairs={{16,32},{32,16},{48,64},{64,48},{80,96},{96,80},{17,33},{33,17},{4... | collective-permute-start | bytes 221192 | tf_op jit(solution)/shard_map/ppermute | solution.py:30
  7.5 5.9 %collective-permute-start = (f32[144,128]{1,0:T(8,128)S(1)}, f32[144,128]{1,0:T(8,128)S(1)}, u32[]{:S(2)}, u32[]{:S(2)}) collective-permute-start(f32[144,128]{1,0:T(8,128)S(1)} %get-tuple-element.28.own_even.own_x), channel_id=1, source_target_pairs={{0,16},{16,0},{32,48},{48,32},{64,80},{80,64},{96,112},{112,96},{1... | collective-permute-start | bytes 221192 | tf_op jit(solution)/shard_map/ppermute | solution.py:30
  13.5 7.4 %collective-permute-start.3 = (f32[288,128]{1,0:T(8,128)S(1)}, f32[288,128]{1,0:T(8,128)S(1)}, u32[]{:S(2)}, u32[]{:S(2)}) collective-permute-start(f32[288,128]{1,0:T(8,128)S(1)} %get-tuple-element.37), channel_id=1, source_target_pairs={{1,2},{2,1},{3,4},{4,3},{5,6},{6,5},{7,8},{8,7},{9,10},{10,9},{11,... | collective-permute-start | bytes 442376 | tf_op jit(solution)/shard_map/ppermute | solution.py:30
  15.4 5.4 %collective-permute-start.2 = (f32[288,128]{1,0:T(8,128)S(1)}, f32[288,128]{1,0:T(8,128)S(1)}, u32[]{:S(2)}, u32[]{:S(2)}) collective-permute-start(f32[288,128]{1,0:T(8,128)S(1)} %get-tuple-element.34.after), channel_id=1, source_target_pairs={{0,1},{1,0},{2,3},{3,2},{4,5},{5,4},{6,7},{7,6},{8,9},{9,8},{10,11... | collective-permute-start | bytes 442376 | tf_op jit(solution)/shard_map/ppermute | solution.py:30
  23.3 14.3 %copy-start.4 = (f32[4,8,16,128]{3,2,1,0:T(8,128)S(1)}, f32[4,8,16,128]{3,2,1,0:T(8,128)}, u32[]{:S(2)}) copy-start(f32[4,8,16,128]{3,2,1,0:T(8,128)} %param.17) | copy-start | bytes 786436
  23.3 14.3 %copy-start.5 = (f32[256,128]{1,0:T(8,128)S(1)}, f32[256,128]{1,0:T(8,128)}, u32[]{:S(2)}) copy-start(f32[256,128]{1,0:T(8,128)} %radiant.1) | copy-start | bytes 393220
  23.3 9.6 %collective-permute-start.5 = (f32[512,128]{1,0:T(8,128)S(1)}, f32[512,128]{1,0:T(8,128)S(1)}, u32[]{:S(2)}, u32[]{:S(2)}) collective-permute-start(f32[512,128]{1,0:T(8,128)S(1)} %get-tuple-element.51), channel_id=1, source_target_pairs={{1,0},{2,1},{3,2},{4,3},{5,4},{6,5},{7,6},{8,7},{9,8},{10,9},{11,1... | collective-permute-start | bytes 786440 | tf_op jit(solution)/shard_map/ppermute | solution.py:34
  30.6 11.1 %collective-permute-start.4 = (f32[512,128]{1,0:T(8,128)S(1)}, f32[512,128]{1,0:T(8,128)S(1)}, u32[]{:S(2)}, u32[]{:S(2)}) collective-permute-start(f32[512,128]{1,0:T(8,128)S(1)} %get-tuple-element.47.after), channel_id=1, source_target_pairs={{1,0},{2,1},{3,2},{4,3},{5,4},{6,5},{7,6},{8,7},{9,8},{10,9},{11,1... | collective-permute-start | bytes 786440 | tf_op jit(solution)/shard_map/ppermute | solution.py:34
  33.0 12.6 %collective-permute-start.6 = (f32[512,128]{1,0:T(8,128)S(1)}, f32[512,128]{1,0:T(8,128)S(1)}, u32[]{:S(2)}, u32[]{:S(2)}) collective-permute-start(f32[512,128]{1,0:T(8,128)S(1)} %add.21), channel_id=1, source_target_pairs={{16,0},{32,16},{48,32},{64,48},{80,64},{96,80},{112,96},{17,1},{33... | collective-permute-start | bytes 786440 | tf_op jit(solution)/shard_map/ppermute | solution.py:34

commit v7 on v6

--- a/solution.py
+++ b/solution.py
@@ -150,7 +150,7 @@
                 inner[vz, r - PAD : r - PAD + CHUNK] = total + d * beside
         return carry
 
-    lax.fori_loop(first, last, variable, 0)
+    lax.fori_loop(first, last, variable, 0, unroll=last - first)
 
 
 def per_level(values, level):
@@ -319,7 +319,7 @@
                 fields[CX + r : CX + r + CHUNK, columns] = low
         return carry
 
-    lax.fori_loop(0, V, variable, 0)
+    lax.fori_loop(0, V, variable, 0, unroll=2)
 
 
 def update_kernel(
@@ -399,7 +399,7 @@
         pltpu.make_async_copy(whole.at[pl.ds(NZ * v, NZ)], states.at[pl.ds(NZ * v, NZ)], sems.at[v]).start()
         return carry
 
-    lax.fori_loop(0, V, variable, 0)
+    lax.fori_loop(0, V, variable, 0, unroll=2)
     u, w, t, h = (whole[NZ * v] for v in range(V))
     speed = jnp.sqrt(u * u + w * w + 0.25)
     excess = radiant[...] - t

time: 46.6 us -> 46.5 us (level)
  no operation moved by 1% of the time
where the time goes in v7:
time: 46.5 us; the launch traced here: 46.3 us
  Pallas kernels  20.2 us (43%)
  starting transfers between devices  18.9 us (41%)
  waiting for transfers between devices  5.42 us (12%)
  between operations  0.93 us (2%)
  other arithmetic  0.81 us (2%)
    ppermute x3, starting transfers between devices, one_lower(): lax.ppermute(value, axis, [(a, a - 1) for a in range(1, lax.axis_size(axi...  10.5 us
    ppermute x4, starting transfers between devices, exchange(): return lax.ppermute(value, axis, pairs)  8.37 us
    pallas_call x1, Pallas kernels, local(): pl.pallas_call(edges_kernel, out_shape=(shape(VZ, CX + 2 * PAD, BLK), sha...  4.77 us
    pallas_call x1, Pallas kernels, local(): pl.pallas_call(middle_kernel, out_shape=(shape(VZ, CX, BLK), fields_shape...  4.15 us
    ppermute x3, waiting for transfers between devices, one_lower(): lax.ppermute(value, axis, [(a, a - 1) for a in range(1, lax.axis_size(axi...  4.04 us
    pallas_call x1, Pallas kernels, local(): pl.pallas_call(own_kernel, out_shape=(shape(VZ, CX, BLK), shape(CX, BLK),...  3.93 us
    pallas_call x1, Pallas kernels, local(): pl.pallas_call(sides_kernel, out_shape=(shape(VZ * PB, BLK),) * 2, in_spe...  3.61 us
    pallas_call x1, Pallas kernels, local(): pl.pallas_call(update_kernel, out_shape=(shape(VZ, CX, BLK), fields_shape...  2.46 us
  transfers between devices with their start and end apart: 7, of which 3 were waited for; matrix products, arithmetic and copies ran while one was open for 0% of the time, Pallas kernels for 36%

profile of v7, /device:TPU:70, one launch (start us, length us, event | category | flops | bytes accessed | tf_op | source)
XLA Modules:
  0.0 46.3 jit_solution(11445270357990838496)
XLA Ops:
  0.6 0.0 copy-start
  0.6 0.0 copy-start.8
  0.7 0.0 copy-start.7
  0.7 0.0 copy-start.6
  0.7 0.0 copy-start.9
  0.7 0.0 copy-start.10
  0.7 0.0 copy-start.11
  0.7 0.0 copy-start.1
  0.7 0.0 copy-start.2
  0.7 0.0 copy-start.3
  0.7 1.3 %shard_map.175 = (f32[144,128]{1,0:T(8,128)S(1)}, f32[144,128]{1,0:T(8,128)S(1)}) custom-call(f32[32,256,128]{2,1,0:T(8,128)} %bitcast.9, f32[64,128]{1,0:T(8,128)} %bitcast.13, s32[16,16]{1,0:T(8,128)} %tile.1, s32[16,16]{1,0:T(8,128)} %row.1, s32[16,16]{1,0:T(8,128)} %op.1), custom_call_target="tpu_custom_call" | custom-call | tf_op jit(solution)/shard_map/pallas_call | solution.py:425
  2.0 5.5 %collective-permute-start.1 = (f32[144,128]{1,0:T(8,128)S(1)}, f32[144,128]{1,0:T(8,128)S(1)}, u32[]{:S(2)}, u32[]{:S(2)}) collective-permute-start(f32[144,128]{1,0:T(8,128)S(1)} %get-tuple-element.31), channel_id=1, source_target_pairs={{16,32},{32,16},{48,64},{64,48},{80,96},{96,80},{17,33},{33,17},{4... | collective-permute-start | bytes 221192 | tf_op jit(solution)/shard_map/ppermute | solution.py:30
  7.5 0.1 collective-permute-start
  7.6 0.0 copy-done
  7.6 0.0 copy-done.8
  7.6 0.0 copy-done.7
  7.6 0.0 copy-done.6
  7.6 4.8 %shard_map.176 = (f32[32,272,128]{2,1,0:T(8,128)S(1)}, f32[128,128]{1,0:T(8,128)S(1)}, f32[128,128]{1,0:T(8,128)S(1)}, f32[32,256,128]{2,1,0:T(8,128)S(1)}) custom-call(f32[8]{0:T(128)S(1)} %copy-done.6, f32[8]{0:T(128)S(1)} %copy-done.7, f32[4]{0:T(128)S(1)} %copy-done.8, f32[32,256,128]{2,1,0:T(8,128)S(1)} %bitcast.10), custom_call_target="tpu_custom_call" | custom-call | tf_op jit(solution)/shard_map/pallas_call | solution.py:439
  12.4 0.0 collective-permute-done.1.odd_x
  12.4 1.0 %collective-permute-done.even_x = f32[144,128]{1,0:T(8,128)S(1)} collective-permute-done((f32[144,128]{1,0:T(8,128)S(1)}, f32[144,128]{1,0:T(8,128)S(1)}, u32[]{:S(2)}, u32[]{:S(2)}) %collective-permute-start) | collective-permute-done | bytes 73760 | tf_op jit(solution)/shard_map/ppermute | solution.py:30
  13.5 1.9 %collective-permute-start.3 = (f32[288,128]{1,0:T(8,128)S(1)}, f32[288,128]{1,0:T(8,128)S(1)}, u32[]{:S(2)}, u32[]{:S(2)}) collective-permute-start(f32[288,128]{1,0:T(8,128)S(1)} %get-tuple-element.37), channel_id=1, source_target_pairs={{1,2},{2,1},{3,4},{4,3},{5,6},{6,5},{7,8},{8,7},{9,10},{10,9},{11,... | collective-permute-start | bytes 442376 | tf_op jit(solution)/shard_map/ppermute | solution.py:30
  15.4 0.9 %collective-permute-start.2 = (f32[288,128]{1,0:T(8,128)S(1)}, f32[288,128]{1,0:T(8,128)S(1)}, u32[]{:S(2)}, u32[]{:S(2)}) collective-permute-start(f32[288,128]{1,0:T(8,128)S(1)} %get-tuple-element.34.after), channel_id=1, source_target_pairs={{0,1},{1,0},{2,3},{3,2},{4,5},{5,4},{6,7},{7,6},{8,9},{9,8},{10,11... | collective-permute-start | bytes 442376 | tf_op jit(solution)/shard_map/ppermute | solution.py:30
  16.3 0.0 copy-done.9
  16.3 0.0 copy-done.10
  16.3 0.0 copy-done.11
  16.3 0.0 copy-done.1
  16.3 0.0 copy-done.2
  16.3 0.0 copy-done.3
  16.3 4.2 %shard_map.178 = (f32[32,256,128]{2,1,0:T(8,128)S(1)}, bf16[512,4096]{1,0:T(8,128)(2,1)S(1)}, bf16[256,1024]{1,0:T(8,128)(2,1)S(1)}, bf16[2,1024,128]{2,1,0:T(8,...) custom-call(f32[8]{0:T(128)S(1)} %copy-done.6, ...), custom_call_target="tpu_custom_call", output_to_operand_aliasing={{0}: (3, {})} | custom-call | tf_op jit(solution)/shard_map/pallas_call | solution.py:459
  20.5 0.4 collective-permute-done.3.odd_y
  20.8 0.0 collective-permute-done.2.even_y
  20.8 2.5 %shard_map.179 = (f32[32,256,128]{2,1,0:T(8,128)S(1)}, bf16[512,4096]{1,0:T(8,128)(2,1)S(1)}, f32[256,128]{1,0:T(8,128)S(1)}, bf16[512,128]{1,0:T(8,128)(2,1)S(1)}, f32[512,128]{1,0:T(8,128)S(1)}) custom-call(f32[32,256,128]{2,1,0:T(8,128)S(1)} %get-tuple-element.35.old, ...), custom_call_target="tpu_custom_call", output_to_operand_aliasing={{0}: (0, {}), {1}: (1, {})} | custom-call | tf_op jit(solution)/shard_map/pallas_call | solution.py:487
  23.3 0.0 copy-start.4
  23.3 0.0 copy-start.5
  23.3 3.8 %collective-permute-start.5 = (f32[512,128]{1,0:T(8,128)S(1)}, f32[512,128]{1,0:T(8,128)S(1)}, u32[]{:S(2)}, u32[]{:S(2)}) collective-permute-start(f32[512,128]{1,0:T(8,128)S(1)} %get-tuple-element.51), channel_id=1, source_target_pairs={{1,0},{2,1},{3,2},{4,3},{5,4},{6,5},{7,6},{8,7},{9,8},{10,9},{11,1... | collective-permute-start | bytes 786440 | tf_op jit(solution)/shard_map/ppermute | solution.py:34
  27.1 3.6 %shard_map.180 = (f32[512,128]{1,0:T(8,128)S(1)}, f32[512,128]{1,0:T(8,128)S(1)}) custom-call(f32[144,128]{1,0:T(8,128)S(1)} %collective-permute-done.even_x, f32[144,128]{1,0:T(8,128)S(1)} %collective-permute-done.1.odd_x, f32[288,128]{1,0:T(8,128)S(1)} %collective-permute-done.2.even_y, f32[288,128]{1,0:T(8,128)S(1)} %collective-permute-done.3.odd_y, ...), custom_call_target="tpu_custom_call" | custom-call | tf_op jit(solution)/shard_map/pallas_call | solution.py:502
  30.7 2.4 %collective-permute-start.4 = (f32[512,128]{1,0:T(8,128)S(1)}, f32[512,128]{1,0:T(8,128)S(1)}, u32[]{:S(2)}, u32[]{:S(2)}) collective-permute-start(f32[512,128]{1,0:T(8,128)S(1)} %get-tuple-element.47.after), channel_id=1, source_target_pairs={{1,0},{2,1},{3,2},{4,3},{5,4},{6,5},{7,6},{8,7},{9,8},{10,9},{11,1... | collective-permute-start | bytes 786440 | tf_op jit(solution)/shard_map/ppermute | solution.py:34
  33.1 0.0 collective-permute-done.5
  33.2 4.4 %collective-permute-start.6 = (f32[512,128]{1,0:T(8,128)S(1)}, f32[512,128]{1,0:T(8,128)S(1)}, u32[]{:S(2)}, u32[]{:S(2)}) collective-permute-start(f32[512,128]{1,0:T(8,128)S(1)} %add.21), channel_id=1, source_target_pairs={{16,0},{32,16},{48,32},{64,48},{80,64},{96,80},{112,96},{17,1},{33... | collective-permute-start | bytes 786440 | tf_op jit(solution)/shard_map/ppermute | solution.py:34
  37.5 0.0 copy-done.4
  37.6 0.0 copy-done.5
  37.6 3.9 %shard_map.181 = (f32[32,256,128]{2,1,0:T(8,128)}, f32[256,128]{1,0:T(8,128)}, f32[512,128]{1,0:T(8,128)S(1)}) custom-call(f32[144,128]{1,0:T(8,128)S(1)} %get-tuple-element.28.own_even.own_x, f32[32,256,128]{2,1,0:T(8,128)S(1)} %get-tuple-element.43.new, f32[256,128]{1,0:T(8,128)S(1)} %get-tuple-element.44.side_fix, ...), custom_call_target="tpu_custom_call" | custom-call | tf_op jit(solution)/shard_map/pallas_call | solution.py:512
  41.5 0.0 collective-permute-done.4
  41.5 4.0 %collective-permute-done.6 = f32[512,128]{1,0:T(8,128)S(1)} collective-permute-done((f32[512,128]{1,0:T(8,128)S(1)}, f32[512,128]{1,0:T(8,128)S(1)}, u32[]{:S(2)}, u32[]{:S(2)}) %collective-permute-start.6) | collective-permute-done | bytes 262176 | tf_op jit(solution)/shard_map/ppermute | solution.py:34
  45.5 0.8 %multiply_add_fusion = f32[512,128]{1,0:T(8,128)} fusion(f32[512,128]{1,0:T(8,128)S(1)} %get-tuple-element.49, f32[512,128]{1,0:T(8,128)S(1)} %collective-permute-done.4, f32[512,128]{1,0:T(8,128)S(1)} %collective-permute-done.6), kind=kLoop, calls=%fused_computation | loop fusion | flops 196608 | bytes 1048576 | tf_op jit(solution)/shard_map/add | solution.py:525
  (3 shorter events, 0.1 us)
Async XLA Ops:
  0.6 7.0 %copy-start = (f32[4,8,256,128]{3,2,1,0:T(8,128)S(1)}, f32[4,8,256,128]{3,2,1,0:T(8,128)}, u32[]{:S(2)}) copy-start(f32[4,8,256,128]{3,2,1,0:T(8,128)} %param.16) | copy-start | bytes 12582916
  0.6 7.0 %copy-start.8 = (f32[4]{0:T(128)S(1)}, f32[4]{0:T(128)}, u32[]{:S(2)}) copy-start(f32[4]{0:T(128)} %diffusion.3) | copy-start | bytes 52
  0.7 7.0 %copy-start.7 = (f32[8]{0:T(128)S(1)}, f32[8]{0:T(128)}, u32[]{:S(2)}) copy-start(f32[8]{0:T(128)} %courant_y.3) | copy-start | bytes 100
  0.7 7.0 %copy-start.6 = (f32[8]{0:T(128)S(1)}, f32[8]{0:T(128)}, u32[]{:S(2)}) copy-start(f32[8]{0:T(128)} %courant_x.3) | copy-start | bytes 100
  0.7 15.6 %copy-start.9 = (s32[256,1,4]{0,2,1:T(4,128)S(1)}, s32[256,1,4]{0,2,1:T(4,128)}, u32[]{:S(2)}) copy-start(s32[256,1,4]{0,2,1:T(4,128)} %param.29) | copy-start | bytes 12292
  0.7 15.6 %copy-start.10 = (s32[256,1,4]{0,2,1:T(4,128)S(1)}, s32[256,1,4]{0,2,1:T(4,128)}, u32[]{:S(2)}) copy-start(s32[256,1,4]{0,2,1:T(4,128)} %param.28) | copy-start | bytes 12292
  0.7 15.6 %copy-start.11 = (s32[256,1,4]{0,2,1:T(4,128)S(1)}, s32[256,1,4]{0,2,1:T(4,128)}, u32[]{:S(2)}) copy-start(s32[256,1,4]{0,2,1:T(4,128)} %param.30) | copy-start | bytes 12292
  0.7 15.6 %copy-start.1 = (s32[8,256,128]{2,1,0:T(8,128)S(1)}, s32[8,256,128]{2,1,0:T(8,128)}, u32[]{:S(2)}) copy-start(s32[8,256,128]{2,1,0:T(8,128)} %walls.3) | copy-start | bytes 3145732
  0.7 15.6 %copy-start.2 = (f32[8,128,128]{2,1,0:T(8,128)S(1)}, f32[8,128,128]{2,1,0:T(8,128)}, u32[]{:S(2)}) copy-start(f32[8,128,128]{2,1,0:T(8,128)} %fine.1) | copy-start | bytes 1572868
  0.7 15.6 %copy-start.3 = (f32[8,128,128]{2,1,0:T(8,128)S(1)}, f32[8,128,128]{2,1,0:T(8,128)}, u32[]{:S(2)}) copy-start(f32[8,128,128]{2,1,0:T(8,128)} %coarse.1) | copy-start | bytes 1572868
  2.0 10.4 %collective-permute-start.1 = (f32[144,128]{1,0:T(8,128)S(1)}, f32[144,128]{1,0:T(8,128)S(1)}, u32[]{:S(2)}, u32[]{:S(2)}) collective-permute-start(f32[144,128]{1,0:T(8,128)S(1)} %get-tuple-element.31), channel_id=1, source_target_pairs={{16,32},{32,16},{48,64},{64,48},{80,96},{96,80},{17,33},{33,17},{4... | collective-permute-start | bytes 221192 | tf_op jit(solution)/shard_map/ppermute | solution.py:30
  7.5 5.9 %collective-permute-start = (f32[144,128]{1,0:T(8,128)S(1)}, f32[144,128]{1,0:T(8,128)S(1)}, u32[]{:S(2)}, u32[]{:S(2)}) collective-permute-start(f32[144,128]{1,0:T(8,128)S(1)} %get-tuple-element.28.own_even.own_x), channel_id=1, source_target_pairs={{0,16},{16,0},{32,48},{48,32},{64,80},{80,64},{96,112},{112,96},{1... | collective-permute-start | bytes 221192 | tf_op jit(solution)/shard_map/ppermute | solution.py:30
  13.5 7.4 %collective-permute-start.3 = (f32[288,128]{1,0:T(8,128)S(1)}, f32[288,128]{1,0:T(8,128)S(1)}, u32[]{:S(2)}, u32[]{:S(2)}) collective-permute-start(f32[288,128]{1,0:T(8,128)S(1)} %get-tuple-element.37), channel_id=1, source_target_pairs={{1,2},{2,1},{3,4},{4,3},{5,6},{6,5},{7,8},{8,7},{9,10},{10,9},{11,... | collective-permute-start | bytes 442376 | tf_op jit(solution)/shard_map/ppermute | solution.py:30
  15.4 5.4 %collective-permute-start.2 = (f32[288,128]{1,0:T(8,128)S(1)}, f32[288,128]{1,0:T(8,128)S(1)}, u32[]{:S(2)}, u32[]{:S(2)}) collective-permute-start(f32[288,128]{1,0:T(8,128)S(1)} %get-tuple-element.34.after), channel_id=1, source_target_pairs={{0,1},{1,0},{2,3},{3,2},{4,5},{5,4},{6,7},{7,6},{8,9},{9,8},{10,11... | collective-permute-start | bytes 442376 | tf_op jit(solution)/shard_map/ppermute | solution.py:30
  23.3 14.2 %copy-start.4 = (f32[4,8,16,128]{3,2,1,0:T(8,128)S(1)}, f32[4,8,16,128]{3,2,1,0:T(8,128)}, u32[]{:S(2)}) copy-start(f32[4,8,16,128]{3,2,1,0:T(8,128)} %param.17) | copy-start | bytes 786436
  23.3 14.2 %copy-start.5 = (f32[256,128]{1,0:T(8,128)S(1)}, f32[256,128]{1,0:T(8,128)}, u32[]{:S(2)}) copy-start(f32[256,128]{1,0:T(8,128)} %radiant.1) | copy-start | bytes 393220
  23.3 9.8 %collective-permute-start.5 = (f32[512,128]{1,0:T(8,128)S(1)}, f32[512,128]{1,0:T(8,128)S(1)}, u32[]{:S(2)}, u32[]{:S(2)}) collective-permute-start(f32[512,128]{1,0:T(8,128)S(1)} %get-tuple-element.51), channel_id=1, source_target_pairs={{1,0},{2,1},{3,2},{4,3},{5,4},{6,5},{7,6},{8,7},{9,8},{10,9},{11,1... | collective-permute-start | bytes 786440 | tf_op jit(solution)/shard_map/ppermute | solution.py:34
  30.7 10.8 %collective-permute-start.4 = (f32[512,128]{1,0:T(8,128)S(1)}, f32[512,128]{1,0:T(8,128)S(1)}, u32[]{:S(2)}, u32[]{:S(2)}) collective-permute-start(f32[512,128]{1,0:T(8,128)S(1)} %get-tuple-element.47.after), channel_id=1, source_target_pairs={{1,0},{2,1},{3,2},{4,3},{5,4},{6,5},{7,6},{8,7},{9,8},{10,9},{11,1... | collective-permute-start | bytes 786440 | tf_op jit(solution)/shard_map/ppermute | solution.py:34
  33.2 12.4 %collective-permute-start.6 = (f32[512,128]{1,0:T(8,128)S(1)}, f32[512,128]{1,0:T(8,128)S(1)}, u32[]{:S(2)}, u32[]{:S(2)}) collective-permute-start(f32[512,128]{1,0:T(8,128)S(1)} %add.21), channel_id=1, source_target_pairs={{16,0},{32,16},{48,32},{64,48},{80,64},{96,80},{112,96},{17,1},{33... | collective-permute-start | bytes 786440 | tf_op jit(solution)/shard_map/ppermute | solution.py:34
